TPU v7x, 32 devices: a whole 2x2x4 slice. The times are simulated.
32 devices in a mesh: dp: 16 (over z, x, core), tensor: 2 (over y).
Axes of the slice: x: 2, y: 2, z: 4, core: 2. Of those that a mesh axis runs over, the one named last changes fastest.
Arguments:
- hidden_in: bfloat16 [32768, 768], P('dp'), may hold values from -6 to 6
- query_weight: bfloat16 [768, 768], P(None, 'tensor'), may hold values from -0.3125 to 0.3125
- key_weight: bfloat16 [768, 768], P(None, 'tensor'), may hold values from -0.3125 to 0.3125
- value_weight: bfloat16 [768, 768], P(None, 'tensor'), may hold values from -0.21875 to 0.21875
- query_bias: bfloat16 [768], P('tensor'), may hold values from -3 to 3
- value_bias: bfloat16 [768], P('tensor'), may hold values from -3 to 3
- mixer_weight: bfloat16 [768, 768], P('tensor'), may hold values from -1.25 to 1.25
- mixer_bias: bfloat16 [768], replicated, may hold values from -3 to 3
- first_gain: bfloat16 [768], replicated, may hold values from 0.5 to 1.5
- first_bias: bfloat16 [768], replicated, may hold values from -3 to 3
- inner_weight: bfloat16 [768, 3072], P(None, 'tensor'), may hold values from -0.21875 to 0.21875
- inner_bias: bfloat16 [3072], P('tensor'), may hold values from -3 to 3
- outer_weight: bfloat16 [3072, 768], P('tensor'), may hold values from -0.109375 to 0.109375
- outer_bias: bfloat16 [768], replicated, may hold values from -3 to 3
- second_gain: bfloat16 [768], replicated, may hold values from 0.5 to 1.5
- second_bias: bfloat16 [768], replicated, may hold values from -3 to 3
- lengths: int32 [64, 4], P('dp'), may hold values from 33 to 512, as said below
- cotangent: bfloat16 [32768, 768], P('dp'), may hold values from -6 to 6
Outputs:
- layer_out: bfloat16 [32768, 768], P('dp')
- input_grad: bfloat16 [32768, 768], P('dp')
- query_weight_grad: float32 [768, 768], P(None, 'tensor')
- key_weight_grad: float32 [768, 768], P(None, 'tensor')
- value_weight_grad: float32 [768, 768], P(None, 'tensor')
- query_bias_grad: float32 [768], P('tensor')
- value_bias_grad: float32 [768], P('tensor')
- mixer_weight_grad: float32 [768, 768], P('tensor')
- mixer_bias_grad: float32 [768], replicated
- first_gain_grad: float32 [768], replicated
- first_bias_grad: float32 [768], replicated
- inner_weight_grad: float32 [768, 3072], P(None, 'tensor')
- inner_bias_grad: float32 [3072], P('tensor')
- outer_weight_grad: float32 [3072, 768], P('tensor')
- outer_bias_grad: float32 [768], replicated
- second_gain_grad: float32 [768], replicated
- second_bias_grad: float32 [768], replicated
Inputs may be any that keep to these rules, and one draw needn't show every extreme that they name: lengths[b, j] counts the live tokens of the j-th sequence of block b, whose sequences have 512 / 2**((b % 4) % 3) positions each; no entry exceeds its sequence's positions; entries with j at or past the block's number of sequences are not read; some sequence is full.
All inputs are finite; a program needn't handle non-finite values.
Results may differ from a plain program's by a relative error of at most 0.014.
The roundings to bfloat16 on the way count: a program that leaves them out, or rounds other values in their place, can miss the bound.
Values sent between devices are 32-bit elements; how exact they have to be, the bound alone decides.
No kernel may reach another device: no remote copies, remote signals or barrier semaphores. Data moves between devices by JAX's collectives and lax.ppermute only.
A program may use at most 256 MiB of HBM per device.

v0:
```python
from functools import partial
import math

import jax
import jax.numpy as jnp
from jax import lax
from jax.sharding import PartitionSpec as P

HD = 64
MAXLEN = 512


EPSILON = 1e-06


def block_masks(lengths_block, block_kind, block_rows):
    seq_span = block_rows >> block_kind
    position = jnp.arange(block_rows, dtype=jnp.int32)
    segment = position // seq_span
    offset = position - segment * seq_span
    slot_index = jnp.arange(lengths_block.shape[0], dtype=jnp.int32)
    picked = jnp.sum(
        jnp.where(segment[:, None] == slot_index[None, :], lengths_block[None, :], 0), axis=1
    )
    live_rows = offset < picked
    allowed = (segment[:, None] == segment[None, :]) & live_rows[None, :]
    return (allowed, live_rows)


def normalize(values, norm_gain, norm_bias):
    center = values - jnp.mean(values, axis=-1, keepdims=True)
    inverse = lax.rsqrt(jnp.mean(center * center, axis=-1, keepdims=True) + EPSILON)
    return center * inverse * norm_gain + norm_bias


def norm_backward(values, norm_gain, upstream):
    center = values - jnp.mean(values, axis=-1, keepdims=True)
    inverse = lax.rsqrt(jnp.mean(center * center, axis=-1, keepdims=True) + EPSILON)
    normed = center * inverse
    gain_grad = jnp.sum(upstream * normed, axis=0)
    bias_grad = jnp.sum(upstream, axis=0)
    scaled = upstream * norm_gain
    grad_in = inverse * (
        scaled
        - jnp.mean(scaled, axis=-1, keepdims=True)
        - normed * jnp.mean(scaled * normed, axis=-1, keepdims=True)
    )
    return (grad_in, gain_grad, bias_grad)


def split_heads(matrix):
    return matrix.reshape(matrix.shape[0], -1, HD)


def block_scores(query_block, key_block, allowed, scale):
    scores = (
        jnp.einsum("qhd,khd->hqk", query_block, key_block, preferred_element_type=jnp.float32)
        * scale
    )
    return jnp.where(allowed[None, :, :], scores, -1e30)


def local(
    hidden_in,
    query_weight,
    key_weight,
    value_weight,
    query_bias,
    value_bias,
    mixer_weight,
    mixer_bias,
    first_gain,
    first_bias,
    inner_weight,
    inner_bias,
    outer_weight,
    outer_bias,
    second_gain,
    second_bias,
    lengths,
    cotangent,
):
    block_count = lengths.shape[0]
    scale = 1.0 / math.sqrt(HD)
    tokens = hidden_in.astype(jnp.float32)
    query = (
        jnp.dot(hidden_in, query_weight, preferred_element_type=jnp.float32)
        + query_bias.astype(jnp.float32)
    ).astype(jnp.bfloat16)
    keys = jnp.dot(hidden_in, key_weight, preferred_element_type=jnp.float32).astype(jnp.bfloat16)
    values = (
        jnp.dot(hidden_in, value_weight, preferred_element_type=jnp.float32)
        + value_bias.astype(jnp.float32)
    ).astype(jnp.bfloat16)
    masks = [
        block_masks(lengths[block_id], block_id % 3, MAXLEN) for block_id in range(block_count)
    ]
    contexts = []
    log_totals = []
    for block_id in range(block_count):
        row_range = slice(block_id * MAXLEN, (block_id + 1) * MAXLEN)
        query_block = split_heads(query[row_range])
        key_block = split_heads(keys[row_range])
        value_block = split_heads(values[row_range])
        scores = block_scores(query_block, key_block, masks[block_id][0], scale)
        peak = jnp.max(scores, axis=-1, keepdims=True)
        log_total = peak + jnp.log(jnp.sum(jnp.exp(scores - peak), axis=-1, keepdims=True))
        probs = jnp.exp(scores - log_total).astype(jnp.bfloat16)
        context_block = jnp.einsum(
            "hqk,khd->qhd", probs, value_block, preferred_element_type=jnp.float32
        )
        contexts.append(context_block.astype(jnp.bfloat16).reshape(MAXLEN, -1))
        log_totals.append(log_total)
    context = jnp.concatenate(contexts, axis=0)
    mixed_part = jnp.dot(context, mixer_weight, preferred_element_type=jnp.float32)
    mixed = lax.psum(mixed_part, "tensor") + mixer_bias.astype(jnp.float32)
    first_in = tokens + mixed
    first = normalize(first_in, first_gain.astype(jnp.float32), first_bias.astype(jnp.float32))
    first_low = first.astype(jnp.bfloat16)
    inner = jnp.dot(
        first_low, inner_weight, preferred_element_type=jnp.float32
    ) + inner_bias.astype(jnp.float32)
    active_full, gelu_pull = jax.vjp(partial(jax.nn.gelu, approximate=False), inner)
    active = active_full.astype(jnp.bfloat16)
    outer_part = jnp.dot(active, outer_weight, preferred_element_type=jnp.float32)
    outer = lax.psum(outer_part, "tensor") + outer_bias.astype(jnp.float32)
    second_in = first + outer
    layer_out = normalize(
        second_in, second_gain.astype(jnp.float32), second_bias.astype(jnp.float32)
    ).astype(jnp.bfloat16)
    live_rows = jnp.concatenate([mask_pair[1] for mask_pair in masks], axis=0)
    grad_out = cotangent.astype(jnp.float32) * live_rows[:, None].astype(jnp.float32)
    grad_second, second_gain_grad, second_bias_grad = norm_backward(
        second_in, second_gain.astype(jnp.float32), grad_out
    )
    outer_bias_grad = jnp.sum(grad_second, axis=0)
    low_outer = grad_second.astype(jnp.bfloat16)
    outer_weight_grad = jnp.einsum(
        "tf,td->fd", active, low_outer, preferred_element_type=jnp.float32
    )
    grad_active = jnp.einsum(
        "td,fd->tf", low_outer, outer_weight, preferred_element_type=jnp.float32
    )
    grad_inner = gelu_pull(grad_active)[0].astype(jnp.bfloat16)
    inner_bias_grad = jnp.sum(grad_inner.astype(jnp.float32), axis=0)
    inner_weight_grad = jnp.einsum(
        "td,tf->df", first_low, grad_inner, preferred_element_type=jnp.float32
    )
    hidden_part = jnp.einsum(
        "tf,df->td", grad_inner, inner_weight, preferred_element_type=jnp.float32
    )
    grad_first = grad_second + lax.psum(hidden_part, "tensor")
    grad_mixed, first_gain_grad, first_bias_grad = norm_backward(
        first_in, first_gain.astype(jnp.float32), grad_first
    )
    mixer_bias_grad = jnp.sum(grad_mixed, axis=0)
    low_mixed = grad_mixed.astype(jnp.bfloat16)
    mixer_weight_grad = jnp.einsum(
        "te,td->ed", context, low_mixed, preferred_element_type=jnp.float32
    )
    grad_context = jnp.einsum(
        "td,ed->te", low_mixed, mixer_weight, preferred_element_type=jnp.float32
    ).astype(jnp.bfloat16)
    query_grads = []
    key_grads = []
    value_grads = []
    for block_id in range(block_count):
        row_range = slice(block_id * MAXLEN, (block_id + 1) * MAXLEN)
        query_block = split_heads(query[row_range])
        key_block = split_heads(keys[row_range])
        value_block = split_heads(values[row_range])
        scores = block_scores(query_block, key_block, masks[block_id][0], scale)
        probs_full = jnp.exp(scores - log_totals[block_id])
        probs = probs_full.astype(jnp.bfloat16)
        upstream = split_heads(grad_context[row_range])
        grad_probs = jnp.einsum(
            "qhd,khd->hqk", upstream, value_block, preferred_element_type=jnp.float32
        )
        grad_value_block = jnp.einsum(
            "hqk,qhd->khd", probs, upstream, preferred_element_type=jnp.float32
        )
        row_delta = jnp.sum(probs_full * grad_probs, axis=-1, keepdims=True)
        grad_scores = (probs_full * (grad_probs - row_delta)).astype(jnp.bfloat16)
        grad_query_block = (
            jnp.einsum("hqk,khd->qhd", grad_scores, key_block, preferred_element_type=jnp.float32)
            * scale
        )
        grad_key_block = (
            jnp.einsum("hqk,qhd->khd", grad_scores, query_block, preferred_element_type=jnp.float32)
            * scale
        )
        query_grads.append(grad_query_block.astype(jnp.bfloat16).reshape(MAXLEN, -1))
        key_grads.append(grad_key_block.astype(jnp.bfloat16).reshape(MAXLEN, -1))
        value_grads.append(grad_value_block.astype(jnp.bfloat16).reshape(MAXLEN, -1))
    grad_query = jnp.concatenate(query_grads, axis=0)
    grad_keys = jnp.concatenate(key_grads, axis=0)
    grad_values = jnp.concatenate(value_grads, axis=0)
    query_weight_grad = jnp.einsum(
        "td,te->de", hidden_in, grad_query, preferred_element_type=jnp.float32
    )
    key_weight_grad = jnp.einsum(
        "td,te->de", hidden_in, grad_keys, preferred_element_type=jnp.float32
    )
    value_weight_grad = jnp.einsum(
        "td,te->de", hidden_in, grad_values, preferred_element_type=jnp.float32
    )
    query_bias_grad = jnp.sum(grad_query.astype(jnp.float32), axis=0)
    value_bias_grad = jnp.sum(grad_values.astype(jnp.float32), axis=0)
    input_part = (
        jnp.einsum("te,de->td", grad_query, query_weight, preferred_element_type=jnp.float32)
        + jnp.einsum("te,de->td", grad_keys, key_weight, preferred_element_type=jnp.float32)
        + jnp.einsum("te,de->td", grad_values, value_weight, preferred_element_type=jnp.float32)
    )
    input_grad = (grad_mixed + lax.psum(input_part, "tensor")).astype(jnp.bfloat16)
    (
        query_weight_grad,
        key_weight_grad,
        value_weight_grad,
        query_bias_grad,
        value_bias_grad,
        mixer_weight_grad,
        mixer_bias_grad,
        first_gain_grad,
        first_bias_grad,
        inner_weight_grad,
        inner_bias_grad,
        outer_weight_grad,
        outer_bias_grad,
        second_gain_grad,
        second_bias_grad,
    ) = lax.psum(
        (
            query_weight_grad,
            key_weight_grad,
            value_weight_grad,
            query_bias_grad,
            value_bias_grad,
            mixer_weight_grad,
            mixer_bias_grad,
            first_gain_grad,
            first_bias_grad,
            inner_weight_grad,
            inner_bias_grad,
            outer_weight_grad,
            outer_bias_grad,
            second_gain_grad,
            second_bias_grad,
        ),
        "dp",
    )
    return (
        layer_out,
        input_grad,
        query_weight_grad,
        key_weight_grad,
        value_weight_grad,
        query_bias_grad,
        value_bias_grad,
        mixer_weight_grad,
        mixer_bias_grad,
        first_gain_grad,
        first_bias_grad,
        inner_weight_grad,
        inner_bias_grad,
        outer_weight_grad,
        outer_bias_grad,
        second_gain_grad,
        second_bias_grad,
    )


def solution(mesh):
    placed = (
        P("dp", None),
        P(None, "tensor"),
        P(None, "tensor"),
        P(None, "tensor"),
        P("tensor"),
        P("tensor"),
        P("tensor", None),
        P(),
        P(),
        P(),
        P(None, "tensor"),
        P("tensor"),
        P("tensor", None),
        P(),
        P(),
        P(),
        P("dp", None),
        P("dp", None),
    )
    return jax.shard_map(
        local,
        mesh=mesh,
        in_specs=placed,
        out_specs=(
            P("dp", None),
            P("dp", None),
            P(None, "tensor"),
            P(None, "tensor"),
            P(None, "tensor"),
            P("tensor"),
            P("tensor"),
            P("tensor", None),
            P(),
            P(),
            P(),
            P(None, "tensor"),
            P("tensor"),
            P("tensor", None),
            P(),
            P(),
            P(),
        ),
        check_vma=False,
    )
```

profile of v0, /device:TPU:0, one launch (start us, length us, event | category | flops | bytes accessed | tf_op | source)
XLA Modules:
  0.0 1139.0 jit_solution(3905697846493004289)
XLA Ops:
  41.6 155.3 %all-reduce.8.cloned.1.call-done = f32[2048,768]{1,0:T(8,128)} async-done(((f32[2048,768]{1,0:T(8,128)}), f32[2048,768]{1,0:T(8,128)}) %all-reduce.8.cloned.1.call-update) | async-done | bytes 6291472 | tf_op jit(solution)/shard_map/psum | solution.py:116
  202.6 34.0 %multiply_convert_fusion = (bf16[2048,1536]{1,0:T(8,128)(2,1)S(1)}, f32[2048,1536]{1,0:T(8,128)}, f32[2048,1536]{1,0:T(8,128)}) fusion(f32[1536]{0:T(1024)S(1)} %convert_element_type.231, bf16[768,1536]{1,0:T(8,128)(2,1)S(1)} %copy-done, f32[2048,768]{1,0:T(8,128)S(1)} %get-tuple-element.86, f32[768]{0:T(1024)S(1)} %convert_element_type.229, ...), kind=kOutput, calls=%fused_computation.4 | convolution fusion | flops 5047320576 | bytes 40136704 | tf_op jit(solution)/shard_map/dot_general | solution.py:120
  239.2 6.9 fusion.69
  246.8 152.6 %all-reduce.10.cloned.1.call-done = f32[2048,768]{1,0:T(8,128)} async-done(((f32[2048,768]{1,0:T(8,128)}), f32[2048,768]{1,0:T(8,128)}) %all-reduce.10.cloned.1.call-update) | async-done | bytes 6291472 | tf_op jit(solution)/shard_map/psum | solution.py:126
  399.5 5.8 fusion.62
  411.4 5.7 fusion.60
  417.1 20.4 %convert_reduce_fusion = (f32[1536]{0:T(1024)}, bf16[2048,1536]{1,0:T(8,128)(2,1)}) fusion(f32[2048,1536]{1,0:T(8,128)} %get-tuple-element.84, bf16[1536,768]{1,0:T(8,128)(2,1)} %param.30, f32[2048,768]{1,0:T(8,128)} %get-tuple-element.77, f32[2048,1536]{1,0:T(8,128)} %get-tuple-element.118, f32[1536]{0:T(1024)S(1)} %convert_element_type.231), kind=kOutput, calls=%fused_computation.2 | convolution fusion | flops 4886886912 | bytes 40120320 | tf_op jit(solution)/shard_map/td,fd->tf/dot_general | solution.py:141
  437.5 9.7 fusion.70
  447.2 153.3 %all-reduce.12.cloned.1.call-done = f32[2048,768]{1,0:T(8,128)} async-done(((f32[2048,768]{1,0:T(8,128)}), f32[2048,768]{1,0:T(8,128)}) %all-reduce.12.cloned.1.call-update) | async-done | bytes 6291472 | tf_op jit(solution)/shard_map/psum | solution.py:152
  600.5 8.3 multiply_reduce_fusion.1
  608.8 4.9 fusion.61
  617.3 4.8 multiply_reduce_fusion.4
  622.1 6.5 multiply_convert_fusion.3
  636.8 4.8 multiply_reduce_fusion.3
  641.7 6.7 multiply_convert_fusion.2
  661.4 6.5 multiply_convert_fusion.4
  680.2 5.2 multiply_convert_fusion.1
  695.8 10.7 fusion.21
  706.5 12.6 %fusion.56 = f32[768,1536]{1,0:T(8,128)} fusion(bf16[2048,1536]{1,0:T(8,128)(2,1)} %get-tuple-element.128, f32[2048,768]{1,0:T(8,128)} %copy-done.2, f32[768]{0:T(1024)S(1)} %copy-done.73, f32[768]{0:T(1024)S(1)} %copy-done.68, f32[2048]{0:T(1024)S(1)} %add_rsqrt_fusion.1, f32[2048]{0:T(1024)S(1)} %broadcast_multiply_fusion.5), kind=kOutput, calls=%fused_computation.168 | convolution fusion | flops 4839702528 | bytes 17324032 | tf_op jit(solution)/shard_map/td,tf->df/dot_general | solution.py:146
  729.6 62.2 %all-reduce = (f32[384]{0:T(512)}, f32[384]{0:T(512)}, f32[768]{0:T(1024)}, f32[768]{0:T(1024)}, f32[768]{0:T(1024)}, /*index=5*/f32[1536]{0:T(1024)}, f32[768]{0:T(1024)}, f32[768]{0:T(1024)}, f32[768]{0:T(1024)}) all-reduce(f32[384]{0:T(512)S(1)} %convert_reduce_fusion.2, ...), channel_id=1, replica_groups=mesh['dp'=16,'tensor'=2] {'dp'}, use_global_device_ids=true, to_apply=%region_32.33 | all-reduce | flops 6912 | bytes 55296 | tf_op jit(solution)/shard_map/psum | solution.py:231
  791.8 57.3 %all-reduce.14.cloned.1.call-done = f32[2048,768]{1,0:T(8,128)} async-done(((f32[2048,768]{1,0:T(8,128)}), f32[2048,768]{1,0:T(8,128)}) %all-reduce.14.cloned.1.call-update) | async-done | bytes 6291472 | tf_op jit(solution)/shard_map/psum | solution.py:214
  849.1 6.9 add_convert_fusion.1
  856.0 259.5 %all-reduce.16.cloned.1.call-done = (f32[768,384]{0,1:T(8,128)}, f32[768,384]{0,1:T(8,128)}, f32[768,384]{0,1:T(8,128)}, f32[384,768]{1,0:T(8,128)}, f32[768,1536]{1,0:T(8,128)}, /*index=5*/f32[1536,768]{1,0:T(8,128)}) async-done(((f32[768,384]{0,1:T(8,128)}, f32[768,384]{0,1:T(8,128)}, f32[768,384]{0,1:T(8,128)}, f32[384,768]{1,0:T(8,128)}, f32[768,1536]{1,0:T(8,128)}, /*index=5*/f32[1536,768]{1,0:T(8,128)}), ...) | async-done | bytes 14155792 | tf_op jit(solution)/shard_map/psum | solution.py:231
  1124.5 5.5 copy.100
  (327 shorter events, 117.4 us)
Async XLA Ops:
  7.2 195.4 %copy-start = (bf16[768,1536]{1,0:T(8,128)(2,1)S(1)}, bf16[768,1536]{1,0:T(8,128)(2,1)}, u32[]{:S(2)}) copy-start(bf16[768,1536]{1,0:T(8,128)(2,1)} %param.28) | copy-start | bytes 7077892
  7.2 189.8 %all-reduce.8.cloned.1.call-start = ((), (), s32[]{:S(2)}) async-start(), calls=%async_computation | async-start | bytes 12582912 | tf_op jit(solution)/shard_map/psum | solution.py:116
  10.0 23.8 %copy-start.13 = (pred[512,512]{0,1:T(8,128)(4,1)}, pred[512,512]{0,1:T(8,128)(4,1)S(1)}, u32[]{:S(2)}) copy-start(pred[512,512]{0,1:T(8,128)(4,1)S(1)} %compare_and_fusion.3) | copy-start | bytes 786436
  10.3 21.8 %copy-start.9 = (pred[512,512]{0,1:T(8,128)(4,1)}, pred[512,512]{0,1:T(8,128)(4,1)S(1)}, u32[]{:S(2)}) copy-start(pred[512,512]{0,1:T(8,128)(4,1)S(1)} %compare_and_fusion.2) | copy-start | bytes 786436
  14.1 14.3 %copy-start.35 = (bf16[512,384]{0,1:T(8,128)(2,1)}, bf16[512,384]{0,1:T(8,128)(2,1)S(1)}, u32[]{:S(2)}) copy-start(bf16[512,384]{0,1:T(8,128)(2,1)S(1)} %get-tuple-element.101) | copy-start | bytes 1179652
  14.1 16.1 %copy-start.37 = (bf16[512,384]{0,1:T(8,128)(2,1)}, bf16[512,384]{0,1:T(8,128)(2,1)S(1)}, u32[]{:S(2)}) copy-start(bf16[512,384]{0,1:T(8,128)(2,1)S(1)} %get-tuple-element.100) | copy-start | bytes 1179652
  14.1 17.9 %copy-start.39 = (bf16[512,384]{0,1:T(8,128)(2,1)}, bf16[512,384]{0,1:T(8,128)(2,1)S(1)}, u32[]{:S(2)}) copy-start(bf16[512,384]{0,1:T(8,128)(2,1)S(1)} %get-tuple-element.102) | copy-start | bytes 1179652
  14.1 19.7 %copy-start.41 = (bf16[512,384]{0,1:T(8,128)(2,1)}, bf16[512,384]{0,1:T(8,128)(2,1)S(1)}, u32[]{:S(2)}) copy-start(bf16[512,384]{0,1:T(8,128)(2,1)S(1)} %get-tuple-element.103) | copy-start | bytes 1179652
  40.9 358.5 %all-reduce.10.cloned.1.call-start = ((), (), s32[]{:S(2)}) async-start(), calls=%async_computation.1 | async-start | bytes 12582912 | tf_op jit(solution)/shard_map/psum | solution.py:126
  41.6 567.2 %copy-start.67 = (f32[768]{0:T(1024)}, f32[768]{0:T(1024)S(1)}, u32[]{:S(2)}) copy-start(f32[768]{0:T(1024)S(1)} %convert_element_type.228) | copy-start | bytes 9220
  41.6 357.9 %copy-start.72 = (f32[768]{0:T(1024)}, f32[768]{0:T(1024)S(1)}, u32[]{:S(2)}) copy-start(f32[768]{0:T(1024)S(1)} %convert_element_type.229) | copy-start | bytes 9220
  201.6 34.9 %copy-start.2 = (f32[2048,768]{1,0:T(8,128)}, f32[2048,768]{1,0:T(8,128)S(1)}, u32[]{:S(2)}) copy-start(f32[2048,768]{1,0:T(8,128)S(1)} %get-tuple-element.86) | copy-start | bytes 18874372
  202.5 36.6 %copy-start.86 = (bf16[1536,768]{1,0:T(8,128)(2,1)S(1)}, bf16[1536,768]{1,0:T(8,128)(2,1)}, u32[]{:S(2)}) copy-start(bf16[1536,768]{1,0:T(8,128)(2,1)} %param.30) | copy-start | bytes 7077892
  246.1 354.4 %all-reduce.12.cloned.1.call-start = ((), (), s32[]{:S(2)}) async-start(), calls=%async_computation.2 | async-start | bytes 12582912 | tf_op jit(solution)/shard_map/psum | solution.py:152
  447.2 401.9 %all-reduce.14.cloned.1.call-start = ((), (), s32[]{:S(2)}) async-start(), calls=%async_computation.3 | async-start | bytes 12582912 | tf_op jit(solution)/shard_map/psum | solution.py:214
  600.5 14.9 %slice-start.6 = ((s8[6291456]{0:T(1024)(128)(4,1)}), s8[4194304]{0:T(1024)(128)(4,1)S(1)}, s32[]{:S(2)}) async-start(s8[6291456]{0:T(1024)(128)(4,1)} %bitcast.146), calls=%async_computation.11 | async-start | bytes 8388608
  617.3 17.7 %slice-start.4 = ((s8[6291456]{0:T(1024)(128)(4,1)}), s8[4194304]{0:T(1024)(128)(4,1)S(1)}, s32[]{:S(2)}) async-start(s8[6291456]{0:T(1024)(128)(4,1)} %bitcast.144), calls=%async_computation.9 | async-start | bytes 8388608
  622.1 12.9 %slice-start.5 = ((s8[6291456]{0:T(1024)(128)(4,1)}), s8[2097152]{0:T(1024)(128)(4,1)S(1)}, s32[]{:S(2)}) async-start(s8[6291456]{0:T(1024)(128)(4,1)} %bitcast.144), calls=%async_computation.10 | async-start | bytes 4194304
  636.8 17.9 %slice-start.2 = ((s8[6291456]{0:T(1024)(128)(4,1)}), s8[4194304]{0:T(1024)(128)(4,1)S(1)}, s32[]{:S(2)}) async-start(s8[6291456]{0:T(1024)(128)(4,1)} %bitcast.142), calls=%async_computation.7 | async-start | bytes 8388608
  641.7 13.1 %slice-start.3 = ((s8[6291456]{0:T(1024)(128)(4,1)}), s8[2097152]{0:T(1024)(128)(4,1)S(1)}, s32[]{:S(2)}) async-start(s8[6291456]{0:T(1024)(128)(4,1)} %bitcast.142), calls=%async_computation.8 | async-start | bytes 4194304
  656.6 17.0 %slice-start = ((s8[6291456]{0:T(1024)(128)(4,1)}), s8[4194304]{0:T(1024)(128)(4,1)S(1)}, s32[]{:S(2)}) async-start(s8[6291456]{0:T(1024)(128)(4,1)} %bitcast.140), calls=%async_computation.5 | async-start | bytes 8388608
  670.9 18.2 %copy-start.55 = (bf16[6,64,512]{2,1,0:T(8,128)(2,1)}, bf16[6,64,512]{2,1,0:T(8,128)(2,1)S(1)}, u32[]{:S(2)}) copy-start(bf16[6,64,512]{2,1,0:T(8,128)(2,1)S(1)} %fusion.28) | copy-start | bytes 1179652
  675.4 15.5 %copy-start.43 = (bf16[6,64,512]{2,1,0:T(8,128)(2,1)}, bf16[6,64,512]{2,1,0:T(8,128)(2,1)S(1)}, u32[]{:S(2)}) copy-start(bf16[6,64,512]{2,1,0:T(8,128)(2,1)S(1)} %convolution_convert_fusion.2) | copy-start | bytes 1179652
  695.8 419.7 %all-reduce.16.cloned.1.call-start = ((), (), s32[]{:S(2)}) async-start(), calls=%async_computation.4 | async-start | bytes 28311552 | tf_op jit(solution)/shard_map/psum | solution.py:231
  (93 other events, 437.4 us)
Sparse Core Ops, SparseCore 0:
  41.1 155.8 all-reduce.7
  246.3 153.1 all-reduce.9
  447.3 153.1 all-reduce.11
  695.9 153.1 all-reduce.13
  855.2 260.1 all-reduce.15
where the time goes:
time: 1150 us; the launch traced here: 1140 us
  waiting for transfers between devices  778 us (68%)
  matrix products  183 us (16%)
  other arithmetic  75.7 us (7%)
  blocking collectives  62.2 us (5%)
  local copies, waits for them, and re-layouts  23.7 us (2%)
  between operations  15.6 us (1%)
    psum x1, waiting for transfers between devices, local(): lax.psum((query_weight_grad, key_weight_grad, value_weight_grad, query_bi...  259 us
    psum x1, waiting for transfers between devices, local(): mixed = lax.psum(mixed_part, 'tensor') + mixer_bias.astype(jnp.float32)  155 us
    psum x1, waiting for transfers between devices, local(): grad_first = grad_second + lax.psum(hidden_part, 'tensor')  153 us
    psum x1, waiting for transfers between devices, local(): outer = lax.psum(outer_part, 'tensor') + outer_bias.astype(jnp.float32)  153 us
    psum x1, blocking collectives, local(): lax.psum((query_weight_grad, key_weight_grad, value_weight_grad, query_bi...  62.2 us
    psum x1, waiting for transfers between devices, local(): lax.psum(input_part, 'tensor')  57.3 us
    dot_general x1, matrix products, local(): jnp.dot(first_low, inner_weight, preferred_element_type=jnp.float32)  34 us
    convert_element_type x4, other arithmetic, local(): grad_scores = (probs_full * (grad_probs - row_delta)).astype(jnp.bfloat16)  24.9 us
  transfers between devices with their start and end apart: 5, of which 5 were waited for; matrix products, arithmetic and copies ran while one was open for 4% of the time, Pallas kernels for 0%

commit v1 on v0

v1 whole, which is shorter than its diff:
```python
import math
from functools import partial

import jax
import jax.numpy as jnp
from jax import lax
from jax.experimental import pallas as pl
from jax.experimental.pallas import tpu as pltpu
from jax.sharding import PartitionSpec as P

HD = 64
MAXLEN = 512
EPSILON = 1e-06
INV_SQRT2 = 1.0 / math.sqrt(2.0)
INV_SQRT_2PI = 1.0 / math.sqrt(2.0 * math.pi)
NEG = -1e30
BF = jnp.bfloat16
F32 = jnp.float32
VMEM_LIMIT = 56 * 1024 * 1024
V_QV, V_MB, V_FG, V_FB, V_IB, V_OB, V_SG, V_SB, V_ROWS = 0, 1, 2, 3, 4, 6, 7, 8, 16


def dot(a, b):
    return lax.dot_general(a, b, (((1,), (0,)), ((), ())), preferred_element_type=F32)


def dot_bt(a, b):
    return lax.dot_general(a, b, (((1,), (1,)), ((), ())), preferred_element_type=F32)


def dot_at(a, b):
    return lax.dot_general(a, b, (((0,), (0,)), ((), ())), preferred_element_type=F32)


def head_lanes(rows):
    return lax.broadcasted_iota(jnp.int32, (rows, 2 * HD), 1) < HD


def params(**kw):
    return pltpu.CompilerParams(vmem_limit_bytes=VMEM_LIMIT, **kw)


def full(shape):
    return pl.BlockSpec(shape, lambda b: (0,) * len(shape), pipeline_mode=pl.Buffered(1))


def rows_spec(cols, rows=MAXLEN):
    return pl.BlockSpec((rows, cols), lambda b: (b, 0))


SMEM = pl.BlockSpec(memory_space=pltpu.SMEM)


def attn_fwd_kernel(len_ref, h_ref, wq_ref, wk_ref, wv_ref, vec_ref, q_ref, k_ref, v_ref, c_ref, l_ref):
    half = wq_ref.shape[1]
    pairs = half // (2 * HD)
    b = pl.program_id(0)
    h = h_ref[...]
    q_ref[...] = (dot(h, wq_ref[...]) + vec_ref[V_QV : V_QV + 1, :half]).astype(BF)
    k_ref[...] = dot(h, wk_ref[...]).astype(BF)
    v_ref[...] = (dot(h, wv_ref[...]) + vec_ref[V_QV : V_QV + 1, half:]).astype(BF)
    l_ref[...] = jnp.zeros_like(l_ref)
    for kind in range(3):

        @pl.when(lax.rem(b, 3) == kind)
        def _():
            span = MAXLEN >> kind
            for seq in range(1 << kind):
                rows = slice(seq * span, (seq + 1) * span)
                live = lax.broadcasted_iota(jnp.int32, (1, span), 1) < len_ref[b, seq]
                bias = jnp.where(live, 0.0, NEG)
                low_lanes = head_lanes(span)
                logs = jnp.zeros((span, 128), F32)
                lane = lax.broadcasted_iota(jnp.int32, (span, 128), 1)
                for pair in range(pairs):
                    cols = slice(pair * 2 * HD, (pair + 1) * 2 * HD)
                    qp = q_ref[rows, cols] * BF(0.125)
                    kp = k_ref[rows, cols]
                    vp = v_ref[rows, cols]
                    outs = []
                    for sub in range(2):
                        qh = jnp.where(low_lanes if sub == 0 else ~low_lanes, qp, BF(0))
                        s = dot_bt(qh, kp) + bias
                        m = jnp.max(s, axis=-1, keepdims=True)
                        e = jnp.exp(s - m)
                        z = jnp.sum(e, axis=-1, keepdims=True)
                        p = (e * (1.0 / z)).astype(BF)
                        logs = jnp.where(lane == 2 * pair + sub, m + jnp.log(z), logs)
                        outs.append(dot(p, vp))
                    c_ref[rows, cols] = jnp.where(low_lanes, outs[0], outs[1]).astype(BF)
                l_ref[:, rows] = logs.T[:8]


def attn_fwd(lengths, hidden, wq, wk, wv, vec):
    n, d = hidden.shape
    half = wq.shape[1]
    blocks = n // MAXLEN
    wide = jax.ShapeDtypeStruct((n, half), BF)
    return pl.pallas_call(
        attn_fwd_kernel,
        grid=(blocks,),
        in_specs=[SMEM, rows_spec(d), full((d, half)), full((d, half)), full((d, half)), full(vec.shape)],
        out_specs=[rows_spec(half)] * 4 + [pl.BlockSpec((8, MAXLEN), lambda b: (b, 0))],
        out_shape=[wide] * 4 + [jax.ShapeDtypeStruct((8 * blocks, MAXLEN), F32)],
        compiler_params=params(),
        cost_estimate=pl.CostEstimate(flops=12_000_000_000, bytes_accessed=16_000_000, transcendentals=0),
        name="attn_fwd",
    )(lengths, hidden, wq, wk, wv, vec)


def live_column(len_ref, b):
    pos = lax.broadcasted_iota(jnp.int32, (MAXLEN, 1), 0)
    kind = lax.rem(b, 3)
    shift = 9 - kind
    seg = lax.shift_right_logical(pos, shift)
    off = pos - lax.shift_left(seg, shift)
    picked = jnp.full((MAXLEN, 1), len_ref[b, 0], jnp.int32)
    for slot in range(1, 4):
        picked = jnp.where(seg == slot, len_ref[b, slot], picked)
    return (off < picked).astype(F32)


def norm_stats(x):
    center = x - jnp.mean(x, axis=-1, keepdims=True)
    inverse = lax.rsqrt(jnp.mean(center * center, axis=-1, keepdims=True) + EPSILON)
    return center * inverse, inverse


def accumulate(ref, value, first_step):
    @pl.when(first_step)
    def _():
        ref[...] = value

    @pl.when(jnp.logical_not(first_step))
    def _():
        ref[...] += value


def ff_fwd_kernel(
    len_ref, h_ref, co_ref, cp_ref, cot_ref, wmo_ref, wmp_ref, wio_ref, wip_ref, woo_ref, wop_ref, vec_ref, pvec_ref,
    out_ref, x_ref, low_ref, gs_ref, lo_ref, gpo_ref, gpp_ref, owg_ref, sums_ref, act_ref, pa_ref, pb_ref,
):
    b = pl.program_id(0)
    d = h_ref.shape[1]
    ff = wio_ref.shape[1]
    width = 512
    pa_ref[...] = dot(co_ref[...], wmo_ref[...])
    pb_ref[...] = dot(cp_ref[...], wmp_ref[...])
    mixed = (pa_ref[...] + pb_ref[...]) + vec_ref[V_MB : V_MB + 1, :]
    x = h_ref[...].astype(F32) + mixed
    x_ref[...] = x
    n1, _ = norm_stats(x)
    first = n1 * vec_ref[V_FG : V_FG + 1, :] + vec_ref[V_FB : V_FB + 1, :]
    low = first.astype(BF)
    low_ref[...] = low
    for wi, wo, vec, gp_ref, part_ref, keep in (
        (wio_ref, woo_ref, vec_ref, gpo_ref, pa_ref, True),
        (wip_ref, wop_ref, pvec_ref, gpp_ref, pb_ref, False),
    ):
        part = None
        for c in range(ff // width):
            cols = slice(c * width, (c + 1) * width)
            row, at = divmod(c * width, d)
            if at + width <= d:
                bias = vec[V_IB + row : V_IB + row + 1, at : at + width]
            else:
                bias = jnp.concatenate(
                    [vec[V_IB + row : V_IB + row + 1, at:], vec[V_IB + row + 1 : V_IB + row + 2, : at + width - d]], axis=1
                )
            inner = dot(low, wi[:, cols]) + bias
            cdf = 0.5 * (1.0 + lax.erf(inner * INV_SQRT2))
            gp_ref[:, cols] = cdf + inner * (jnp.exp(-0.5 * inner * inner) * INV_SQRT_2PI)
            active = (inner * cdf).astype(BF)
            if keep:
                act_ref[:, cols] = active
            term = dot(active, wo[cols, :])
            part = term if part is None else part + term
        part_ref[...] = part
    r = first + ((pa_ref[...] + pb_ref[...]) + vec_ref[V_OB : V_OB + 1, :])
    n2, inv2 = norm_stats(r)
    gain = vec_ref[V_SG : V_SG + 1, :]
    out_ref[...] = (n2 * gain + vec_ref[V_SB : V_SB + 1, :]).astype(BF)
    g = cot_ref[...].astype(F32) * live_column(len_ref, b)
    scaled = g * gain
    gs = inv2 * (
        scaled - jnp.mean(scaled, axis=-1, keepdims=True) - n2 * jnp.mean(scaled * n2, axis=-1, keepdims=True)
    )
    gs_ref[...] = gs
    lo = gs.astype(BF)
    lo_ref[...] = lo
    sums = jnp.concatenate(
        [
            jnp.sum(gs, axis=0, keepdims=True),
            jnp.sum(g * n2, axis=0, keepdims=True),
            jnp.sum(g, axis=0, keepdims=True),
            jnp.zeros((5, d), F32),
        ],
        axis=0,
    )
    accumulate(sums_ref, sums, b == 0)
    accumulate(owg_ref, dot_at(act_ref[...], lo), b == 0)


def ff_fwd(lengths, hidden, co, cp, cot, wmo, wmp, wio, wip, woo, wop, vec, pvec):
    n, d = hidden.shape
    half = co.shape[1]
    ff = wio.shape[1]
    return pl.pallas_call(
        ff_fwd_kernel,
        grid=(n // MAXLEN,),
        in_specs=[
            SMEM, rows_spec(d), rows_spec(half), rows_spec(half), rows_spec(d), full((half, d)), full((half, d)),
            full((d, ff)), full((d, ff)), full((ff, d)), full((ff, d)), full(vec.shape), full(pvec.shape),
        ],
        out_specs=[
            rows_spec(d), rows_spec(d), rows_spec(d), rows_spec(d), rows_spec(d), rows_spec(ff), rows_spec(ff),
            full((ff, d)), full((8, d)),
        ],
        out_shape=[
            jax.ShapeDtypeStruct((n, d), BF),
            jax.ShapeDtypeStruct((n, d), F32),
            jax.ShapeDtypeStruct((n, d), BF),
            jax.ShapeDtypeStruct((n, d), F32),
            jax.ShapeDtypeStruct((n, d), BF),
            jax.ShapeDtypeStruct((n, ff), F32),
            jax.ShapeDtypeStruct((n, ff), F32),
            jax.ShapeDtypeStruct((ff, d), F32),
            jax.ShapeDtypeStruct((8, d), F32),
        ],
        scratch_shapes=[pltpu.VMEM((MAXLEN, ff), BF), pltpu.VMEM((MAXLEN, d), F32), pltpu.VMEM((MAXLEN, d), F32)],
        compiler_params=params(),
        cost_estimate=pl.CostEstimate(flops=30_000_000_000, bytes_accessed=70_000_000, transcendentals=0),
        name="ff_fwd",
    )(lengths, hidden, co, cp, cot, wmo, wmp, wio, wip, woo, wop, vec, pvec)


def ff_bwd_kernel(
    lo_ref, gs_ref, x_ref, low_ref, gpo_ref, gpp_ref, co_ref, wio_ref, wip_ref, woo_ref, wop_ref, vec_ref,
    gm_ref, lm_ref, iwg_ref, mwg_ref, sums_ref, isum_ref, gi_ref, pa_ref, pb_ref,
):
    b = pl.program_id(0)
    d = lo_ref.shape[1]
    ff = wio_ref.shape[1]
    width = 512
    lo = lo_ref[...]
    for wi, wo, gp_ref, part_ref, keep in (
        (wio_ref, woo_ref, gpo_ref, pa_ref, True),
        (wip_ref, wop_ref, gpp_ref, pb_ref, False),
    ):
        part = None
        for c in range(ff // width):
            cols = slice(c * width, (c + 1) * width)
            gi32 = dot_bt(lo, wo[cols, :]) * gp_ref[:, cols]
            gi = gi32.astype(BF)
            if keep:
                gi_ref[:, cols] = gi
            term = dot_bt(gi, wi[:, cols])
            part = term if part is None else part + term
        part_ref[...] = part
    gi = gi_ref[...]
    accumulate(iwg_ref, dot_at(low_ref[...], gi), b == 0)
    accumulate(isum_ref, jnp.sum(gi.astype(F32), axis=0, keepdims=True), b == 0)
    g = gs_ref[...] + (pa_ref[...] + pb_ref[...])
    n1, inv1 = norm_stats(x_ref[...])
    scaled = g * vec_ref[V_FG : V_FG + 1, :]
    gm = inv1 * (
        scaled - jnp.mean(scaled, axis=-1, keepdims=True) - n1 * jnp.mean(scaled * n1, axis=-1, keepdims=True)
    )
    gm_ref[...] = gm
    lm = gm.astype(BF)
    lm_ref[...] = lm
    sums = jnp.concatenate(
        [
            jnp.sum(gm, axis=0, keepdims=True),
            jnp.sum(g * n1, axis=0, keepdims=True),
            jnp.sum(g, axis=0, keepdims=True),
            jnp.zeros((5, d), F32),
        ],
        axis=0,
    )
    accumulate(sums_ref, sums, b == 0)
    accumulate(mwg_ref, dot_at(co_ref[...], lm), b == 0)


def ff_bwd(lo, gs, x, low, gpo, gpp, co, wio, wip, woo, wop, vec):
    n, d = lo.shape
    half = co.shape[1]
    ff = wio.shape[1]
    return pl.pallas_call(
        ff_bwd_kernel,
        grid=(n // MAXLEN,),
        in_specs=[
            rows_spec(d), rows_spec(d), rows_spec(d), rows_spec(d), rows_spec(ff), rows_spec(ff), rows_spec(half),
            full((d, ff)), full((d, ff)), full((ff, d)), full((ff, d)), full(vec.shape),
        ],
        out_specs=[rows_spec(d), rows_spec(d), full((d, ff)), full((half, d)), full((8, d)), full((1, ff))],
        out_shape=[
            jax.ShapeDtypeStruct((n, d), F32),
            jax.ShapeDtypeStruct((n, d), BF),
            jax.ShapeDtypeStruct((d, ff), F32),
            jax.ShapeDtypeStruct((half, d), F32),
            jax.ShapeDtypeStruct((8, d), F32),
            jax.ShapeDtypeStruct((1, ff), F32),
        ],
        scratch_shapes=[pltpu.VMEM((MAXLEN, ff), BF), pltpu.VMEM((MAXLEN, d), F32), pltpu.VMEM((MAXLEN, d), F32)],
        compiler_params=params(),
        cost_estimate=pl.CostEstimate(flops=26_000_000_000, bytes_accessed=60_000_000, transcendentals=0),
        name="ff_bwd",
    )(lo, gs, x, low, gpo, gpp, co, wio, wip, woo, wop, vec)


def attn_bwd_kernel(own, len_ref, lm_ref, wm_ref, q_ref, k_ref, v_ref, l_ref, wq_ref, wk_ref, wv_ref, *rest):
    if own:
        h_ref, part_ref, wg_ref, sums_ref, gc_ref, dq_ref, dk_ref, dv_ref = rest
    else:
        gm_ref, opart_ref, ig_ref, gc_ref, dq_ref, dk_ref, dv_ref, part_ref = rest
    half = wq_ref.shape[1]
    pairs = half // (2 * HD)
    b = pl.program_id(0)
    gc_ref[...] = dot_bt(lm_ref[...], wm_ref[...]).astype(BF)
    for kind in range(3):

        @pl.when(lax.rem(b, 3) == kind)
        def _():
            span = MAXLEN >> kind
            low_lanes = head_lanes(span)
            for seq in range(1 << kind):
                rows = slice(seq * span, (seq + 1) * span)
                live = lax.broadcasted_iota(jnp.int32, (span, 1), 0) < len_ref[b, seq]
                bias = jnp.where(live, 0.0, NEG)
                for pair in range(pairs):
                    cols = slice(pair * 2 * HD, (pair + 1) * 2 * HD)
                    qp = q_ref[rows, cols] * BF(0.125)
                    kp = k_ref[rows, cols]
                    vp = v_ref[rows, cols]
                    up = gc_ref[rows, cols]
                    dqs, dks, dvs = [], [], []
                    for sub in range(2):
                        mask = low_lanes if sub == 0 else ~low_lanes
                        s = dot_bt(kp, jnp.where(mask, qp, BF(0))) + bias
                        p = jnp.exp(s - l_ref[2 * pair + sub : 2 * pair + sub + 1, rows])
                        dp = dot_bt(vp, jnp.where(mask, up, BF(0)))
                        delta = jnp.sum(p * dp, axis=0, keepdims=True)
                        ds = (p * (dp - delta)).astype(BF)
                        dvs.append(dot(p.astype(BF), up))
                        dks.append(dot(ds, qp))
                        dqs.append(dot_at(ds, kp))
                    dv_ref[rows, cols] = jnp.where(low_lanes, dvs[0], dvs[1]).astype(BF)
                    dk_ref[rows, cols] = jnp.where(low_lanes, dks[0], dks[1]).astype(BF)
                    dq_ref[rows, cols] = (jnp.where(low_lanes, dqs[0], dqs[1]) * 0.125).astype(BF)

    dq, dk, dv = dq_ref[...], dk_ref[...], dv_ref[...]
    part = (dot_bt(dq, wq_ref[...]) + dot_bt(dk, wk_ref[...])) + dot_bt(dv, wv_ref[...])
    part_ref[...] = part
    if own:
        sums = jnp.concatenate(
            [jnp.sum(dq.astype(F32), axis=0, keepdims=True), jnp.sum(dv.astype(F32), axis=0, keepdims=True)], axis=1
        )
        accumulate(sums_ref, sums, b == 0)
        h = h_ref[...]
        accumulate(wg_ref, jnp.concatenate([dot_at(h, dq), dot_at(h, dk), dot_at(h, dv)], axis=1), b == 0)
    else:
        ig_ref[...] = (gm_ref[...] + (opart_ref[...] + part_ref[...])).astype(BF)


def attn_bwd(own, lengths, lm, wm, q, k, v, logs, wq, wk, wv, *extra):
    n, d = lm.shape
    half = wq.shape[1]
    if own:
        extra_specs = [rows_spec(d)]
        out_specs = [rows_spec(d), full((d, 3 * half)), full((1, 2 * half))]
        out_shape = [
            jax.ShapeDtypeStruct((n, d), F32),
            jax.ShapeDtypeStruct((d, 3 * half), F32),
            jax.ShapeDtypeStruct((1, 2 * half), F32),
        ]
    else:
        extra_specs = [rows_spec(d), rows_spec(d)]
        out_specs = rows_spec(d)
        out_shape = jax.ShapeDtypeStruct((n, d), BF)
    return pl.pallas_call(
        partial(attn_bwd_kernel, own),
        grid=(n // MAXLEN,),
        in_specs=[
            SMEM, rows_spec(d), full((half, d)), rows_spec(half), rows_spec(half), rows_spec(half),
            pl.BlockSpec((8, MAXLEN), lambda b: (b, 0)), full((d, half)), full((d, half)), full((d, half)), *extra_specs,
        ],
        out_specs=out_specs,
        out_shape=out_shape,
        scratch_shapes=[pltpu.VMEM((MAXLEN, half), BF)] * 4 + ([] if own else [pltpu.VMEM((MAXLEN, d), F32)]),
        compiler_params=params(),
        cost_estimate=pl.CostEstimate(flops=25_000_000_000, bytes_accessed=25_000_000, transcendentals=0),
        name="attn_bwd_own" if own else "attn_bwd_peer",
    )(lengths, lm, wm, q, k, v, logs, wq, wk, wv, *extra)


def cast_kernel(*refs):
    count = len(refs) // 2
    for src, dst in zip(refs[:count], refs[count:]):
        dst[...] = src[...].astype(BF)


def cast_down(arrays):
    return pl.pallas_call(
        cast_kernel,
        out_shape=[jax.ShapeDtypeStruct(a.shape, BF) for a in arrays],
        compiler_params=params(),
        name="cast_down",
    )(*arrays)


def fetch_peer(weights, n_dp):
    me = lax.axis_index("dp")
    got = []
    for w in weights:
        rows = w.shape[0] // n_dp
        piece = lax.dynamic_slice_in_dim(w, me * rows, rows, 0).astype(F32)
        piece = lax.ppermute(piece, "tensor", [(0, 1), (1, 0)])
        got.append(lax.all_gather(piece, "dp", tiled=True))
    return cast_down(got)


def local(
    n_dp, hidden_in, query_weight, key_weight, value_weight, query_bias, value_bias, mixer_weight, mixer_bias,
    first_gain, first_bias, inner_weight, inner_bias, outer_weight, outer_bias, second_gain, second_bias, lengths,
    cotangent,
):
    n, d = hidden_in.shape
    half = query_weight.shape[1]
    ff = inner_weight.shape[1]
    vec = jnp.concatenate(
        [
            query_bias, value_bias, mixer_bias, first_gain, first_bias, inner_bias, outer_bias, second_gain, second_bias,
            jnp.zeros(((V_ROWS - 9) * d,), BF),
        ]
    ).astype(F32).reshape(V_ROWS, d)
    pvec = lax.ppermute(vec, "tensor", [(0, 1), (1, 0)])
    wqp, wkp, wvp, wmp, wip, wop = fetch_peer(
        (query_weight, key_weight, value_weight, mixer_weight, inner_weight, outer_weight), n_dp
    )
    qo, ko, vo, co, lgo = attn_fwd(lengths, hidden_in, query_weight, key_weight, value_weight, vec)
    qp, kp, vp, cp, lgp = attn_fwd(lengths, hidden_in, wqp, wkp, wvp, pvec)
    layer_out, x, low, gs, lo, gpo, gpp, owg, osums = ff_fwd(
        lengths, hidden_in, co, cp, cotangent, mixer_weight, wmp, inner_weight, wip, outer_weight, wop, vec, pvec
    )
    gm, lm, iwg, mwg, isums, ibg = ff_bwd(lo, gs, x, low, gpo, gpp, co, inner_weight, wip, outer_weight, wop, vec)
    part, qkvg, qvsum = attn_bwd(
        True, lengths, lm, mixer_weight, qo, ko, vo, lgo, query_weight, key_weight, value_weight, hidden_in
    )
    input_grad = attn_bwd(False, lengths, lm, wmp, qp, kp, vp, lgp, wqp, wkp, wvp, gm, part)
    small = jnp.concatenate([qvsum.reshape(1, d), isums[:3], osums[:3], ibg.reshape(-1, d)], axis=0)
    owg = lax.psum(owg, "dp")
    iwg = lax.psum(iwg, "dp")
    mwg, qkvg, small = lax.psum((mwg, qkvg, small), "dp")
    return (
        layer_out, input_grad, qkvg[:, :half], qkvg[:, half : 2 * half], qkvg[:, 2 * half :], small[0, :half],
        small[0, half:], mwg, small[1], small[2], small[3], iwg, small[7:].reshape(ff), owg, small[4], small[5],
        small[6],
    )


def solution(mesh):
    col, row, rep = P(None, "tensor"), P("tensor", None), P()
    vec, tok = P("tensor"), P("dp", None)
    return jax.shard_map(
        partial(local, mesh.shape["dp"]),
        mesh=mesh,
        in_specs=(tok, col, col, col, vec, vec, row, rep, rep, rep, col, vec, row, rep, rep, rep, tok, tok),
        out_specs=(tok, tok, col, col, col, vec, vec, row, rep, rep, rep, col, vec, row, rep, rep, rep),
        check_vma=False,
    )
```

time: 1150 us -> 752 us (0.65)
  waiting for transfers between devices: 778 us -> 380 us
  Pallas kernels: 0 us -> 239 us
  matrix products: 183 us -> 0 us
  other arithmetic: 75.7 us -> 5.04 us
  starting transfers between devices: 0.82 us -> 16.1 us
    psum x5 -> x1, waiting for transfers between devices: 778 us -> 160 us  [local(): mwg, qkvg, small = lax.psum((mwg, qkvg, small), 'dp')]
    pallas_call x0 -> x7, Pallas kernels: none -> 239 us  [the longest x2 75.4 us: attn_bwd(): pl.pallas_call(partial(attn_bwd_kernel, own), grid=(n // MAXLEN,), in_spe...]
    all_gather x0 -> x6, waiting for transfers between devices: none -> 200 us  [fetch_peer(): got.append(lax.all_gather(piece, 'dp', tiled=True))]
    dot_general x42 -> x0, matrix products: 183 us -> none  [the longest x1 34 us: local(): jnp.dot(first_low, inner_weight, preferred_element_type=jnp.float32)]
    reduce_sum x16 -> x0, other arithmetic: 41.4 us -> none  [the longest x2 12.5 us: norm_backward(): gain_grad = jnp.sum(upstream * normed, axis=0)]
    convert_element_type x15 -> x6, other arithmetic: 33.3 us -> 4.99 us  [fetch_peer(): piece = lax.dynamic_slice_in_dim(w, me * rows, rows, 0).astype(F32)]
    ppermute x0 -> x7, waiting for transfers between devices: none -> 19.7 us  [the longest x6 19.7 us: fetch_peer(): piece = lax.ppermute(piece, 'tensor', [(0, 1), (1, 0)])]
    ppermute x0 -> x7, starting transfers between devices: none -> 15.8 us  [the longest x6 13.7 us: fetch_peer(): piece = lax.ppermute(piece, 'tensor', [(0, 1), (1, 0)])]
  transfers between devices with their start and end apart: 5 -> 14, of which waited for: 5 -> 12; matrix products, arithmetic and copies ran while one was open for 4% -> 2% of each run, Pallas kernels for 0% -> 9%
where the time goes in v1:
time: 752 us; the launch traced here: 743 us
  waiting for transfers between devices  380 us (51%)
  Pallas kernels  239 us (32%)
  blocking collectives  62.7 us (8%)
  local copies, waits for them, and re-layouts  26 us (3%)
  starting transfers between devices  16.1 us (2%)
  between operations  14.5 us (2%)
    all_gather x6, waiting for transfers between devices, fetch_peer(): got.append(lax.all_gather(piece, 'dp', tiled=True))  200 us
    psum x1, waiting for transfers between devices, local(): mwg, qkvg, small = lax.psum((mwg, qkvg, small), 'dp')  160 us
    pallas_call x2, Pallas kernels, attn_bwd(): pl.pallas_call(partial(attn_bwd_kernel, own), grid=(n // MAXLEN,), in_spe...  75.4 us
    psum x1, blocking collectives, local(): mwg, qkvg, small = lax.psum((mwg, qkvg, small), 'dp')  62.7 us
    pallas_call x1, Pallas kernels, ff_fwd(): pl.pallas_call(ff_fwd_kernel, grid=(n // MAXLEN,), in_specs=[SMEM, rows_s...  57.6 us
    pallas_call x2, Pallas kernels, attn_fwd(): pl.pallas_call(attn_fwd_kernel, grid=(blocks,), in_specs=[SMEM, rows_spec...  49.1 us
    pallas_call x1, Pallas kernels, ff_bwd(): pl.pallas_call(ff_bwd_kernel, grid=(n // MAXLEN,), in_specs=[rows_spec(d)...  48.6 us
    ppermute x6, waiting for transfers between devices, fetch_peer(): piece = lax.ppermute(piece, 'tensor', [(0, 1), (1, 0)])  19.7 us
  transfers between devices with their start and end apart: 14, of which 12 were waited for; matrix products, arithmetic and copies ran while one was open for 2% of the time, Pallas kernels for 9%

profile of v1, /device:TPU:0, one launch (start us, length us, event | category | flops | bytes accessed | tf_op | source)
XLA Modules:
  0.0 743.1 jit_solution(11106823994469579020)
XLA Ops:
  8.0 3.0 collective-permute-start.2
  11.0 2.3 collective-permute-done.2
  16.8 2.3 collective-permute-done.1
  22.7 2.3 collective-permute-done
  28.5 2.6 collective-permute-done.3
  35.0 5.5 collective-permute-done.5
  42.2 2.4 collective-permute-start.4
  44.6 4.7 collective-permute-done.4
  60.3 24.3 %attn_fwd.2 = (bf16[2048,384]{1,0:T(8,128)(2,1)}, bf16[2048,384]{1,0:T(8,128)(2,1)}, bf16[2048,384]{1,0:T(8,128)(2,1)}, bf16[2048,384]{1,0:T(8,128)(2,1)}, f32[32,512]{1,0:T(8,128)}) custom-call(s32[4,4]{1,0:T(4,128)} %len_ref.9, bf16[2048,768]{1,0:T(8,128)(2,1)} %rest_0_.1, bf16[768,384]{1,0:T(8,128)(2,1)} %wq_ref.3, bf16[768,384]{1,0:T(8,128)(2,1)} %wk_ref.3, ...), custom_call_target="tpu_custom_call" | custom-call | flops 12000000000 | bytes 16000000 | tf_op jit(solution)/shard_map/attn_fwd/pallas_call | solution.py:99
  84.6 9.9 %all-gather.9.cloned.1.call-done.refs_1_ = f32[768,384]{1,0:T(8,128)} async-done(((f32[48,384]{1,0:T(8,128)}), f32[768,384]{1,0:T(8,128)}) %all-gather.9.cloned.1.call-update) | async-done | bytes 1179664 | tf_op jit(solution)/shard_map/all_gather | solution.py:419
  94.5 40.3 %all-gather.7.cloned.1.call-done.refs_0_ = f32[768,384]{1,0:T(8,128)} async-done(((f32[48,384]{1,0:T(8,128)}), f32[768,384]{1,0:T(8,128)}) %all-gather.7.cloned.1.call-update) | async-done | bytes 1179664 | tf_op jit(solution)/shard_map/all_gather | solution.py:419
  134.9 40.0 %all-gather.13.cloned.1.call-done.refs_3_ = f32[384,768]{1,0:T(8,128)} async-done(((f32[24,768]{1,0:T(8,128)}), f32[384,768]{1,0:T(8,128)}) %all-gather.13.cloned.1.call-update) | async-done | bytes 1179664 | tf_op jit(solution)/shard_map/all_gather | solution.py:419
  174.9 54.9 %all-gather.17.cloned.1.call-done.refs_5_ = f32[1536,768]{1,0:T(8,128)} async-done(((f32[96,768]{1,0:T(8,128)}), f32[1536,768]{1,0:T(8,128)}) %all-gather.17.cloned.1.call-update) | async-done | bytes 4718608 | tf_op jit(solution)/shard_map/all_gather | solution.py:419
  229.8 54.5 %all-gather.15.cloned.1.call-done.refs_4_ = f32[768,1536]{1,0:T(8,128)} async-done(((f32[48,1536]{1,0:T(8,128)}), f32[768,1536]{1,0:T(8,128)}) %all-gather.15.cloned.1.call-update) | async-done | bytes 4718608 | tf_op jit(solution)/shard_map/all_gather | solution.py:419
  284.3 8.2 %cast_down.1 = (bf16[768,384]{1,0:T(8,128)(2,1)}, bf16[768,384]{1,0:T(8,128)(2,1)}, bf16[768,384]{1,0:T(8,128)(2,1)}, bf16[384,768]{1,0:T(8,128)(2,1)}, bf16[768...) custom-call(f32[768,384]{1,0:T(8,128)} %all-gather.7.cloned.1.call-done.refs_0_, ...), custom_call_target="tpu_custom_call" | custom-call | tf_op jit(solution)/shard_map/cast_down/pallas_call | solution.py:404
  293.1 24.7 %attn_fwd.3 = (bf16[2048,384]{1,0:T(8,128)(2,1)}, bf16[2048,384]{1,0:T(8,128)(2,1)}, bf16[2048,384]{1,0:T(8,128)(2,1)}, bf16[2048,384]{1,0:T(8,128)(2,1)}, f32[32,512]{1,0:T(8,128)}) custom-call(s32[4,4]{1,0:T(4,128)} %len_ref.9, bf16[2048,768]{1,0:T(8,128)(2,1)} %rest_0_.1, bf16[768,384]{1,0:T(8,128)(2,1)} %get-tuple-element.52.wq_ref, ...), custom_call_target="tpu_custom_call" | custom-call | flops 12000000000 | bytes 16000000 | tf_op jit(solution)/shard_map/attn_fwd/pallas_call | solution.py:99
  317.9 57.6 %ff_fwd.1 = (bf16[2048,768]{1,0:T(8,128)(2,1)}, f32[2048,768]{1,0:T(8,128)}, bf16[2048,768]{1,0:T(8,128)(2,1)}, f32[2048,768]{1,0:T(8,128)}, bf16[2048,768]{1,0:...) custom-call(s32[4,4]{1,0:T(4,128)} %len_ref.9, ...), custom_call_target="tpu_custom_call" | custom-call | flops 30000001024 | bytes 70000000 | tf_op jit(solution)/shard_map/ff_fwd/pallas_call | solution.py:208
  375.5 48.6 %ff_bwd.1 = (f32[2048,768]{1,0:T(8,128)}, bf16[2048,768]{1,0:T(8,128)(2,1)}, f32[768,1536]{1,0:T(8,128)}, f32[384,768]{1,0:T(8,128)}, f32[8,768]{1,0:T(8,128)}, /*index=5*/f32[1,1536]{1,0:T(1,128)}) custom-call(bf16[2048,768]{1,0:T(8,128)(2,1)} %get-tuple-element.60.lo_ref, f32[2048,768]{1,0:T(8,128)} %get-tuple-element.61.gs_ref, ...), custom_call_target="tpu_custom_call" | custom-call | flops 25999998976 | bytes 60000000 | tf_op jit(solution)/shard_map/ff_bwd/pallas_call | solution.py:289
  424.0 43.2 %attn_bwd_own.1 = (f32[2048,768]{1,0:T(8,128)}, f32[768,1152]{1,0:T(8,128)}, f32[1,768]{1,0:T(1,128)}) custom-call(s32[4,4]{1,0:T(4,128)} %len_ref.9, bf16[2048,768]{1,0:T(8,128)(2,1)} %get-tuple-element.66.lm_ref, bf16[384,768]{1,0:T(8,128)(2,1)} %wm_ref.1, bf16[2048,384]{1,0:T(8,128)(2,1)} %get-tuple-element.72.q_ref, ...), custom_call_target="tpu_custom_call" | custom-call | flops 24999999488 | bytes 25000000 | tf_op jit(solution)/shard_map/attn_bwd_own/pallas_call | solution.py:381
  468.1 62.7 %psum.36 = f32[9,768]{1,0:T(8,128)S(1)} all-reduce(f32[9,768]{1,0:T(8,128)S(1)} %pad_maximum_fusion), channel_id=1, replica_groups=mesh['dp'=16,'tensor'=2] {'dp'}, use_global_device_ids=true, to_apply=%region_1.0 | all-reduce | flops 6912 | bytes 55296 | tf_op jit(solution)/shard_map/psum | solution.py:454
  532.7 32.2 %attn_bwd_peer.1 = bf16[2048,768]{1,0:T(8,128)(2,1)} custom-call(s32[4,4]{1,0:T(4,128)} %len_ref.9, bf16[2048,768]{1,0:T(8,128)(2,1)} %get-tuple-element.66.lm_ref, bf16[384,768]{1,0:T(8,128)(2,1)} %get-tuple-element.56.wmp_ref.wm_ref, bf16[2048,384]{1,0:T(8,128)(2,1)} %get-tuple-element.67.q_ref, bf16[2048,384]{1,0:T(8,128)(2,1)} %get-tuple-element.68.k_ref, ...), custom_call_target="tpu_custom_call" | custom-call | flops 24999999488 | bytes 25000000 | tf_op jit(solution)/shard_map/attn_bwd_peer/pallas_call | solution.py:381
  564.9 160.4 %all-reduce.3.cloned.1.call-done = (f32[768,1152]{1,0:T(8,128)}, f32[384,768]{1,0:T(8,128)}, f32[768,1536]{1,0:T(8,128)}, f32[1536,768]{1,0:T(8,128)}) async-done(((f32[768,1152]{1,0:T(8,128)}, f32[384,768]{1,0:T(8,128)}, f32[768,1536]{1,0:T(8,128)}, f32[1536,768]{1,0:T(8,128)}), (f32[768,1152]{1,0:T(8,128)}, f32[384,768]{1,0:T(8,128)}, f32[768,1536]{1,0:T(8,128)}, ...) | async-done | bytes 14155792 | tf_op jit(solution)/shard_map/psum | solution.py:454
  725.3 4.0 fusion
  730.5 2.4 copy.50
  (87 shorter events, 35.4 us)
Async XLA Ops:
  7.2 77.4 %all-gather.11.cloned.1.call-start = ((), (), s32[]{:S(2)}) async-start(), calls=%async_computation.2 | async-start | bytes 1253376 | tf_op jit(solution)/shard_map/all_gather | solution.py:419
  8.0 5.3 collective-permute-start.2
  14.0 80.6 %all-gather.9.cloned.1.call-start = ((), (), s32[]{:S(2)}) async-start(), calls=%async_computation.1 | async-start | bytes 1253376 | tf_op jit(solution)/shard_map/all_gather | solution.py:419
  14.8 4.4 collective-permute-start.1
  19.8 115.0 %all-gather.7.cloned.1.call-start = ((), (), s32[]{:S(2)}) async-start(), calls=%async_computation | async-start | bytes 1253376 | tf_op jit(solution)/shard_map/all_gather | solution.py:419
  20.6 4.4 collective-permute-start
  25.7 149.2 %all-gather.13.cloned.1.call-start = ((), (), s32[]{:S(2)}) async-start(), calls=%async_computation.3 | async-start | bytes 1253376 | tf_op jit(solution)/shard_map/all_gather | solution.py:419
  26.5 4.6 collective-permute-start.3
  31.7 198.1 %all-gather.17.cloned.1.call-start = ((), (), s32[]{:S(2)}) async-start(), calls=%async_computation.5 | async-start | bytes 5013504 | tf_op jit(solution)/shard_map/all_gather | solution.py:419
  32.7 7.8 %collective-permute-start.5 = (f32[96,768]{1,0:T(8,128)S(1)}, f32[96,768]{1,0:T(8,128)S(1)}, u32[]{:S(2)}, u32[]{:S(2)}) collective-permute-start(f32[96,768]{1,0:T(8,128)S(1)} %dynamic-slice_convert_fusion), channel_id=1, source_target_pairs={{0,1},{1,0},{2,3},{3,2},{4,5},{5,4},{6,7},{7,6},{8,9},{9,8},{10,11... | collective-permute-start | bytes 884744 | tf_op jit(solution)/shard_map/ppermute | solution.py:418
  41.3 243.1 %all-gather.15.cloned.1.call-start = ((), (), s32[]{:S(2)}) async-start(), calls=%async_computation.4 | async-start | bytes 5013504 | tf_op jit(solution)/shard_map/all_gather | solution.py:419
  42.2 7.1 collective-permute-start.4
  50.0 675.3 %all-reduce.3.cloned.1.call-start = ((), (), s32[]{:S(2)}) async-start(), calls=%async_computation.6 | async-start | bytes 28311552 | tf_op jit(solution)/shard_map/psum | solution.py:454
  58.2 2.1 copy-start.7
  58.2 234.3 %collective-permute-start.6 = (f32[16,768]{1,0:T(8,128)S(1)}, f32[16,768]{1,0:T(8,128)S(1)}, u32[]{:S(2)}, u32[]{:S(2)}) collective-permute-start(f32[16,768]{1,0:T(8,128)S(1)} %reshape.46.vec_ref), channel_id=1, source_target_pairs={{0,1},{1,0},{2,3},{3,2},{4,5},{5,4},{6,7},{7,6},{8,9},{9,8},{10,11... | collective-permute-start | bytes 147464 | tf_op jit(solution)/shard_map/ppermute | solution.py:437
  467.2 0.7 copy-start.8
  467.2 0.7 copy-start.10
  467.3 0.8 copy-start.9
  467.3 0.8 copy-start.11
  725.3 5.1 slice-start.2
  725.3 4.0 copy-start
  725.3 5.2 slice-start.3
  729.3 4.2 slice-start
  730.5 3.4 slice-start.1
  (7 other events, 4.6 us)
Sparse Core Ops, SparseCore 0:
  14.1 40.0 all-gather.10
  57.1 37.4 all-gather.8
  97.4 37.4 all-gather.6
  137.6 37.2 all-gather.12
  177.6 52.1 all-gather.16
  232.5 51.7 all-gather.14
  467.4 257.8 all-reduce.2

commit v2 on v1

--- a/solution.py
+++ b/solution.py
@@ -17,6 +17,7 @@
 BF = jnp.bfloat16
 F32 = jnp.float32
 VMEM_LIMIT = 56 * 1024 * 1024
+PAD = 64
 V_QV, V_MB, V_FG, V_FB, V_IB, V_OB, V_SG, V_SB, V_ROWS = 0, 1, 2, 3, 4, 6, 7, 8, 16
 
 
@@ -44,17 +45,20 @@
     return pl.BlockSpec(shape, lambda b: (0,) * len(shape), pipeline_mode=pl.Buffered(1))
 
 
-def rows_spec(cols, rows=MAXLEN):
-    return pl.BlockSpec((rows, cols), lambda b: (b, 0))
+def rows_spec(cols, start=0):
+    return pl.BlockSpec((MAXLEN, cols), lambda b: (b + start, 0))
 
 
 SMEM = pl.BlockSpec(memory_space=pltpu.SMEM)
-
-
-def attn_fwd_kernel(len_ref, h_ref, wq_ref, wk_ref, wv_ref, vec_ref, q_ref, k_ref, v_ref, c_ref, l_ref):
+ANY = pl.BlockSpec(memory_space=pl.ANY)
+COST = pl.CostEstimate(flops=1_000_000_000, bytes_accessed=1_000_000, transcendentals=0)
+
+
+def attn_fwd_kernel(start, skip, len_ref, h_ref, wq_ref, wk_ref, wv_ref, vec_ref, *rest):
+    q_ref, k_ref, v_ref, c_ref, l_ref = rest[skip:]
     half = wq_ref.shape[1]
     pairs = half // (2 * HD)
-    b = pl.program_id(0)
+    b = pl.program_id(0) + start
     h = h_ref[...]
     q_ref[...] = (dot(h, wq_ref[...]) + vec_ref[V_QV : V_QV + 1, :half]).astype(BF)
     k_ref[...] = dot(h, wk_ref[...]).astype(BF)
@@ -91,21 +95,27 @@
                 l_ref[:, rows] = logs.T[:8]
 
 
-def attn_fwd(lengths, hidden, wq, wk, wv, vec):
+def attn_fwd(lengths, hidden, wq, wk, wv, vec, start, count, prior=None, after=()):
     n, d = hidden.shape
     half = wq.shape[1]
     blocks = n // MAXLEN
     wide = jax.ShapeDtypeStruct((n, half), BF)
+    prior = list(prior or ())
+    extra = prior + list(after)
     return pl.pallas_call(
-        attn_fwd_kernel,
-        grid=(blocks,),
-        in_specs=[SMEM, rows_spec(d), full((d, half)), full((d, half)), full((d, half)), full(vec.shape)],
-        out_specs=[rows_spec(half)] * 4 + [pl.BlockSpec((8, MAXLEN), lambda b: (b, 0))],
+        partial(attn_fwd_kernel, start, len(extra)),
+        grid=(count,),
+        in_specs=[
+            SMEM, rows_spec(d, start), full((d, half)), full((d, half)), full((d, half)), full(vec.shape),
+            *[ANY] * len(extra),
+        ],
+        out_specs=[rows_spec(half, start)] * 4 + [pl.BlockSpec((8, MAXLEN), lambda b: (b + start, 0))],
         out_shape=[wide] * 4 + [jax.ShapeDtypeStruct((8 * blocks, MAXLEN), F32)],
+        input_output_aliases={6 + i: i for i in range(len(prior))},
         compiler_params=params(),
-        cost_estimate=pl.CostEstimate(flops=12_000_000_000, bytes_accessed=16_000_000, transcendentals=0),
+        cost_estimate=COST,
         name="attn_fwd",
-    )(lengths, hidden, wq, wk, wv, vec)
+    )(lengths, hidden, wq, wk, wv, vec, *extra)
 
 
 def live_column(len_ref, b):
@@ -229,38 +239,60 @@
         ],
         scratch_shapes=[pltpu.VMEM((MAXLEN, ff), BF), pltpu.VMEM((MAXLEN, d), F32), pltpu.VMEM((MAXLEN, d), F32)],
         compiler_params=params(),
-        cost_estimate=pl.CostEstimate(flops=30_000_000_000, bytes_accessed=70_000_000, transcendentals=0),
+        cost_estimate=COST,
         name="ff_fwd",
     )(lengths, hidden, co, cp, cot, wmo, wmp, wio, wip, woo, wop, vec, pvec)
 
 
-def ff_bwd_kernel(
-    lo_ref, gs_ref, x_ref, low_ref, gpo_ref, gpp_ref, co_ref, wio_ref, wip_ref, woo_ref, wop_ref, vec_ref,
-    gm_ref, lm_ref, iwg_ref, mwg_ref, sums_ref, isum_ref, gi_ref, pa_ref, pb_ref,
-):
+def ff_bwd_half(lo, wi_ref, wo_ref, gp_ref, gi_ref, part_ref):
+    width = 512
+    part = None
+    for c in range(wi_ref.shape[1] // width):
+        cols = slice(c * width, (c + 1) * width)
+        gi = (dot_bt(lo, wo_ref[cols, :]) * gp_ref[:, cols]).astype(BF)
+        if gi_ref is not None:
+            gi_ref[:, cols] = gi
+        term = dot_bt(gi, wi_ref[:, cols])
+        part = term if part is None else part + term
+    part_ref[...] = part
+
+
+def ff_bwd_own_kernel(lo_ref, low_ref, gp_ref, wi_ref, wo_ref, part_ref, iwg_ref, isum_ref, gi_ref):
     b = pl.program_id(0)
-    d = lo_ref.shape[1]
-    ff = wio_ref.shape[1]
-    width = 512
-    lo = lo_ref[...]
-    for wi, wo, gp_ref, part_ref, keep in (
-        (wio_ref, woo_ref, gpo_ref, pa_ref, True),
-        (wip_ref, wop_ref, gpp_ref, pb_ref, False),
-    ):
-        part = None
-        for c in range(ff // width):
-            cols = slice(c * width, (c + 1) * width)
-            gi32 = dot_bt(lo, wo[cols, :]) * gp_ref[:, cols]
-            gi = gi32.astype(BF)
-            if keep:
-                gi_ref[:, cols] = gi
-            term = dot_bt(gi, wi[:, cols])
-            part = term if part is None else part + term
-        part_ref[...] = part
+    ff_bwd_half(lo_ref[...], wi_ref, wo_ref, gp_ref, gi_ref, part_ref)
     gi = gi_ref[...]
     accumulate(iwg_ref, dot_at(low_ref[...], gi), b == 0)
     accumulate(isum_ref, jnp.sum(gi.astype(F32), axis=0, keepdims=True), b == 0)
-    g = gs_ref[...] + (pa_ref[...] + pb_ref[...])
+
+
+def ff_bwd_own(lo, low, gp, wi, wo):
+    n, d = lo.shape
+    ff = wi.shape[1]
+    return pl.pallas_call(
+        ff_bwd_own_kernel,
+        grid=(n // MAXLEN,),
+        in_specs=[rows_spec(d), rows_spec(d), rows_spec(ff), full((d, ff)), full((ff, d))],
+        out_specs=[rows_spec(d), full((d, ff)), full((1, ff))],
+        out_shape=[
+            jax.ShapeDtypeStruct((n, d), F32),
+            jax.ShapeDtypeStruct((d, ff), F32),
+            jax.ShapeDtypeStruct((1, ff), F32),
+        ],
+        scratch_shapes=[pltpu.VMEM((MAXLEN, ff), BF)],
+        compiler_params=params(),
+        cost_estimate=COST,
+        name="ff_bwd_own",
+    )(lo, low, gp, wi, wo)
+
+
+def ff_bwd_peer_kernel(
+    skip, lo_ref, gs_ref, x_ref, gp_ref, opart_ref, co_ref, wi_ref, wo_ref, vec_ref, *rest
+):
+    gm_ref, lm_ref, mwg_ref, sums_ref, part_ref = rest[skip:]
+    b = pl.program_id(0)
+    d = lo_ref.shape[1]
+    ff_bwd_half(lo_ref[...], wi_ref, wo_ref, gp_ref, None, part_ref)
+    g = gs_ref[...] + (opart_ref[...] + part_ref[...])
     n1, inv1 = norm_stats(x_ref[...])
     scaled = g * vec_ref[V_FG : V_FG + 1, :]
     gm = inv1 * (
@@ -282,41 +314,42 @@
     accumulate(mwg_ref, dot_at(co_ref[...], lm), b == 0)
 
 
-def ff_bwd(lo, gs, x, low, gpo, gpp, co, wio, wip, woo, wop, vec):
+def ff_bwd_peer(lo, gs, x, gp, opart, co, wi, wo, vec, *after):
     n, d = lo.shape
     half = co.shape[1]
-    ff = wio.shape[1]
+    ff = wi.shape[1]
     return pl.pallas_call(
-        ff_bwd_kernel,
+        partial(ff_bwd_peer_kernel, len(after)),
         grid=(n // MAXLEN,),
         in_specs=[
-            rows_spec(d), rows_spec(d), rows_spec(d), rows_spec(d), rows_spec(ff), rows_spec(ff), rows_spec(half),
-            full((d, ff)), full((d, ff)), full((ff, d)), full((ff, d)), full(vec.shape),
-        ],
-        out_specs=[rows_spec(d), rows_spec(d), full((d, ff)), full((half, d)), full((8, d)), full((1, ff))],
+            rows_spec(d), rows_spec(d), rows_spec(d), rows_spec(ff), rows_spec(d), rows_spec(half), full((d, ff)),
+            full((ff, d)), full(vec.shape), *[ANY] * len(after),
+        ],
+        out_specs=[rows_spec(d), rows_spec(d), full((half, d)), full((8, d))],
         out_shape=[
             jax.ShapeDtypeStruct((n, d), F32),
             jax.ShapeDtypeStruct((n, d), BF),
-            jax.ShapeDtypeStruct((d, ff), F32),
             jax.ShapeDtypeStruct((half, d), F32),
             jax.ShapeDtypeStruct((8, d), F32),
-            jax.ShapeDtypeStruct((1, ff), F32),
-        ],
-        scratch_shapes=[pltpu.VMEM((MAXLEN, ff), BF), pltpu.VMEM((MAXLEN, d), F32), pltpu.VMEM((MAXLEN, d), F32)],
+        ],
+        scratch_shapes=[pltpu.VMEM((MAXLEN, d), F32)],
         compiler_params=params(),
-        cost_estimate=pl.CostEstimate(flops=26_000_000_000, bytes_accessed=60_000_000, transcendentals=0),
-        name="ff_bwd",
-    )(lo, gs, x, low, gpo, gpp, co, wio, wip, woo, wop, vec)
-
-
-def attn_bwd_kernel(own, len_ref, lm_ref, wm_ref, q_ref, k_ref, v_ref, l_ref, wq_ref, wk_ref, wv_ref, *rest):
+        cost_estimate=COST,
+        name="ff_bwd_peer",
+    )(lo, gs, x, gp, opart, co, wi, wo, vec, *after)
+
+
+def attn_bwd_kernel(own, start, skip, len_ref, lm_ref, wm_ref, q_ref, k_ref, v_ref, l_ref, wq_ref, wk_ref, wv_ref, *rest):
     if own:
-        h_ref, part_ref, wg_ref, sums_ref, gc_ref, dq_ref, dk_ref, dv_ref = rest
+        h_ref, *given = rest[: 2 if start else 5]
+        rest = rest[2 if start else 5 :][skip:]
+        part_ref, wg_ref, gc_ref, dq_ref, dk_ref, dv_ref = rest
     else:
-        gm_ref, opart_ref, ig_ref, gc_ref, dq_ref, dk_ref, dv_ref, part_ref = rest
+        gm_ref, opart_ref = rest[:2]
+        ig_ref, gc_ref, dq_ref, dk_ref, dv_ref, part_ref = rest[2 + skip :]
     half = wq_ref.shape[1]
     pairs = half // (2 * HD)
-    b = pl.program_id(0)
+    b = pl.program_id(0) + start
     gc_ref[...] = dot_bt(lm_ref[...], wm_ref[...]).astype(BF)
     for kind in range(3):
 
@@ -353,71 +386,159 @@
     part = (dot_bt(dq, wq_ref[...]) + dot_bt(dk, wk_ref[...])) + dot_bt(dv, wv_ref[...])
     part_ref[...] = part
     if own:
+        d = h_ref.shape[1]
         sums = jnp.concatenate(
             [jnp.sum(dq.astype(F32), axis=0, keepdims=True), jnp.sum(dv.astype(F32), axis=0, keepdims=True)], axis=1
         )
-        accumulate(sums_ref, sums, b == 0)
         h = h_ref[...]
-        accumulate(wg_ref, jnp.concatenate([dot_at(h, dq), dot_at(h, dk), dot_at(h, dv)], axis=1), b == 0)
+        first_step = b == start
+
+        @pl.when(first_step)
+        def _():
+            if start:
+                wg_ref[...] = given[0][...]
+                return
+            mwg_ref, fsum_ref, isum_ref, osum_ref = given
+            wg_ref[:d, 3 * half :] = jnp.concatenate([mwg_ref[:, :half], mwg_ref[:, half:]], axis=0)
+            pad = jnp.zeros((1, d), F32)
+            top = jnp.concatenate([pad, fsum_ref[0:1, :]], axis=1)
+            mid = jnp.concatenate([fsum_ref[1:2, :], fsum_ref[2:3, :]], axis=1)
+            low = jnp.concatenate([osum_ref[0:1, :], osum_ref[1:2, :]], axis=1)
+            end = jnp.concatenate([osum_ref[2:3, :], pad], axis=1)
+            wg_ref[d : d + 8, :] = jnp.concatenate(
+                [top, mid, isum_ref[...], low, end, jnp.zeros((3, 2 * d), F32)], axis=0
+            )
+            wg_ref[d + 8 :, :] = jnp.zeros((wg_ref.shape[0] - d - 8, 2 * d), F32)
+
+        for i, grad in enumerate((dq, dk, dv)):
+            value = dot_at(h, grad)
+            cols = slice(i * half, (i + 1) * half)
+
+            if start:
+                wg_ref[:d, cols] += value
+                continue
+
+            @pl.when(first_step)
+            def _(value=value, cols=cols):
+                wg_ref[:d, cols] = value
+
+            @pl.when(jnp.logical_not(first_step))
+            def _(value=value, cols=cols):
+                wg_ref[:d, cols] += value
+
+        wg_ref[d : d + 1, :d] += sums
     else:
         ig_ref[...] = (gm_ref[...] + (opart_ref[...] + part_ref[...])).astype(BF)
 
 
-def attn_bwd(own, lengths, lm, wm, q, k, v, logs, wq, wk, wv, *extra):
+def attn_bwd(own, start, count, lengths, lm, wm, q, k, v, logs, wq, wk, wv, extra, prior=None, after=()):
     n, d = lm.shape
     half = wq.shape[1]
+    after = ([] if prior is None else [prior]) + list(after)
     if own:
-        extra_specs = [rows_spec(d)]
-        out_specs = [rows_spec(d), full((d, 3 * half)), full((1, 2 * half))]
-        out_shape = [
-            jax.ShapeDtypeStruct((n, d), F32),
-            jax.ShapeDtypeStruct((d, 3 * half), F32),
-            jax.ShapeDtypeStruct((1, 2 * half), F32),
-        ]
+        extra_specs = [rows_spec(d, start)] + [full(x.shape) for x in extra[1:]]
+        out_specs = [rows_spec(d, start), full((d + PAD, 4 * half))]
+        out_shape = [jax.ShapeDtypeStruct((n, d), F32), jax.ShapeDtypeStruct((d + PAD, 4 * half), F32)]
     else:
-        extra_specs = [rows_spec(d), rows_spec(d)]
-        out_specs = rows_spec(d)
-        out_shape = jax.ShapeDtypeStruct((n, d), BF)
+        extra_specs = [rows_spec(d, start)] * 2
+        out_specs = [rows_spec(d, start)]
+        out_shape = [jax.ShapeDtypeStruct((n, d), BF)]
     return pl.pallas_call(
-        partial(attn_bwd_kernel, own),
-        grid=(n // MAXLEN,),
+        partial(attn_bwd_kernel, own, start, len(after)),
+        grid=(count,),
         in_specs=[
-            SMEM, rows_spec(d), full((half, d)), rows_spec(half), rows_spec(half), rows_spec(half),
-            pl.BlockSpec((8, MAXLEN), lambda b: (b, 0)), full((d, half)), full((d, half)), full((d, half)), *extra_specs,
+            SMEM, rows_spec(d, start), full((half, d)), rows_spec(half, start), rows_spec(half, start),
+            rows_spec(half, start), pl.BlockSpec((8, MAXLEN), lambda b: (b + start, 0)), full((d, half)),
+            full((d, half)), full((d, half)), *extra_specs, *[ANY] * len(after),
         ],
         out_specs=out_specs,
         out_shape=out_shape,
+        input_output_aliases={} if prior is None else {10 + len(extra): 0},
         scratch_shapes=[pltpu.VMEM((MAXLEN, half), BF)] * 4 + ([] if own else [pltpu.VMEM((MAXLEN, d), F32)]),
         compiler_params=params(),
-        cost_estimate=pl.CostEstimate(flops=25_000_000_000, bytes_accessed=25_000_000, transcendentals=0),
+        cost_estimate=COST,
         name="attn_bwd_own" if own else "attn_bwd_peer",
-    )(lengths, lm, wm, q, k, v, logs, wq, wk, wv, *extra)
-
-
-def cast_kernel(*refs):
-    count = len(refs) // 2
-    for src, dst in zip(refs[:count], refs[count:]):
-        dst[...] = src[...].astype(BF)
-
-
-def cast_down(arrays):
+    )(lengths, lm, wm, q, k, v, logs, wq, wk, wv, *extra, *after)
+
+
+CORE, NEAR, FAR = 1, 2, 4
+TENSOR_SWAP = [(0, 1), (1, 0)]
+
+
+def bit_of(mask):
+    return (lax.axis_index("dp") & mask) != 0
+
+
+def swap(x, mask, n_dp):
+    return lax.ppermute(x, "dp", [(i, i ^ mask) for i in range(n_dp)])
+
+
+def in_order(mask, mine, other):
+    return jnp.where(bit_of(mask), jnp.concatenate([other, mine]), jnp.concatenate([mine, other]))
+
+
+def away(x, mask):
+    rows = x.shape[0] // 2
+    return lax.dynamic_slice_in_dim(x, jnp.where(bit_of(mask), 0, rows), rows, 0)
+
+
+def kept(x, mask):
+    rows = x.shape[0] // 2
+    return lax.dynamic_slice_in_dim(x, jnp.where(bit_of(mask), rows, 0), rows, 0)
+
+
+def beyond(x, n_dp):
+    mask = 4 * FAR
+    while mask < n_dp:
+        x = x + swap(x, mask, n_dp)
+        mask *= 2
+    return x
+
+
+def piece(arrays, masks, base, rows):
+    index = jnp.int32(0)
+    for mask in masks:
+        index = index * 2 + bit_of(mask).astype(jnp.int32)
+    cut = [lax.dynamic_slice_in_dim(a, base + index * rows, rows, 0) for a in arrays]
+    return jnp.concatenate(cut, axis=1).astype(F32)
+
+
+def tie(*arrays):
+    return lax.optimization_barrier(arrays)
+
+
+def assemble_kernel(square, a_ref, ra_ref, b_ref, rb_ref, *outs):
+    rows = a_ref.shape[0]
+    odd = lax.axis_index("dp") & CORE
+    for base, mine, other in ((0, a_ref, ra_ref), (2 * rows, b_ref, rb_ref)):
+        for ref, side in ((mine, odd), (other, 1 - odd)):
+            at = pl.ds(pl.multiple_of(base + side * rows, 16), rows)
+            if not square:
+                outs[0][at, :] = ref[...].astype(BF)
+                continue
+            half = ref.shape[1] // 4
+            for i in range(3):
+                outs[i][at, :] = ref[:, i * half : (i + 1) * half].astype(BF)
+            at = pl.ds(pl.multiple_of(side * rows, 16), rows)
+            left = base == 0
+            cols = slice(0, half) if left else slice(half, 2 * half)
+            outs[3][at, cols] = ref[:, 3 * half :].astype(BF)
+
+
+def assemble(square, a, ra, b, rb):
+    rows, cols = 4 * a.shape[0], a.shape[1]
+    half = cols // 4
+    if square:
+        shapes = [(rows, half)] * 3 + [(rows // 2, 2 * half)]
+    else:
+        shapes = [(rows, cols)]
     return pl.pallas_call(
-        cast_kernel,
-        out_shape=[jax.ShapeDtypeStruct(a.shape, BF) for a in arrays],
+        partial(assemble_kernel, square),
+        out_shape=[jax.ShapeDtypeStruct(shape, BF) for shape in shapes],
         compiler_params=params(),
-        name="cast_down",
-    )(*arrays)
-
-
-def fetch_peer(weights, n_dp):
-    me = lax.axis_index("dp")
-    got = []
-    for w in weights:
-        rows = w.shape[0] // n_dp
-        piece = lax.dynamic_slice_in_dim(w, me * rows, rows, 0).astype(F32)
-        piece = lax.ppermute(piece, "tensor", [(0, 1), (1, 0)])
-        got.append(lax.all_gather(piece, "dp", tiled=True))
-    return cast_down(got)
+        cost_estimate=COST,
+        name="assemble",
+    )(a, ra, b, rb)
 
 
 def local(
@@ -434,28 +555,125 @@
             jnp.zeros(((V_ROWS - 9) * d,), BF),
         ]
     ).astype(F32).reshape(V_ROWS, d)
-    pvec = lax.ppermute(vec, "tensor", [(0, 1), (1, 0)])
-    wqp, wkp, wvp, wmp, wip, wop = fetch_peer(
-        (query_weight, key_weight, value_weight, mixer_weight, inner_weight, outer_weight), n_dp
-    )
-    qo, ko, vo, co, lgo = attn_fwd(lengths, hidden_in, query_weight, key_weight, value_weight, vec)
-    qp, kp, vp, cp, lgp = attn_fwd(lengths, hidden_in, wqp, wkp, wvp, pvec)
+    heads = [query_weight, key_weight, value_weight, jnp.concatenate([mixer_weight[:, :half], mixer_weight[:, half:]])]
+    sixteenth = d // 16
+    h_out = jnp.concatenate(
+        [piece(heads, (CORE, FAR, NEAR), 0, sixteenth), piece(heads, (CORE, NEAR, FAR), d // 2, sixteenth)]
+    )
+    i_out = jnp.concatenate(
+        [
+            piece([inner_weight], (CORE, FAR, NEAR), 0, sixteenth),
+            piece([inner_weight], (CORE, NEAR, FAR), d // 2, sixteenth),
+        ]
+    )
+    eighth = ff // 8
+    o_out = jnp.concatenate(
+        [piece([outer_weight], (CORE, NEAR), 0, eighth), piece([outer_weight], (CORE, FAR), ff // 2, eighth)]
+    )
+    pvec = lax.ppermute(vec, "tensor", TENSOR_SWAP)
+    h_out, pvec = tie(h_out, pvec)
+    h0 = lax.ppermute(h_out, "tensor", TENSOR_SWAP)
+    own = list(attn_fwd(lengths, hidden_in, query_weight, key_weight, value_weight, vec, 0, 2))
+    h0, i_out, own[0] = tie(h0, i_out, own[0])
+    i0 = lax.ppermute(i_out, "tensor", TENSOR_SWAP)
+    ha, hb = h0[:sixteenth], h0[sixteenth:]
+    hra, hrb = swap(ha, NEAR, n_dp), swap(hb, FAR, n_dp)
+    qo, ko, vo, co, lgo = attn_fwd(
+        lengths, hidden_in, query_weight, key_weight, value_weight, vec, 2, 2, own, (ha, hb)
+    )
+    hra, hrb, i0, co, o_out = tie(hra, hrb, i0, co, o_out)
+    ha, hb = in_order(NEAR, ha, hra), in_order(FAR, hb, hrb)
+    hra, hrb = swap(ha, FAR, n_dp), swap(hb, NEAR, n_dp)
+    o0 = lax.ppermute(o_out, "tensor", TENSOR_SWAP)
+    ia, ib = i0[:sixteenth], i0[sixteenth:]
+    ira, irb = swap(ia, NEAR, n_dp), swap(ib, FAR, n_dp)
+    ha, hb = in_order(FAR, ha, hra), in_order(NEAR, hb, hrb)
+    hra, hrb = swap(ha, CORE, n_dp), swap(hb, CORE, n_dp)
+    ha, hb, ira, irb = tie(ha, hb, ira, irb)
+    ia, ib = in_order(NEAR, ia, ira), in_order(FAR, ib, irb)
+    ira, irb = swap(ia, FAR, n_dp), swap(ib, NEAR, n_dp)
+    wqp, wkp, wvp, wmp = assemble(True, ha, hra, hb, hrb)
+    peer = list(attn_fwd(lengths, hidden_in, wqp, wkp, wvp, pvec, 0, 2, None, (ia, ib)))
+    ira, irb, o0, peer[0] = tie(ira, irb, o0, peer[0])
+    ia, ib = in_order(FAR, ia, ira), in_order(NEAR, ib, irb)
+    ira, irb = swap(ia, CORE, n_dp), swap(ib, CORE, n_dp)
+    oa, ob = o0[:eighth], o0[eighth:]
+    ora, orb = swap(oa, NEAR, n_dp), swap(ob, FAR, n_dp)
+    qp, kp, vp, cp, lgp = attn_fwd(lengths, hidden_in, wqp, wkp, wvp, pvec, 2, 2, peer, (ia, ib, oa, ob))
+    ora, orb, cp = tie(ora, orb, cp)
+    oa, ob = in_order(NEAR, oa, ora), in_order(FAR, ob, orb)
+    ora, orb = swap(oa, CORE, n_dp), swap(ob, CORE, n_dp)
+    (wip,) = assemble(False, ia, ira, ib, irb)
+    (wop,) = assemble(False, oa, ora, ob, orb)
     layer_out, x, low, gs, lo, gpo, gpp, owg, osums = ff_fwd(
         lengths, hidden_in, co, cp, cotangent, mixer_weight, wmp, inner_weight, wip, outer_weight, wop, vec, pvec
     )
-    gm, lm, iwg, mwg, isums, ibg = ff_bwd(lo, gs, x, low, gpo, gpp, co, inner_weight, wip, outer_weight, wop, vec)
-    part, qkvg, qvsum = attn_bwd(
-        True, lengths, lm, mixer_weight, qo, ko, vo, lgo, query_weight, key_weight, value_weight, hidden_in
-    )
-    input_grad = attn_bwd(False, lengths, lm, wmp, qp, kp, vp, lgp, wqp, wkp, wvp, gm, part)
-    small = jnp.concatenate([qvsum.reshape(1, d), isums[:3], osums[:3], ibg.reshape(-1, d)], axis=0)
-    owg = lax.psum(owg, "dp")
-    iwg = lax.psum(iwg, "dp")
-    mwg, qkvg, small = lax.psum((mwg, qkvg, small), "dp")
+    o = swap(away(owg, CORE), CORE, n_dp)
+    opart, iwg, ibg = ff_bwd_own(lo, low, gpo, inner_weight, outer_weight)
+    o, owg, iwg = tie(o, owg, iwg)
+    i = swap(away(iwg, CORE), CORE, n_dp)
+    o1 = kept(owg, CORE) + o
+    o_out = away(o1, NEAR)
+    o = swap(o_out, NEAR, n_dp)
+    gm, lm, mwg, isums = ff_bwd_peer(lo, gs, x, gpp, opart, co, wip, wop, vec, o_out)
+    o, i, lm = tie(o, i, lm)
+    o2 = kept(o1, NEAR) + o
+    o_out = away(o2, FAR)
+    o = swap(o_out, FAR, n_dp)
+    i1 = kept(iwg, CORE) + i
+    i_out = away(i1, NEAR)
+    i = swap(i_out, NEAR, n_dp)
+    own = (lengths, lm, mixer_weight, qo, ko, vo, lgo, query_weight, key_weight, value_weight)
+    part, hg = attn_bwd(True, 0, 2, *own, (hidden_in, mwg, isums, ibg, osums), None, (o_out, i_out))
+    o, hg = tie(o, hg)
+    o3 = kept(o2, FAR) + o
+    o = swap(o3, 2 * FAR, n_dp) if n_dp > 2 * FAR else jnp.zeros_like(o3)
+    part, hg = attn_bwd(True, 2, 2, *own, (hidden_in, hg), part, (o3,))
+    i, o, hg = tie(i, o, hg)
+    h = swap(away(hg, CORE), CORE, n_dp)
+    i2 = kept(i1, NEAR) + i
+    i_out = away(i2, FAR)
+    i = swap(i_out, FAR, n_dp)
+    o = beyond(o3 + o, n_dp)
+    o_ = swap(o, FAR, n_dp)
+    h1 = kept(hg, CORE) + h
+    ha, hb = h1[:, :d], h1[:, d:]
+    ha_out, hb_out = away(ha, NEAR), away(hb, FAR)
+    hra, hrb = swap(ha_out, NEAR, n_dp), swap(hb_out, FAR, n_dp)
+    peer = (lengths, lm, wmp, qp, kp, vp, lgp, wqp, wkp, wvp)
+    (input_grad,) = attn_bwd(False, 0, 2, *peer, (gm, part), None, (o, i_out, ha_out, hb_out))
+    hra, hrb, i, o_, input_grad = tie(hra, hrb, i, o_, input_grad)
+    ha, hb = kept(ha, NEAR) + hra, kept(hb, FAR) + hrb
+    ha_out, hb_out = away(ha, FAR), away(hb, NEAR)
+    hra, hrb = swap(ha_out, FAR, n_dp), swap(hb_out, NEAR, n_dp)
+    i3 = kept(i2, FAR) + i
+    i = swap(i3, 2 * FAR, n_dp) if n_dp > 2 * FAR else jnp.zeros_like(i3)
+    o = in_order(FAR, o, o_)
+    o_ = swap(o, NEAR, n_dp)
+    (input_grad,) = attn_bwd(False, 2, 2, *peer, (gm, part), input_grad, (ha_out, hb_out, i3, o))
+    hra, hrb, i, o_, input_grad = tie(hra, hrb, i, o_, input_grad)
+    h = jnp.concatenate([kept(ha, FAR) + hra, kept(hb, NEAR) + hrb])
+    if n_dp > 2 * FAR:
+        h = h + swap(h, 2 * FAR, n_dp)
+    h = beyond(h, n_dp)
+    i = beyond(i3 + i, n_dp)
+    i = in_order(FAR, i, swap(i, FAR, n_dp))
+    o = in_order(NEAR, o, o_)
+    owg = in_order(CORE, o, swap(o, CORE, n_dp))
+    i = in_order(NEAR, i, swap(i, NEAR, n_dp))
+    iwg = in_order(CORE, i, swap(i, CORE, n_dp))
+    rows = h.shape[0] // 2
+    ha, hb = h[:rows], h[rows:]
+    ha, hb = in_order(FAR, ha, swap(ha, FAR, n_dp)), in_order(NEAR, hb, swap(hb, NEAR, n_dp))
+    ha, hb = in_order(NEAR, ha, swap(ha, NEAR, n_dp)), in_order(FAR, hb, swap(hb, FAR, n_dp))
+    hg = jnp.concatenate(
+        [in_order(CORE, ha, swap(ha, CORE, n_dp)), in_order(CORE, hb, swap(hb, CORE, n_dp))], axis=1
+    )
+    small = hg[d : d + 5].reshape(10, d)
     return (
-        layer_out, input_grad, qkvg[:, :half], qkvg[:, half : 2 * half], qkvg[:, 2 * half :], small[0, :half],
-        small[0, half:], mwg, small[1], small[2], small[3], iwg, small[7:].reshape(ff), owg, small[4], small[5],
-        small[6],
+        layer_out, input_grad, hg[:d, :half], hg[:d, half : 2 * half], hg[:d, 2 * half : 3 * half], small[0, :half],
+        small[0, half:], jnp.concatenate([hg[:half, 3 * half :], hg[half:d, 3 * half :]], axis=1), small[1], small[2],
+        small[3], iwg, small[4:6].reshape(ff), owg, small[6], small[7], small[8],
     )
 
 

time: 752 us -> 507 us (0.67)
  waiting for transfers between devices: 380 us -> 114 us
  blocking collectives: 62.7 us -> 0 us
  other arithmetic: 5.04 us -> 42.4 us
  Pallas kernels: 239 us -> 263 us
  starting transfers between devices: 16.1 us -> 39.8 us
  between operations: 14.5 us -> 2.01 us
  local copies, waits for them, and re-layouts: 26 us -> 37.4 us
    all_gather x6 -> x0, waiting for transfers between devices: 200 us -> none  [fetch_peer(): got.append(lax.all_gather(piece, 'dp', tiled=True))]
    psum x1 -> x0, waiting for transfers between devices: 160 us -> none  [local(): mwg, qkvg, small = lax.psum((mwg, qkvg, small), 'dp')]
    ppermute x7 -> x46, waiting for transfers between devices: 19.7 us -> 114 us  [the longest x42 106 us: swap(): return lax.ppermute(x, 'dp', [(i, i ^ mask) for i in range(n_dp)])]
    psum x1 -> x0, blocking collectives: 62.7 us -> none  [local(): mwg, qkvg, small = lax.psum((mwg, qkvg, small), 'dp')]
    pallas_call x6 -> x13, Pallas kernels: 181 us -> 206 us  [the longest x4 88.2 us: attn_bwd(): pl.pallas_call(partial(attn_bwd_kernel, own, start, len(after)), grid=(co...]
    ppermute x7 -> x46, starting transfers between devices: 15.8 us -> 39.8 us  [the longest x42 33.5 us: swap(): return lax.ppermute(x, 'dp', [(i, i ^ mask) for i in range(n_dp)])]
    select_n x0 -> x22, other arithmetic: none -> 20.3 us  [in_order(): jnp.where(bit_of(mask), jnp.concatenate([other, mine]), jnp.concatenate([...]
    add x0 -> x14, other arithmetic: none -> 18.6 us  [the longest x1 2.76 us: local(): i1 = kept(iwg, CORE) + i]
  transfers between devices with their start and end apart: 14 -> 46, of which waited for: 12 -> 15; matrix products, arithmetic and copies ran while one was open for 2% -> 9% of each run, Pallas kernels for 9% -> 40%
where the time goes in v2:
time: 507 us; the launch traced here: 498 us
  Pallas kernels  263 us (52%)
  waiting for transfers between devices  114 us (22%)
  other arithmetic  42.4 us (8%)
  starting transfers between devices  39.8 us (8%)
  local copies, waits for them, and re-layouts  37.4 us (7%)
    ppermute x42, waiting for transfers between devices, swap(): return lax.ppermute(x, 'dp', [(i, i ^ mask) for i in range(n_dp)])  106 us
    pallas_call x4, Pallas kernels, attn_bwd(): pl.pallas_call(partial(attn_bwd_kernel, own, start, len(after)), grid=(co...  88.2 us
    pallas_call x1, Pallas kernels, ff_fwd(): pl.pallas_call(ff_fwd_kernel, grid=(n // MAXLEN,), in_specs=[SMEM, rows_s...  57.6 us
    pallas_call x4, Pallas kernels, attn_fwd(): pl.pallas_call(partial(attn_fwd_kernel, start, len(extra)), grid=(count,)...  54.9 us
    ppermute x42, starting transfers between devices, swap(): return lax.ppermute(x, 'dp', [(i, i ^ mask) for i in range(n_dp)])  33.5 us
    pallas_call x1, Pallas kernels, ff_bwd_own(): pl.pallas_call(ff_bwd_own_kernel, grid=(n // MAXLEN,), in_specs=[rows_spe...  25.7 us
    pallas_call x1, Pallas kernels, ff_bwd_peer(): pl.pallas_call(partial(ff_bwd_peer_kernel, len(after)), grid=(n // MAXLEN...  24.9 us
    select_n x22, other arithmetic, in_order(): jnp.where(bit_of(mask), jnp.concatenate([other, mine]), jnp.concatenate([...  20.3 us
  transfers between devices with their start and end apart: 46, of which 15 were waited for; matrix products, arithmetic and copies ran while one was open for 9% of the time, Pallas kernels for 40%

profile of v2, /device:TPU:0, one launch (start us, length us, event | category | flops | bytes accessed | tf_op | source)
XLA Modules:
  0.0 498.5 jit_solution(15530439268551563150)
XLA Ops:
  15.9 10.6 %attn_fwd.4 = (bf16[2048,384]{1,0:T(8,128)(2,1)}, bf16[2048,384]{1,0:T(8,128)(2,1)}, bf16[2048,384]{1,0:T(8,128)(2,1)}, bf16[2048,384]{1,0:T(8,128)(2,1)}, f32[32,512]{1,0:T(8,128)}) custom-call(s32[4,4]{1,0:T(4,128)} %len_ref.17, bf16[2048,768]{1,0:T(8,128)(2,1)} %rest_0_.3, bf16[768,384]{1,0:T(8,128)(2,1)} %wq_ref.7, bf16[768,384]{1,0:T(8,128)(2,1)} %wk_ref.7, ...), custom_call_target="tpu_custom_call" | custom-call | flops 1000000000 | bytes 1000000 | tf_op jit(solution)/shard_map/attn_fwd/pallas_call | solution.py:105
  34.5 16.7 %attn_fwd.5 = (bf16[2048,384]{1,0:T(8,128)(2,1)}, bf16[2048,384]{1,0:T(8,128)(2,1)}, bf16[2048,384]{1,0:T(8,128)(2,1)}, bf16[2048,384]{1,0:T(8,128)(2,1)}, f32[32,512]{1,0:T(8,128)}) custom-call(s32[4,4]{1,0:T(4,128)} %len_ref.17, bf16[2048,768]{1,0:T(8,128)(2,1)} %rest_0_.3, ...), custom_call_target="tpu_custom_call", output_to_operand_aliasing={{0}: (6, {}), {1}: (7, {}), {2}: (8, {}), {3}: (9, {}), {4}... | custom-call | flops 1000000000 | bytes 1000000 | tf_op jit(solution)/shard_map/attn_fwd/pallas_call | solution.py:105
  56.7 11.7 %collective-permute-done.6 = f32[96,1536]{1,0:T(8,128)S(1)} collective-permute-done((f32[96,1536]{1,0:T(8,128)S(1)}, f32[96,1536]{1,0:T(8,128)S(1)}, u32[]{:S(2)}, u32[]{:S(2)}) %collective-permute-start.6) | collective-permute-done | bytes 589856 | tf_op jit(solution)/shard_map/ppermute | solution.py:473
  76.9 4.0 assemble.3
  80.9 11.0 %attn_fwd.6 = (bf16[2048,384]{1,0:T(8,128)(2,1)}, bf16[2048,384]{1,0:T(8,128)(2,1)}, bf16[2048,384]{1,0:T(8,128)(2,1)}, bf16[2048,384]{1,0:T(8,128)(2,1)}, f32[32,512]{1,0:T(8,128)}) custom-call(s32[4,4]{1,0:T(4,128)} %len_ref.17, bf16[2048,768]{1,0:T(8,128)(2,1)} %rest_0_.3, bf16[768,384]{1,0:T(8,128)(2,1)} %get-tuple-element.122.wq_ref, ...), custom_call_target="tpu_custom_call" | custom-call | flops 1000000000 | bytes 1000000 | tf_op jit(solution)/shard_map/attn_fwd/pallas_call | solution.py:105
  91.9 5.4 %collective-permute-done.11 = f32[384,768]{1,0:T(8,128)S(1)} collective-permute-done((f32[384,768]{1,0:T(8,128)S(1)}, f32[384,768]{1,0:T(8,128)S(1)}, u32[]{:S(2)}, u32[]{:S(2)}) %collective-permute-start.11) | collective-permute-done | bytes 1179680 | tf_op jit(solution)/shard_map/ppermute | solution.py:587
  102.2 16.6 %attn_fwd.7 = (bf16[2048,384]{1,0:T(8,128)(2,1)}, bf16[2048,384]{1,0:T(8,128)(2,1)}, bf16[2048,384]{1,0:T(8,128)(2,1)}, bf16[2048,384]{1,0:T(8,128)(2,1)}, f32[32,512]{1,0:T(8,128)}) custom-call(s32[4,4]{1,0:T(4,128)} %len_ref.17, bf16[2048,768]{1,0:T(8,128)(2,1)} %rest_0_.3, ...), custom_call_target="tpu_custom_call", output_to_operand_aliasing={{0}: (6, {}), {1}: (7, {}), {2}: (8, {}), {3}: (9, {}), {4}... | custom-call | flops 1000000000 | bytes 1000000 | tf_op jit(solution)/shard_map/attn_fwd/pallas_call | solution.py:105
  121.9 4.0 assemble.4.wip_ref.wi_ref
  125.9 4.0 assemble.5.wop_ref.wo_ref
  129.9 57.6 %ff_fwd.1 = (bf16[2048,768]{1,0:T(8,128)(2,1)}, f32[2048,768]{1,0:T(8,128)}, bf16[2048,768]{1,0:T(8,128)(2,1)}, f32[2048,768]{1,0:T(8,128)}, bf16[2048,768]{1,0:...) custom-call(s32[4,4]{1,0:T(4,128)} %len_ref.17, ...), custom_call_target="tpu_custom_call" | custom-call | flops 1000000000 | bytes 1000000 | tf_op jit(solution)/shard_map/ff_fwd/pallas_call | solution.py:218
  191.1 25.7 %ff_bwd_own.1 = (f32[2048,768]{1,0:T(8,128)}, f32[768,1536]{1,0:T(8,128)}, f32[1,1536]{1,0:T(1,128)}) custom-call(bf16[2048,768]{1,0:T(8,128)(2,1)} %get-tuple-element.142.lo_ref, bf16[2048,768]{1,0:T(8,128)(2,1)} %get-tuple-element.143.low_ref, f32[2048,1536]{1,0:T(8,128)} %get-tuple-element.144.gp_ref, bf16[768,1536]{1,0:T(8,128)(2,1)} %wi_ref.1, ...), custom_call_target="tpu_custom_call" | custom-call | flops 1000000000 | bytes 1000000 | tf_op jit(solution)/shard_map/ff_bwd_own/pallas_call | solution.py:271
  216.8 4.1 constant_dynamic-slice_fusion.8
  224.9 24.9 %ff_bwd_peer.1 = (f32[2048,768]{1,0:T(8,128)}, bf16[2048,768]{1,0:T(8,128)(2,1)}, f32[384,768]{1,0:T(8,128)}, f32[8,768]{1,0:T(8,128)}) custom-call(bf16[2048,768]{1,0:T(8,128)(2,1)} %get-tuple-element.142.lo_ref, f32[2048,768]{1,0:T(8,128)} %get-tuple-element.149.gs_ref, f32[2048,768]{1,0:T(8,128)} %get-tuple-element.150.x_ref, ...), custom_call_target="tpu_custom_call" | custom-call | flops 1000000000 | bytes 1000000 | tf_op jit(solution)/shard_map/ff_bwd_peer/pallas_call | solution.py:321
  260.7 24.7 %attn_bwd_own.2 = (f32[2048,768]{1,0:T(8,128)}, f32[832,1536]{1,0:T(8,128)}) custom-call(s32[4,4]{1,0:T(4,128)} %len_ref.17, bf16[2048,768]{1,0:T(8,128)(2,1)} %get-tuple-element.156.lm_ref, bf16[384,768]{1,0:T(8,128)(2,1)} %wm_ref.3, bf16[2048,384]{1,0:T(8,128)(2,1)} %get-tuple-element.157.q_ref, bf16[2048,384]{1,0:T(8,128)(2,1)} %get-tuple-element.158.k_ref, ...), custom_call_target="tpu_custom_call" | custom-call | flops 1000000000 | bytes 1000000 | tf_op jit(solution)/shard_map/attn_bwd_own/pallas_call | solution.py:446
  288.1 26.3 %attn_bwd_own.3 = (f32[2048,768]{1,0:T(8,128)}, f32[832,1536]{1,0:T(8,128)}) custom-call(s32[4,4]{1,0:T(4,128)} %len_ref.17, bf16[2048,768]{1,0:T(8,128)(2,1)} %get-tuple-element.156.lm_ref, bf16[384,768]{1,0:T(8,128)(2,1)} %wm_ref.3, bf16[2048,384]{1,0:T(8,128)(2,1)} %get-tuple-element.157.q_ref, ...), custom_call_target="tpu_custom_call", output_to_operand_aliasing={{0}: (12, {})} | custom-call | flops 1000000000 | bytes 1000000 | tf_op jit(solution)/shard_map/attn_bwd_own/pallas_call | solution.py:446
  330.9 17.5 %attn_bwd_peer.2.rest_2_ = bf16[2048,768]{1,0:T(8,128)(2,1)} custom-call(s32[4,4]{1,0:T(4,128)} %len_ref.17, bf16[2048,768]{1,0:T(8,128)(2,1)} %get-tuple-element.156.lm_ref, bf16[384,768]{1,0:T(8,128)(2,1)} %get-tuple-element.137.wmp_ref.wm_ref, bf16[2048,384]{1,0:T(8,128)(2,1)} %get-tuple-element.173.q_ref, bf16[2048,384]{1,0:T(8,128)(2,1)} %get-tuple-element.174.k_ref, ...), custom_call_target="tpu_custom_call" | custom-call | flops 1000000000 | bytes 1000000 | tf_op jit(solution)/shard_map/attn_bwd_peer/pallas_call | solution.py:446
  348.4 13.8 %collective-permute-done.29 = f32[96,1536]{1,0:T(8,128)} collective-permute-done((f32[96,1536]{1,0:T(8,128)S(1)}, f32[96,1536]{1,0:T(8,128)}, u32[]{:S(2)}, u32[]{:S(2)}) %collective-permute-start.29) | collective-permute-done | bytes 589856 | tf_op jit(solution)/shard_map/ppermute | solution.py:473
  371.0 19.7 %attn_bwd_peer.3 = bf16[2048,768]{1,0:T(8,128)(2,1)} custom-call(s32[4,4]{1,0:T(4,128)} %len_ref.17, bf16[2048,768]{1,0:T(8,128)(2,1)} %get-tuple-element.156.lm_ref, bf16[384,768]{1,0:T(8,128)(2,1)} %get-tuple-element.137.wmp_ref.wm_ref, bf16[2048,384]{1,0:T(8,128)(2,1)} %get-tuple-element.173.q_ref, ...), custom_call_target="tpu_custom_call", output_to_operand_aliasing={{}: (12, {})} | custom-call | flops 1000000000 | bytes 1000000 | tf_op jit(solution)/shard_map/attn_bwd_peer/pallas_call | solution.py:446
  390.7 6.3 %collective-permute-done.32 = f32[104,768]{1,0:T(8,128)} collective-permute-done((f32[104,768]{1,0:T(8,128)S(1)}, f32[104,768]{1,0:T(8,128)}, u32[]{:S(2)}, u32[]{:S(2)}) %collective-permute-start.32) | collective-permute-done | bytes 319520 | tf_op jit(solution)/shard_map/ppermute | solution.py:473
  404.2 24.6 %collective-permute-done.35 = f32[208,768]{1,0:T(8,128)S(1)} collective-permute-done((f32[208,768]{1,0:T(8,128)S(1)}, f32[208,768]{1,0:T(8,128)S(1)}, u32[]{:S(2)}, u32[]{:S(2)}) %collective-permute-start.35) | collective-permute-done | bytes 639008 | tf_op jit(solution)/shard_map/ppermute | solution.py:473
  431.3 8.2 %collective-permute-done.39 = f32[104,768]{1,0:T(8,128)S(1)} collective-permute-done((f32[104,768]{1,0:T(8,128)S(1)}, f32[104,768]{1,0:T(8,128)S(1)}, u32[]{:S(2)}, u32[]{:S(2)}) %collective-permute-start.39) | collective-permute-done | bytes 319520 | tf_op jit(solution)/shard_map/ppermute | solution.py:473
  441.3 12.8 %collective-permute-done.40 = f32[208,768]{1,0:T(8,128)S(1)} collective-permute-done((f32[208,768]{1,0:T(8,128)S(1)}, f32[208,768]{1,0:T(8,128)S(1)}, u32[]{:S(2)}, u32[]{:S(2)}) %collective-permute-start.40) | collective-permute-done | bytes 639008 | tf_op jit(solution)/shard_map/ppermute | solution.py:473
  454.3 23.2 %collective-permute-done.37 = f32[208,768]{1,0:T(8,128)S(1)} collective-permute-done((f32[208,768]{1,0:T(8,128)S(1)}, f32[208,768]{1,0:T(8,128)S(1)}, u32[]{:S(2)}, u32[]{:S(2)}) %collective-permute-start.37) | collective-permute-done | bytes 639008 | tf_op jit(solution)/shard_map/ppermute | solution.py:473
  491.1 6.9 %maximum_select_fusion = f32[768,1536]{1,0:T(8,128)} fusion(f32[384,1536]{1,0:T(8,128)} %maximum_select_fusion.4, f32[384,1536]{1,0:T(8,128)} %collective-permute-done.44, pred[]{:T(512)S(6)} %ne.6), kind=kLoop, calls=%fused_computation | loop fusion | flops 3538944 | bytes 9437185 | tf_op jit(solution)/shard_map/jit(_where)/select_n | solution.py:477
  (249 shorter events, 116.1 us)
Async XLA Ops:
  29.6 21.6 %collective-permute-start.4 = (f32[96,1536]{1,0:T(8,128)S(1)}, f32[96,1536]{1,0:T(8,128)S(1)}, u32[]{:S(2)}, u32[]{:S(2)}) collective-permute-start(f32[96,1536]{1,0:T(8,128)S(1)} %maximum_convert_fusion.2), channel_id=1, source_target_pairs={{0,1},{1,0},{2,3},{3,2},{4,5},{5,4},{6,7},{7,6},{8,9},{9,8},{10,11... | collective-permute-start | bytes 1769480 | tf_op jit(solution)/shard_map/ppermute | solution.py:578
  30.0 21.2 %collective-permute-start.2 = (f32[48,1536]{1,0:T(8,128)S(1)}, f32[48,1536]{1,0:T(8,128)S(1)}, u32[]{:S(2)}, u32[]{:S(2)}) collective-permute-start(f32[48,1536]{1,0:T(8,128)S(1)} %get-tuple-element.214.rest_5_), channel_id=1, source_target_pairs={{0,4},{2,6},{4,0},{6,2},{8,12},{10,14},{12,8},{14,10},{16,20},{18,... | collective-permute-start | bytes 884744 | tf_op jit(solution)/shard_map/ppermute | solution.py:473
  69.2 28.1 %collective-permute-start.11 = (f32[384,768]{1,0:T(8,128)S(1)}, f32[384,768]{1,0:T(8,128)S(1)}, u32[]{:S(2)}, u32[]{:S(2)}) collective-permute-start(f32[384,768]{1,0:T(8,128)S(1)} %maximum_convert_fusion), channel_id=1, source_target_pairs={{0,1},{1,0},{2,3},{3,2},{4,5},{5,4},{6,7},{7,6},{8,9},{9,8},{10,11... | collective-permute-start | bytes 3538952 | tf_op jit(solution)/shard_map/ppermute | solution.py:587
  97.4 21.4 %collective-permute-start.14 = (f32[192,768]{1,0:T(8,128)S(1)}, f32[192,768]{1,0:T(8,128)S(1)}, u32[]{:S(2)}, u32[]{:S(2)}) collective-permute-start(f32[192,768]{1,0:T(8,128)S(1)} %get-tuple-element.208.rest_7_), channel_id=1, source_target_pairs={{0,4},{2,6},{4,0},{6,2},{8,12},{10,14},{12,8},{14,10},{16,20},{18,... | collective-permute-start | bytes 1769480 | tf_op jit(solution)/shard_map/ppermute | solution.py:473
  190.8 26.0 %collective-permute-start.20 = (f32[768,768]{1,0:T(8,128)}, f32[768,768]{1,0:T(8,128)S(1)}, u32[]{:S(2)}, u32[]{:S(2)}) collective-permute-start(f32[768,768]{1,0:T(8,128)} %constant_dynamic-slice_fusion.10), channel_id=1, source_target_pairs={{0,2},{2,0},{4,6},{6,4},{8,10},{10,8},{12,14},{14,12},{16,18},{18,... | collective-permute-start | bytes 7077896 | tf_op jit(solution)/shard_map/ppermute | solution.py:473
  220.9 31.3 %collective-permute-start.22 = (f32[384,1536]{1,0:T(8,128)}, f32[384,1536]{1,0:T(8,128)}, u32[]{:S(2)}, u32[]{:S(2)}) collective-permute-start(f32[384,1536]{1,0:T(8,128)} %constant_dynamic-slice_fusion.8), channel_id=1, source_target_pairs={{0,2},{2,0},{4,6},{6,4},{8,10},{10,8},{12,14},{14,12},{16,18},{18,... | collective-permute-start | bytes 7077896 | tf_op jit(solution)/shard_map/ppermute | solution.py:473
  223.9 28.3 %collective-permute-start.21 = (f32[384,768]{1,0:T(8,128)S(1)}, f32[384,768]{1,0:T(8,128)}, u32[]{:S(2)}, u32[]{:S(2)}) collective-permute-start(f32[384,768]{1,0:T(8,128)S(1)} %constant_dynamic-slice_fusion.9.rest_0_), channel_id=1, source_target_pairs={{0,4},{2,6},{4,0},{6,2},{8,12},{10,14},{12,8},{14,10},{16,20},{18,... | collective-permute-start | bytes 3538952 | tf_op jit(solution)/shard_map/ppermute | solution.py:473
  254.7 30.7 %collective-permute-start.24 = (f32[192,768]{1,0:T(8,128)S(1)}, f32[192,768]{1,0:T(8,128)S(1)}, u32[]{:S(2)}, u32[]{:S(2)}) collective-permute-start(f32[192,768]{1,0:T(8,128)S(1)} %constant_dynamic-slice_fusion.6.rest_5_), channel_id=1, source_target_pairs={{0,8},{2,10},{4,12},{6,14},{8,0},{10,2},{12,4},{14,6},{16,24},{18,... | collective-permute-start | bytes 1769480 | tf_op jit(solution)/shard_map/ppermute | solution.py:473
  260.1 54.3 %collective-permute-start.23 = (f32[192,1536]{1,0:T(8,128)}, f32[192,1536]{1,0:T(8,128)}, u32[]{:S(2)}, u32[]{:S(2)}) collective-permute-start(f32[192,1536]{1,0:T(8,128)} %constant_dynamic-slice_fusion.7.rest_6_), channel_id=1, source_target_pairs={{0,4},{2,6},{4,0},{6,2},{8,12},{10,14},{12,8},{14,10},{16,20},{18,... | collective-permute-start | bytes 3538952 | tf_op jit(solution)/shard_map/ppermute | solution.py:473
  285.5 29.0 %collective-permute-start.25 = (f32[192,768]{1,0:T(8,128)S(1)}, f32[192,768]{1,0:T(8,128)S(1)}, u32[]{:S(2)}, u32[]{:S(2)}) collective-permute-start(f32[192,768]{1,0:T(8,128)S(1)} %dynamic-slice_add_fusion.8.rest_3_), channel_id=1, source_target_pairs={{0,16},{2,18},{4,20},{6,22},{8,24},{10,26},{12,28},{14,30},{16,0},... | collective-permute-start | bytes 1769480 | tf_op jit(solution)/shard_map/ppermute | solution.py:473
  320.0 28.4 %collective-permute-start.30 = (f32[192,768]{1,0:T(8,128)S(1)}, f32[192,768]{1,0:T(8,128)S(1)}, u32[]{:S(2)}, u32[]{:S(2)}) collective-permute-start(f32[192,768]{1,0:T(8,128)S(1)} %add.132.rest_2_), channel_id=1, source_target_pairs={{0,8},{2,10},{4,12},{6,14},{8,0},{10,2},{12,4},{14,6},{16,24},{18,... | collective-permute-start | bytes 1769480 | tf_op jit(solution)/shard_map/ppermute | solution.py:473
  326.3 36.0 %collective-permute-start.28 = (f32[208,768]{1,0:T(8,128)S(1)}, f32[208,768]{1,0:T(8,128)}, u32[]{:S(2)}, u32[]{:S(2)}) collective-permute-start(f32[208,768]{1,0:T(8,128)S(1)} %constant_dynamic-slice_fusion.3.rest_5_), channel_id=1, source_target_pairs={{0,8},{2,10},{4,12},{6,14},{8,0},{10,2},{12,4},{14,6},{16,24},{18,... | collective-permute-start | bytes 1916936 | tf_op jit(solution)/shard_map/ppermute | solution.py:473
  328.1 34.2 %collective-permute-start.27 = (f32[208,768]{1,0:T(8,128)}, f32[208,768]{1,0:T(8,128)}, u32[]{:S(2)}, u32[]{:S(2)}) collective-permute-start(f32[208,768]{1,0:T(8,128)} %constant_dynamic-slice_fusion.4.rest_4_), channel_id=1, source_target_pairs={{0,4},{2,6},{4,0},{6,2},{8,12},{10,14},{12,8},{14,10},{16,20},{18,... | collective-permute-start | bytes 1916936 | tf_op jit(solution)/shard_map/ppermute | solution.py:473
  329.6 32.6 %collective-permute-start.29 = (f32[96,1536]{1,0:T(8,128)S(1)}, f32[96,1536]{1,0:T(8,128)}, u32[]{:S(2)}, u32[]{:S(2)}) collective-permute-start(f32[96,1536]{1,0:T(8,128)S(1)} %constant_dynamic-slice_fusion.2.rest_3_), channel_id=1, source_target_pairs={{0,8},{2,10},{4,12},{6,14},{8,0},{10,2},{12,4},{14,6},{16,24},{18,... | collective-permute-start | bytes 1769480 | tf_op jit(solution)/shard_map/ppermute | solution.py:473
  362.4 34.6 %collective-permute-start.34 = (f32[384,768]{1,0:T(8,128)S(1)}, f32[384,768]{1,0:T(8,128)}, u32[]{:S(2)}, u32[]{:S(2)}) collective-permute-start(f32[384,768]{1,0:T(8,128)S(1)} %maximum_select_fusion.14.rest_6_), channel_id=1, source_target_pairs={{0,4},{2,6},{4,0},{6,2},{8,12},{10,14},{12,8},{14,10},{16,20},{18,... | collective-permute-start | bytes 3538952 | tf_op jit(solution)/shard_map/ppermute | solution.py:473
  365.1 31.9 %collective-permute-start.33 = (f32[96,1536]{1,0:T(8,128)S(1)}, f32[96,1536]{1,0:T(8,128)}, u32[]{:S(2)}, u32[]{:S(2)}) collective-permute-start(f32[96,1536]{1,0:T(8,128)S(1)} %dynamic-slice_add_fusion.7.rest_5_), channel_id=1, source_target_pairs={{0,16},{2,18},{4,20},{6,22},{8,24},{10,26},{12,28},{14,30},{16,0},... | collective-permute-start | bytes 1769480 | tf_op jit(solution)/shard_map/ppermute | solution.py:473
  367.2 29.8 %collective-permute-start.32 = (f32[104,768]{1,0:T(8,128)S(1)}, f32[104,768]{1,0:T(8,128)}, u32[]{:S(2)}, u32[]{:S(2)}) collective-permute-start(f32[104,768]{1,0:T(8,128)S(1)} %constant_dynamic-slice_fusion.rest_4_), channel_id=1, source_target_pairs={{0,4},{2,6},{4,0},{6,2},{8,12},{10,14},{12,8},{14,10},{16,20},{18,... | collective-permute-start | bytes 958472 | tf_op jit(solution)/shard_map/ppermute | solution.py:473
  369.9 27.1 %collective-permute-start.31 = (f32[104,768]{1,0:T(8,128)}, f32[104,768]{1,0:T(8,128)}, u32[]{:S(2)}, u32[]{:S(2)}) collective-permute-start(f32[104,768]{1,0:T(8,128)} %constant_dynamic-slice_fusion.1.rest_3_), channel_id=1, source_target_pairs={{0,8},{2,10},{4,12},{6,14},{8,0},{10,2},{12,4},{14,6},{16,24},{18,... | collective-permute-start | bytes 958472 | tf_op jit(solution)/shard_map/ppermute | solution.py:473
  399.2 29.7 %collective-permute-start.35 = (f32[208,768]{1,0:T(8,128)S(1)}, f32[208,768]{1,0:T(8,128)S(1)}, u32[]{:S(2)}, u32[]{:S(2)}) collective-permute-start(f32[208,768]{1,0:T(8,128)S(1)} %pad_maximum_fusion.1), channel_id=1, source_target_pairs={{0,16},{2,18},{4,20},{6,22},{8,24},{10,26},{12,28},{14,30},{16,0},... | collective-permute-start | bytes 1916936 | tf_op jit(solution)/shard_map/ppermute | solution.py:473
  401.1 29.4 %collective-permute-start.42 = (f32[96,1536]{1,0:T(8,128)S(1)}, f32[96,1536]{1,0:T(8,128)S(1)}, u32[]{:S(2)}, u32[]{:S(2)}) collective-permute-start(f32[96,1536]{1,0:T(8,128)S(1)} %add.139), channel_id=1, source_target_pairs={{0,8},{2,10},{4,12},{6,14},{8,0},{10,2},{12,4},{14,6},{16,24},{18,... | collective-permute-start | bytes 1769480 | tf_op jit(solution)/shard_map/ppermute | solution.py:473
  404.2 75.6 %collective-permute-start.45 = (f32[768,768]{1,0:T(8,128)S(1)}, f32[768,768]{1,0:T(8,128)S(1)}, u32[]{:S(2)}, u32[]{:S(2)}) collective-permute-start(f32[768,768]{1,0:T(8,128)S(1)} %maximum_select_fusion.5), channel_id=1, source_target_pairs={{0,2},{2,0},{4,6},{6,4},{8,10},{10,8},{12,14},{14,12},{16,18},{18,... | collective-permute-start | bytes 7077896 | tf_op jit(solution)/shard_map/ppermute | solution.py:473
  430.7 47.0 %collective-permute-start.43 = (f32[192,1536]{1,0:T(8,128)S(1)}, f32[192,1536]{1,0:T(8,128)S(1)}, u32[]{:S(2)}, u32[]{:S(2)}) collective-permute-start(f32[192,1536]{1,0:T(8,128)S(1)} %maximum_select_fusion.15), channel_id=1, source_target_pairs={{0,4},{2,6},{4,0},{6,2},{8,12},{10,14},{12,8},{14,10},{16,20},{18,... | collective-permute-start | bytes 3538952 | tf_op jit(solution)/shard_map/ppermute | solution.py:473
  439.8 37.7 %collective-permute-start.37 = (f32[208,768]{1,0:T(8,128)S(1)}, f32[208,768]{1,0:T(8,128)S(1)}, u32[]{:S(2)}, u32[]{:S(2)}) collective-permute-start(f32[208,768]{1,0:T(8,128)S(1)} %maximum_select_fusion.16), channel_id=1, source_target_pairs={{0,4},{2,6},{4,0},{6,2},{8,12},{10,14},{12,8},{14,10},{16,20},{18,... | collective-permute-start | bytes 1916936 | tf_op jit(solution)/shard_map/ppermute | solution.py:473
  454.2 28.2 %collective-permute-start.41 = (f32[416,768]{1,0:T(8,128)S(1)}, f32[416,768]{1,0:T(8,128)S(1)}, u32[]{:S(2)}, u32[]{:S(2)}) collective-permute-start(f32[416,768]{1,0:T(8,128)S(1)} %maximum_select_fusion.7), channel_id=1, source_target_pairs={{0,2},{2,0},{4,6},{6,4},{8,10},{10,8},{12,14},{14,12},{16,18},{18,... | collective-permute-start | bytes 3833864 | tf_op jit(solution)/shard_map/ppermute | solution.py:473
  (64 other events, 491.5 us)

commit v3 on v2

v3 whole, which is shorter than its diff:
```python
import math
from functools import partial

import jax
import jax.numpy as jnp
from jax import lax
from jax.experimental import pallas as pl
from jax.experimental.pallas import tpu as pltpu
from jax.sharding import PartitionSpec as P

HD = 64
MAXLEN = 512
EPSILON = 1e-06
INV_SQRT2 = 1.0 / math.sqrt(2.0)
INV_SQRT_2PI = 1.0 / math.sqrt(2.0 * math.pi)
NEG = -1e30
FWD_GROUP = (1, 6, 6)
BWD_GROUP = (2, 6, 6)
BF = jnp.bfloat16
F32 = jnp.float32
VMEM_LIMIT = 56 * 1024 * 1024
PAD = 32
V_QV, V_MB, V_FG, V_FB, V_IB, V_OB, V_SG, V_SB = (0, 0), (0, 1), (1, 0), (1, 1), 2, (3, 0), (3, 1), (4, 0)


def vector(ref, place):
    row, side = place
    d = ref.shape[1] // 2
    return ref[row : row + 1, side * d : (side + 1) * d]


def dot(a, b):
    return lax.dot_general(a, b, (((1,), (0,)), ((), ())), preferred_element_type=F32)


def dot_bt(a, b):
    return lax.dot_general(a, b, (((1,), (1,)), ((), ())), preferred_element_type=F32)


def dot_at(a, b):
    return lax.dot_general(a, b, (((0,), (0,)), ((), ())), preferred_element_type=F32)


def core_halves(size):
    core = lax.axis_index("dp") & 1
    return [pl.ds(pl.multiple_of(side * size, 128), size) for side in (core, 1 - core)]


def head_lanes(rows):
    return lax.broadcasted_iota(jnp.int32, (rows, 2 * HD), 1) < HD


def params(**kw):
    return pltpu.CompilerParams(vmem_limit_bytes=VMEM_LIMIT, **kw)


def full(shape):
    return pl.BlockSpec(shape, lambda b: (0,) * len(shape), pipeline_mode=pl.Buffered(1))


def rows_spec(cols, start=0):
    return pl.BlockSpec((MAXLEN, cols), lambda b: (b + start, 0))


SMEM = pl.BlockSpec(memory_space=pltpu.SMEM)
ANY = pl.BlockSpec(memory_space=pl.ANY)


def cost(us):
    return pl.CostEstimate(flops=int(us * 1e9), bytes_accessed=1_000_000, transcendentals=0)


def attn_fwd_kernel(start, skip, len_ref, h_ref, wq_ref, wk_ref, wv_ref, vec_ref, *rest):
    q_ref, k_ref, v_ref, c_ref, l_ref = rest[skip:]
    half = wq_ref.shape[1]
    pairs = half // (2 * HD)
    b = pl.program_id(0) + start
    h = h_ref[...]
    q_ref[...] = (dot(h, wq_ref[...]) + vec_ref[0:1, :half]).astype(BF)
    k_ref[...] = dot(h, wk_ref[...]).astype(BF)
    v_ref[...] = (dot(h, wv_ref[...]) + vec_ref[0:1, half : 2 * half]).astype(BF)
    l_ref[...] = jnp.zeros_like(l_ref)
    for kind in range(3):

        @pl.when(lax.rem(b, 3) == kind)
        def _():
            span = MAXLEN >> kind
            low_lanes = head_lanes(span)
            lane = lax.broadcasted_iota(jnp.int32, (span, 128), 1)
            for seq in range(1 << kind):
                rows = slice(seq * span, (seq + 1) * span)
                live = lax.broadcasted_iota(jnp.int32, (1, span), 1) < len_ref[b, seq]
                bias = jnp.where(live, 0.0, NEG)
                logs = jnp.zeros((span, 128), F32)
                outs = []
                group = FWD_GROUP[kind]
                for first in range(0, 2 * pairs, group):
                    heads = range(first, first + group)
                    cols = [slice(head // 2 * 2 * HD, (head // 2 + 1) * 2 * HD) for head in heads]
                    qs = [
                        jnp.where(low_lanes if head % 2 == 0 else ~low_lanes, q_ref[rows, at] * BF(0.125), BF(0))
                        for head, at in zip(heads, cols)
                    ]
                    scores = [dot_bt(q, k_ref[rows, at]) + bias for q, at in zip(qs, cols)]
                    peaks = [jnp.max(x, axis=-1, keepdims=True) for x in scores]
                    exps = [jnp.exp(x - m) for x, m in zip(scores, peaks)]
                    totals = [jnp.sum(x, axis=-1, keepdims=True) for x in exps]
                    probs = [(x * (1.0 / z)).astype(BF) for x, z in zip(exps, totals)]
                    outs += [dot(p, v_ref[rows, at]) for p, at in zip(probs, cols)]
                    for head, m, z in zip(heads, peaks, totals):
                        logs = jnp.where(lane == head, m + jnp.log(z), logs)
                for pair in range(pairs):
                    both = jnp.where(low_lanes, outs[2 * pair], outs[2 * pair + 1])
                    c_ref[rows, pair * 2 * HD : (pair + 1) * 2 * HD] = both.astype(BF)
                l_ref[:, rows] = logs.T[:8]


def attn_fwd(lengths, hidden, wq, wk, wv, vec, start, count, prior=None, after=()):
    n, d = hidden.shape
    half = wq.shape[1]
    blocks = n // MAXLEN
    wide = jax.ShapeDtypeStruct((n, half), BF)
    prior = list(prior or ())
    extra = prior + list(after)
    return pl.pallas_call(
        partial(attn_fwd_kernel, start, len(extra)),
        grid=(count,),
        in_specs=[
            SMEM, rows_spec(d, start), full((d, half)), full((d, half)), full((d, half)), full(vec.shape),
            *[ANY] * len(extra),
        ],
        out_specs=[rows_spec(half, start)] * 4 + [pl.BlockSpec((8, MAXLEN), lambda b: (b + start, 0))],
        out_shape=[wide] * 4 + [jax.ShapeDtypeStruct((8 * blocks, MAXLEN), F32)],
        input_output_aliases={6 + i: i for i in range(len(prior))},
        compiler_params=params(),
        cost_estimate=cost(7 * count),
        name="attn_fwd",
    )(lengths, hidden, wq, wk, wv, vec, *extra)


def live_column(len_ref, b):
    pos = lax.broadcasted_iota(jnp.int32, (MAXLEN, 1), 0)
    kind = lax.rem(b, 3)
    shift = 9 - kind
    seg = lax.shift_right_logical(pos, shift)
    off = pos - lax.shift_left(seg, shift)
    picked = jnp.full((MAXLEN, 1), len_ref[b, 0], jnp.int32)
    for slot in range(1, 4):
        picked = jnp.where(seg == slot, len_ref[b, slot], picked)
    return (off < picked).astype(F32)


def norm_stats(x):
    center = x - jnp.mean(x, axis=-1, keepdims=True)
    inverse = lax.rsqrt(jnp.mean(center * center, axis=-1, keepdims=True) + EPSILON)
    return center * inverse, inverse


def accumulate(ref, value, first_step):
    @pl.when(first_step)
    def _():
        ref[...] = value

    @pl.when(jnp.logical_not(first_step))
    def _():
        ref[...] += value


def ff_fwd_kernel(
    len_ref, h_ref, co_ref, cp_ref, cot_ref, wmo_ref, wmp_ref, wio_ref, wip_ref, woo_ref, wop_ref, vec_ref, pvec_ref,
    out_ref, x_ref, low_ref, gs_ref, lo_ref, gpo_ref, gpp_ref, owk_ref, owa_ref, sums_ref, act_ref, pa_ref, pb_ref,
):
    b = pl.program_id(0)
    d = h_ref.shape[1]
    ff = wio_ref.shape[1]
    width = 512
    pa_ref[...] = dot(co_ref[...], wmo_ref[...])
    pb_ref[...] = dot(cp_ref[...], wmp_ref[...])
    mixed = (pa_ref[...] + pb_ref[...]) + vector(vec_ref, V_MB)
    x = h_ref[...].astype(F32) + mixed
    x_ref[...] = x
    n1, _ = norm_stats(x)
    first = n1 * vector(vec_ref, V_FG) + vector(vec_ref, V_FB)
    low = first.astype(BF)
    low_ref[...] = low
    for wi, wo, vec, gp_ref, part_ref, keep in (
        (wio_ref, woo_ref, vec_ref, gpo_ref, pa_ref, True),
        (wip_ref, wop_ref, pvec_ref, gpp_ref, pb_ref, False),
    ):
        part = None
        for c in range(ff // width):
            cols = slice(c * width, (c + 1) * width)
            inner = dot(low, wi[:, cols]) + vec[V_IB : V_IB + 1, cols]
            cdf = 0.5 * (1.0 + lax.erf(inner * INV_SQRT2))
            gp_ref[:, cols] = cdf + inner * (jnp.exp(-0.5 * inner * inner) * INV_SQRT_2PI)
            active = (inner * cdf).astype(BF)
            if keep:
                act_ref[:, cols] = active
            term = dot(active, wo[cols, :])
            part = term if part is None else part + term
        part_ref[...] = part
    r = first + ((pa_ref[...] + pb_ref[...]) + vector(vec_ref, V_OB))
    n2, inv2 = norm_stats(r)
    gain = vector(vec_ref, V_SG)
    out_ref[...] = (n2 * gain + vector(vec_ref, V_SB)).astype(BF)
    g = cot_ref[...].astype(F32) * live_column(len_ref, b)
    scaled = g * gain
    gs = inv2 * (
        scaled - jnp.mean(scaled, axis=-1, keepdims=True) - n2 * jnp.mean(scaled * n2, axis=-1, keepdims=True)
    )
    gs_ref[...] = gs
    lo = gs.astype(BF)
    lo_ref[...] = lo
    sums = jnp.concatenate(
        [
            jnp.sum(gs, axis=0, keepdims=True),
            jnp.sum(g * n2, axis=0, keepdims=True),
            jnp.sum(g, axis=0, keepdims=True),
            jnp.zeros((5, d), F32),
        ],
        axis=0,
    )
    accumulate(sums_ref, sums, b == 0)
    for ref, cols in zip((owk_ref, owa_ref), core_halves(ff // 2)):
        accumulate(ref, dot_at(act_ref[:, cols], lo), b == 0)


def ff_fwd(lengths, hidden, co, cp, cot, wmo, wmp, wio, wip, woo, wop, vec, pvec):
    n, d = hidden.shape
    half = co.shape[1]
    ff = wio.shape[1]
    return pl.pallas_call(
        ff_fwd_kernel,
        grid=(n // MAXLEN,),
        in_specs=[
            SMEM, rows_spec(d), rows_spec(half), rows_spec(half), rows_spec(d), full((half, d)), full((half, d)),
            full((d, ff)), full((d, ff)), full((ff, d)), full((ff, d)), full(vec.shape), full(pvec.shape),
        ],
        out_specs=[
            rows_spec(d), rows_spec(d), rows_spec(d), rows_spec(d), rows_spec(d), rows_spec(ff), rows_spec(ff),
            full((ff // 2, d)), full((ff // 2, d)), full((8, d)),
        ],
        out_shape=[
            jax.ShapeDtypeStruct((n, d), BF),
            jax.ShapeDtypeStruct((n, d), F32),
            jax.ShapeDtypeStruct((n, d), BF),
            jax.ShapeDtypeStruct((n, d), F32),
            jax.ShapeDtypeStruct((n, d), BF),
            jax.ShapeDtypeStruct((n, ff), F32),
            jax.ShapeDtypeStruct((n, ff), F32),
            jax.ShapeDtypeStruct((ff // 2, d), F32),
            jax.ShapeDtypeStruct((ff // 2, d), F32),
            jax.ShapeDtypeStruct((8, d), F32),
        ],
        scratch_shapes=[pltpu.VMEM((MAXLEN, ff), BF), pltpu.VMEM((MAXLEN, d), F32), pltpu.VMEM((MAXLEN, d), F32)],
        compiler_params=params(),
        cost_estimate=cost(58),
        name="ff_fwd",
    )(lengths, hidden, co, cp, cot, wmo, wmp, wio, wip, woo, wop, vec, pvec)


def ff_bwd_half(lo, wi_ref, wo_ref, gp_ref, gi_ref, part_ref):
    width = 512
    part = None
    for c in range(wi_ref.shape[1] // width):
        cols = slice(c * width, (c + 1) * width)
        gi = (dot_bt(lo, wo_ref[cols, :]) * gp_ref[:, cols]).astype(BF)
        if gi_ref is not None:
            gi_ref[:, cols] = gi
        term = dot_bt(gi, wi_ref[:, cols])
        part = term if part is None else part + term
    part_ref[...] = part


def ff_bwd_own_kernel(skip, lo_ref, low_ref, gp_ref, wi_ref, wo_ref, *rest):
    part_ref, iwk_ref, iwa_ref, isum_ref, gi_ref = rest[skip:]
    b = pl.program_id(0)
    ff_bwd_half(lo_ref[...], wi_ref, wo_ref, gp_ref, gi_ref, part_ref)
    gi = gi_ref[...]
    for ref, cols in zip((iwk_ref, iwa_ref), core_halves(low_ref.shape[1] // 2)):
        accumulate(ref, dot_at(low_ref[:, cols], gi), b == 0)
    accumulate(isum_ref, jnp.sum(gi.astype(F32), axis=0, keepdims=True), b == 0)


def ff_bwd_own(lo, low, gp, wi, wo, *after):
    n, d = lo.shape
    ff = wi.shape[1]
    return pl.pallas_call(
        partial(ff_bwd_own_kernel, len(after)),
        grid=(n // MAXLEN,),
        in_specs=[rows_spec(d), rows_spec(d), rows_spec(ff), full((d, ff)), full((ff, d)), *[ANY] * len(after)],
        out_specs=[rows_spec(d), full((d // 2, ff)), full((d // 2, ff)), full((1, ff))],
        out_shape=[
            jax.ShapeDtypeStruct((n, d), F32),
            jax.ShapeDtypeStruct((d // 2, ff), F32),
            jax.ShapeDtypeStruct((d // 2, ff), F32),
            jax.ShapeDtypeStruct((1, ff), F32),
        ],
        scratch_shapes=[pltpu.VMEM((MAXLEN, ff), BF)],
        compiler_params=params(),
        cost_estimate=cost(26),
        name="ff_bwd_own",
    )(lo, low, gp, wi, wo, *after)


def ff_bwd_peer_kernel(
    skip, lo_ref, gs_ref, x_ref, gp_ref, opart_ref, co_ref, wi_ref, wo_ref, vec_ref, *rest
):
    gm_ref, lm_ref, mwg_ref, sums_ref, part_ref = rest[skip:]
    b = pl.program_id(0)
    d = lo_ref.shape[1]
    ff_bwd_half(lo_ref[...], wi_ref, wo_ref, gp_ref, None, part_ref)
    g = gs_ref[...] + (opart_ref[...] + part_ref[...])
    n1, inv1 = norm_stats(x_ref[...])
    scaled = g * vector(vec_ref, V_FG)
    gm = inv1 * (
        scaled - jnp.mean(scaled, axis=-1, keepdims=True) - n1 * jnp.mean(scaled * n1, axis=-1, keepdims=True)
    )
    gm_ref[...] = gm
    lm = gm.astype(BF)
    lm_ref[...] = lm
    sums = jnp.concatenate(
        [
            jnp.sum(gm, axis=0, keepdims=True),
            jnp.sum(g * n1, axis=0, keepdims=True),
            jnp.sum(g, axis=0, keepdims=True),
            jnp.zeros((5, d), F32),
        ],
        axis=0,
    )
    accumulate(sums_ref, sums, b == 0)
    accumulate(mwg_ref, dot_at(co_ref[...], lm), b == 0)


def ff_bwd_peer(lo, gs, x, gp, opart, co, wi, wo, vec, *after):
    n, d = lo.shape
    half = co.shape[1]
    ff = wi.shape[1]
    return pl.pallas_call(
        partial(ff_bwd_peer_kernel, len(after)),
        grid=(n // MAXLEN,),
        in_specs=[
            rows_spec(d), rows_spec(d), rows_spec(d), rows_spec(ff), rows_spec(d), rows_spec(half), full((d, ff)),
            full((ff, d)), full(vec.shape), *[ANY] * len(after),
        ],
        out_specs=[rows_spec(d), rows_spec(d), full((half, d)), full((8, d))],
        out_shape=[
            jax.ShapeDtypeStruct((n, d), F32),
            jax.ShapeDtypeStruct((n, d), BF),
            jax.ShapeDtypeStruct((half, d), F32),
            jax.ShapeDtypeStruct((8, d), F32),
        ],
        scratch_shapes=[pltpu.VMEM((MAXLEN, d), F32)],
        compiler_params=params(),
        cost_estimate=cost(25),
        name="ff_bwd_peer",
    )(lo, gs, x, gp, opart, co, wi, wo, vec, *after)


def attn_bwd_kernel(own, start, skip, len_ref, lm_ref, wm_ref, q_ref, k_ref, v_ref, l_ref, wq_ref, wk_ref, wv_ref, *rest):
    if own:
        given = 3 if start else 5
        h_ref, *given = rest[:given]
        part_ref, wk_out, wa_out, gc_ref, dq_ref, dk_ref, dv_ref = rest[len(given) + 1 + skip :]
    else:
        gm_ref, opart_ref = rest[:2]
        ig_ref, gc_ref, dq_ref, dk_ref, dv_ref, part_ref = rest[2 + skip :]
    half = wq_ref.shape[1]
    pairs = half // (2 * HD)
    b = pl.program_id(0) + start
    gc_ref[...] = dot_bt(lm_ref[...], wm_ref[...]).astype(BF)
    for kind in range(3):

        @pl.when(lax.rem(b, 3) == kind)
        def _():
            span = MAXLEN >> kind
            low_lanes = head_lanes(span)
            for seq in range(1 << kind):
                rows = slice(seq * span, (seq + 1) * span)
                live = lax.broadcasted_iota(jnp.int32, (span, 1), 0) < len_ref[b, seq]
                bias = jnp.where(live, 0.0, NEG)
                dqs, dks, dvs = [], [], []
                group = BWD_GROUP[kind]
                for first in range(0, 2 * pairs, group):
                    heads = range(first, first + group)
                    cols = [slice(head // 2 * 2 * HD, (head // 2 + 1) * 2 * HD) for head in heads]
                    masks = [low_lanes if head % 2 == 0 else ~low_lanes for head in heads]
                    qs = [q_ref[rows, at] * BF(0.125) for at in cols]
                    ups = [gc_ref[rows, at] for at in cols]
                    scores = [
                        dot_bt(k_ref[rows, at], jnp.where(mask, q, BF(0))) + bias for q, at, mask in zip(qs, cols, masks)
                    ]
                    dprobs = [
                        dot_bt(v_ref[rows, at], jnp.where(mask, up, BF(0))) for up, at, mask in zip(ups, cols, masks)
                    ]
                    probs = [jnp.exp(x - l_ref[head : head + 1, rows]) for x, head in zip(scores, heads)]
                    deltas = [jnp.sum(p * dp, axis=0, keepdims=True) for p, dp in zip(probs, dprobs)]
                    dscores = [(p * (dp - delta)).astype(BF) for p, dp, delta in zip(probs, dprobs, deltas)]
                    dvs += [dot(p.astype(BF), up) for p, up in zip(probs, ups)]
                    dks += [dot(ds, q) for ds, q in zip(dscores, qs)]
                    dqs += [dot_at(ds, k_ref[rows, at]) for ds, at in zip(dscores, cols)]
                for pair in range(pairs):
                    at = slice(pair * 2 * HD, (pair + 1) * 2 * HD)
                    dv_ref[rows, at] = jnp.where(low_lanes, dvs[2 * pair], dvs[2 * pair + 1]).astype(BF)
                    dk_ref[rows, at] = jnp.where(low_lanes, dks[2 * pair], dks[2 * pair + 1]).astype(BF)
                    dq = jnp.where(low_lanes, dqs[2 * pair], dqs[2 * pair + 1]) * 0.125
                    dq_ref[rows, at] = dq.astype(BF)

    dq, dk, dv = dq_ref[...], dk_ref[...], dv_ref[...]
    part = (dot_bt(dq, wq_ref[...]) + dot_bt(dk, wk_ref[...])) + dot_bt(dv, wv_ref[...])
    part_ref[...] = part
    if own:
        d = h_ref.shape[1]
        sums = jnp.concatenate(
            [jnp.sum(dq.astype(F32), axis=0, keepdims=True), jnp.sum(dv.astype(F32), axis=0, keepdims=True)], axis=1
        )
        first_step = b == start
        core = lax.axis_index("dp") & 1
        for side, (out, cols) in enumerate(zip((wk_out, wa_out), core_halves(half))):
            holds = (core == side).astype(F32)

            @pl.when(first_step)
            def _(side=side, out=out, cols=cols, holds=holds):
                if start:
                    out[...] = given[side][...]
                    return
                mwg_ref, fsum_ref, isum_ref, osum_ref = given
                pad = jnp.zeros((1, d), F32)
                top = jnp.concatenate([pad, fsum_ref[0:1, :]], axis=1)
                mid = jnp.concatenate([fsum_ref[1:2, :], fsum_ref[2:3, :]], axis=1)
                low = jnp.concatenate([osum_ref[0:1, :], osum_ref[1:2, :]], axis=1)
                end = jnp.concatenate([osum_ref[2:3, :], pad], axis=1)
                vectors = jnp.concatenate([top, mid, isum_ref[...], low, end, jnp.zeros((3, 2 * d), F32)], axis=0)
                out[:half, : 3 * half] = jnp.zeros((half, 3 * half), F32)
                out[:half, 3 * half :] = mwg_ref[:, cols]
                out[half : half + 8, :] = vectors * holds
                out[half + 8 :, :] = jnp.zeros((PAD - 8, 2 * d), F32)

            h = h_ref[:, cols]
            for i, grad in enumerate((dq, dk, dv)):
                out[:half, i * half : (i + 1) * half] += dot_at(h, grad)
            out[half : half + 1, :d] += sums * holds
    else:
        ig_ref[...] = (gm_ref[...] + (opart_ref[...] + part_ref[...])).astype(BF)


def attn_bwd(own, start, count, lengths, lm, wm, q, k, v, logs, wq, wk, wv, extra, prior=None, after=()):
    n, d = lm.shape
    half = wq.shape[1]
    after = ([] if prior is None else [prior]) + list(after)
    if own:
        extra_specs = [rows_spec(d, start)] + [full(x.shape) for x in extra[1:]]
        out_specs = [rows_spec(d, start)] + [full((half + PAD, 4 * half))] * 2
        out_shape = [jax.ShapeDtypeStruct((n, d), F32)] + [jax.ShapeDtypeStruct((half + PAD, 4 * half), F32)] * 2
    else:
        extra_specs = [rows_spec(d, start)] * 2
        out_specs = [rows_spec(d, start)]
        out_shape = [jax.ShapeDtypeStruct((n, d), BF)]
    return pl.pallas_call(
        partial(attn_bwd_kernel, own, start, len(after)),
        grid=(count,),
        in_specs=[
            SMEM, rows_spec(d, start), full((half, d)), rows_spec(half, start), rows_spec(half, start),
            rows_spec(half, start), pl.BlockSpec((8, MAXLEN), lambda b: (b + start, 0)), full((d, half)),
            full((d, half)), full((d, half)), *extra_specs, *[ANY] * len(after),
        ],
        out_specs=out_specs,
        out_shape=out_shape,
        input_output_aliases={} if prior is None else {10 + len(extra): 0},
        scratch_shapes=[pltpu.VMEM((MAXLEN, half), BF)] * 4 + ([] if own else [pltpu.VMEM((MAXLEN, d), F32)]),
        compiler_params=params(),
        cost_estimate=cost(12 * count if own else 40),
        name="attn_bwd_own" if own else "attn_bwd_peer",
    )(lengths, lm, wm, q, k, v, logs, wq, wk, wv, *extra, *after)


CORE, NEAR, FAR = 1, 2, 4
TENSOR_SWAP = [(0, 1), (1, 0)]


def bit_of(mask):
    return (lax.axis_index("dp") & mask) != 0


def swap(x, mask, n_dp):
    return lax.ppermute(x, "dp", [(i, i ^ mask) for i in range(n_dp)])


def in_order(mask, mine, other):
    return jnp.where(bit_of(mask), jnp.concatenate([other, mine]), jnp.concatenate([mine, other]))


def away(x, mask):
    rows = x.shape[0] // 2
    return lax.dynamic_slice_in_dim(x, jnp.where(bit_of(mask), 0, rows), rows, 0)


def kept(x, mask):
    rows = x.shape[0] // 2
    return lax.dynamic_slice_in_dim(x, jnp.where(bit_of(mask), rows, 0), rows, 0)


def exchange(x, mask, n_dp):
    return swap(x, mask, n_dp) if mask < n_dp else jnp.zeros_like(x)


def join_kernel(mine_ref, other_ref, out_ref):
    rows = mine_ref.shape[0]
    core = lax.axis_index("dp") & 1
    out_ref[pl.ds(pl.multiple_of(core * rows, 8), rows), :] = mine_ref[...]
    out_ref[pl.ds(pl.multiple_of((1 - core) * rows, 8), rows), :] = other_ref[...]


def join(mine, other):
    return pl.pallas_call(
        join_kernel,
        out_shape=jax.ShapeDtypeStruct((2 * mine.shape[0], mine.shape[1]), mine.dtype),
        compiler_params=params(),
        cost_estimate=cost(0.1),
        name="join",
    )(mine, other)


def beyond(x, n_dp):
    mask = 4 * FAR
    while mask < n_dp:
        x = x + swap(x, mask, n_dp)
        mask *= 2
    return x


def piece(arrays, masks, base, rows):
    index = jnp.int32(0)
    for mask in masks:
        index = index * 2 + bit_of(mask).astype(jnp.int32)
    cut = [lax.dynamic_slice_in_dim(a, base + index * rows, rows, 0) for a in arrays]
    return jnp.concatenate(cut, axis=1).astype(F32)


def tie(*arrays):
    return lax.optimization_barrier(arrays)


def prepare_kernel(*refs):
    weights, vectors, (vec_ref, out_ref) = refs[:4], refs[4:-2], refs[-2:]
    d = vec_ref.shape[1] // 2
    qb, vb, mb, fg, fb, ib, ob, sg, sb = [ref[...].astype(F32).reshape(1, -1) for ref in vectors]
    zero = jnp.zeros((1, d), F32)
    rows = [(qb, vb, mb), (fg, fb), (ib,), (ob, sg), (sb, zero)]
    vec = jnp.concatenate(
        [jnp.concatenate(row, axis=1) for row in rows] + [jnp.zeros((3, 2 * d), F32)], axis=0
    )
    vec_ref[...] = vec
    me = lax.axis_index("dp")
    core, near, far = me & 1, (me >> 1) & 1, (me >> 2) & 1
    half = d // 2
    rows = d // 16
    for base, index in ((0, core * 4 + far * 2 + near), (8 * rows, core * 4 + near * 2 + far)):
        at = pl.ds(pl.multiple_of(base + index * rows, 16), rows)
        to = slice(base // 8, base // 8 + rows)
        for i in range(3):
            out_ref[to, i * half : (i + 1) * half] = weights[i][at, :].astype(F32)
        at = pl.ds(pl.multiple_of(index * rows, 16), rows)
        cols = slice(0, half) if base == 0 else slice(half, d)
        out_ref[to, 3 * half :] = weights[3][at, cols].astype(F32)
    out_ref[2 * rows :, :] = vec


def prepare(weights, vectors):
    d = weights[0].shape[0]
    return pl.pallas_call(
        prepare_kernel,
        out_shape=[jax.ShapeDtypeStruct((8, 2 * d), F32), jax.ShapeDtypeStruct((d // 8 + 8, 2 * d), F32)],
        compiler_params=params(),
        cost_estimate=cost(2),
        name="prepare",
    )(*weights, *vectors)


def finish_kernel(a_ref, ra_ref, b_ref, rb_ref, q_ref, k_ref, v_ref, m_ref, *vectors):
    half = m_ref.shape[0]
    d = 2 * half
    mine, other = core_halves(half)
    core = lax.axis_index("dp") & 1
    for cols, x_ref, y_ref in ((mine, a_ref, b_ref), (other, ra_ref, rb_ref)):
        q_ref[cols, :] = x_ref[:half, :half]
        k_ref[cols, :] = x_ref[:half, half:]
        v_ref[cols, :] = y_ref[:half, :half]
        m_ref[:, cols] = y_ref[:half, half:]
    pad = slice(half, half + 8)
    left = jnp.where(core == 0, a_ref[pad, :], ra_ref[pad, :])
    right = jnp.where(core == 0, b_ref[pad, :], rb_ref[pad, :])
    rows = (
        left[0:1, :half], left[0:1, half:], right[0:1], left[1:2], right[1:2],
        jnp.concatenate([left[2:3], right[2:3]], axis=1), left[3:4], right[3:4], left[4:5],
    )
    for ref, row in zip(vectors, rows):
        ref[...] = row.reshape(-1)


def finish(a, ra, b, rb):
    d = a.shape[1]
    half = d // 2
    return pl.pallas_call(
        finish_kernel,
        out_shape=[jax.ShapeDtypeStruct((d, half), F32)] * 3
        + [jax.ShapeDtypeStruct((half, d), F32)]
        + [jax.ShapeDtypeStruct((size,), F32) for size in (half, half, d, d, d, 2 * d, d, d, d)],
        compiler_params=params(),
        cost_estimate=cost(0.1),
        name="finish",
    )(a, ra, b, rb)


def assemble_kernel(square, a_ref, ra_ref, b_ref, rb_ref, *outs):
    rows = a_ref.shape[0]
    odd = lax.axis_index("dp") & CORE
    for base, mine, other in ((0, a_ref, ra_ref), (2 * rows, b_ref, rb_ref)):
        for ref, side in ((mine, odd), (other, 1 - odd)):
            at = pl.ds(pl.multiple_of(base + side * rows, 16), rows)
            if not square:
                outs[0][at, :] = ref[...].astype(BF)
                continue
            half = ref.shape[1] // 4
            for i in range(3):
                outs[i][at, :] = ref[:, i * half : (i + 1) * half].astype(BF)
            at = pl.ds(pl.multiple_of(side * rows, 16), rows)
            left = base == 0
            cols = slice(0, half) if left else slice(half, 2 * half)
            outs[3][at, cols] = ref[:, 3 * half :].astype(BF)


def assemble(square, a, ra, b, rb):
    rows, cols = 4 * a.shape[0], a.shape[1]
    half = cols // 4
    if square:
        shapes = [(rows, half)] * 3 + [(rows // 2, 2 * half)]
    else:
        shapes = [(rows, cols)]
    return pl.pallas_call(
        partial(assemble_kernel, square),
        out_shape=[jax.ShapeDtypeStruct(shape, BF) for shape in shapes],
        compiler_params=params(),
        cost_estimate=cost(4),
        name="assemble",
    )(a, ra, b, rb)


def local(
    n_dp, hidden_in, query_weight, key_weight, value_weight, query_bias, value_bias, mixer_weight, mixer_bias,
    first_gain, first_bias, inner_weight, inner_bias, outer_weight, outer_bias, second_gain, second_bias, lengths,
    cotangent,
):
    n, d = hidden_in.shape
    half = query_weight.shape[1]
    ff = inner_weight.shape[1]
    vec, h_out = prepare(
        (query_weight, key_weight, value_weight, mixer_weight),
        (
            query_bias, value_bias, mixer_bias, first_gain, first_bias, inner_bias, outer_bias, second_gain,
            second_bias,
        ),
    )
    sixteenth = d // 16
    i_out = jnp.concatenate(
        [
            piece([inner_weight], (CORE, FAR, NEAR), 0, sixteenth),
            piece([inner_weight], (CORE, NEAR, FAR), d // 2, sixteenth),
        ]
    )
    eighth = ff // 8
    o_out = jnp.concatenate(
        [piece([outer_weight], (CORE, NEAR), 0, eighth), piece([outer_weight], (CORE, FAR), ff // 2, eighth)]
    )
    h0 = lax.ppermute(h_out, "tensor", TENSOR_SWAP)
    own = list(attn_fwd(lengths, hidden_in, query_weight, key_weight, value_weight, vec, 0, 2))
    h0, i_out, own[0] = tie(h0, i_out, own[0])
    i0 = lax.ppermute(i_out, "tensor", TENSOR_SWAP)
    ha, hb, pvec = h0[:sixteenth], h0[sixteenth : 2 * sixteenth], h0[2 * sixteenth :]
    hra, hrb = swap(ha, NEAR, n_dp), swap(hb, FAR, n_dp)
    qo, ko, vo, co, lgo = attn_fwd(
        lengths, hidden_in, query_weight, key_weight, value_weight, vec, 2, 2, own, (ha, hb)
    )
    hra, hrb, i0, co, o_out = tie(hra, hrb, i0, co, o_out)
    ha, hb = in_order(NEAR, ha, hra), in_order(FAR, hb, hrb)
    hra, hrb = swap(ha, FAR, n_dp), swap(hb, NEAR, n_dp)
    o0 = lax.ppermute(o_out, "tensor", TENSOR_SWAP)
    ia, ib = i0[:sixteenth], i0[sixteenth:]
    ira, irb = swap(ia, NEAR, n_dp), swap(ib, FAR, n_dp)
    ha, hb = in_order(FAR, ha, hra), in_order(NEAR, hb, hrb)
    hra, hrb = swap(ha, CORE, n_dp), swap(hb, CORE, n_dp)
    ha, hb, ira, irb = tie(ha, hb, ira, irb)
    ia, ib = in_order(NEAR, ia, ira), in_order(FAR, ib, irb)
    ira, irb = swap(ia, FAR, n_dp), swap(ib, NEAR, n_dp)
    wqp, wkp, wvp, wmp = assemble(True, ha, hra, hb, hrb)
    peer = list(attn_fwd(lengths, hidden_in, wqp, wkp, wvp, pvec, 0, 2, None, (ia, ib)))
    ira, irb, o0, peer[0] = tie(ira, irb, o0, peer[0])
    ia, ib = in_order(FAR, ia, ira), in_order(NEAR, ib, irb)
    ira, irb = swap(ia, CORE, n_dp), swap(ib, CORE, n_dp)
    oa, ob = o0[:eighth], o0[eighth:]
    ora, orb = swap(oa, NEAR, n_dp), swap(ob, FAR, n_dp)
    qp, kp, vp, cp, lgp = attn_fwd(lengths, hidden_in, wqp, wkp, wvp, pvec, 2, 2, peer, (ia, ib, oa, ob))
    ora, orb, cp = tie(ora, orb, cp)
    oa, ob = in_order(NEAR, oa, ora), in_order(FAR, ob, orb)
    ora, orb = swap(oa, CORE, n_dp), swap(ob, CORE, n_dp)
    (wip,) = assemble(False, ia, ira, ib, irb)
    (wop,) = assemble(False, oa, ora, ob, orb)
    layer_out, x, low, gs, lo, gpo, gpp, owk, owa, osums = ff_fwd(
        lengths, hidden_in, co, cp, cotangent, mixer_weight, wmp, inner_weight, wip, outer_weight, wop, vec, pvec
    )
    o, lo = tie(swap(owa, CORE, n_dp), lo)
    o1 = owk + o
    o_out = away(o1, NEAR)
    o = swap(o_out, NEAR, n_dp)
    opart, iwk, iwa, ibg = ff_bwd_own(lo, low, gpo, inner_weight, outer_weight, o_out)
    o, opart, iwa = tie(o, opart, iwa)
    i, opart = tie(swap(iwa, CORE, n_dp), opart)
    i1 = iwk + i
    i_out = away(i1, NEAR)
    i = swap(i_out, NEAR, n_dp)
    o2 = kept(o1, NEAR) + o
    o_out = away(o2, FAR)
    o = swap(o_out, FAR, n_dp)
    gm, lm, mwg, isums = ff_bwd_peer(lo, gs, x, gpp, opart, co, wip, wop, vec, o_out, i_out)
    o, i, lm = tie(o, i, lm)
    i2 = kept(i1, NEAR) + i
    i_out = away(i2, FAR)
    i = swap(i_out, FAR, n_dp)
    o3 = kept(o2, FAR) + o
    o3, i_out = tie(o3, i_out)
    o = exchange(o3, 2 * FAR, n_dp)
    own = (lengths, lm, mixer_weight, qo, ko, vo, lgo, query_weight, key_weight, value_weight)
    part, hk, ha = attn_bwd(True, 0, 2, *own, (hidden_in, mwg, isums, ibg, osums), None, (o3, i_out))
    o, i, part = tie(o, i, part)
    o = beyond(o3 + o, n_dp)
    o_ = swap(o, FAR, n_dp)
    i3 = kept(i2, FAR) + i
    i3, o = tie(i3, o)
    i = exchange(i3, 2 * FAR, n_dp)
    part, hk, ha = attn_bwd(True, 2, 2, *own, (hidden_in, hk, ha), part, (o, i3))
    h = swap(ha, CORE, n_dp)
    o_, ha = tie(o_, ha)
    o = in_order(FAR, o, o_)
    cut = o.shape[0] // 2
    oa_, ob = swap(o[:cut], NEAR, n_dp), o[cut:]
    peer = (lengths, lm, wmp, qp, kp, vp, lgp, wqp, wkp, wvp)
    (ig,) = attn_bwd(False, 0, 1, *peer, (gm, part), None, (o,))
    h, i, ig = tie(h, i, ig)
    h1 = hk + h
    ha, hb = h1[:, :d], h1[:, d:]
    ha_out, hb_out = away(ha, NEAR), away(hb, FAR)
    hra, hrb = swap(ha_out, NEAR, n_dp), swap(hb_out, FAR, n_dp)
    i = beyond(i3 + i, n_dp)
    i, hb_out = tie(i, hb_out)
    i_ = swap(i, FAR, n_dp)
    (ig,) = attn_bwd(False, 1, 1, *peer, (gm, part), ig, (ha_out, hb_out, i))
    hra, hrb, ob, ig = tie(hra, hrb, ob, ig)
    ha, hb = kept(ha, NEAR) + hra, kept(hb, FAR) + hrb
    ha_out, hb_out = away(ha, FAR), away(hb, NEAR)
    hra, hrb = swap(ha_out, FAR, n_dp), swap(hb_out, NEAR, n_dp)
    ob, hb_out = tie(ob, hb_out)
    ob_ = swap(ob, NEAR, n_dp)
    (ig,) = attn_bwd(False, 2, 1, *peer, (gm, part), ig, (ha_out, hb_out, ob))
    hra, hrb, i_, ig = tie(hra, hrb, i_, ig)
    h = jnp.concatenate([kept(ha, FAR) + hra, kept(hb, NEAR) + hrb])
    h_ = exchange(h, 2 * FAR, n_dp)
    i = in_order(FAR, i, i_)
    i_ = swap(i, NEAR, n_dp)
    (input_grad,) = attn_bwd(False, 3, 1, *peer, (gm, part), ig, (h, i))
    h_, input_grad = tie(h_, input_grad)
    h = beyond(h + h_, n_dp)
    rows = h.shape[0] // 2
    ha, hb = h[:rows], h[rows:]
    hra, hrb = swap(ha, FAR, n_dp), swap(hb, NEAR, n_dp)
    hra, hrb, i_, oa_, ob_ = tie(hra, hrb, i_, oa_, ob_)
    ha, hb = in_order(FAR, ha, hra), in_order(NEAR, hb, hrb)
    hra, hrb = swap(ha, NEAR, n_dp), swap(hb, FAR, n_dp)
    i = in_order(NEAR, i, i_)
    i_ = swap(i, CORE, n_dp)
    o = in_order(NEAR, o, jnp.concatenate([oa_, ob_]))
    o_ = swap(o, CORE, n_dp)
    owg = join(o, o_)
    hra, hrb, owg, i_ = tie(hra, hrb, owg, i_)
    ha, hb = in_order(NEAR, ha, hra), in_order(FAR, hb, hrb)
    hra, hrb = swap(ha, CORE, n_dp), swap(hb, CORE, n_dp)
    iwg = join(i, i_)
    hra, hrb, iwg = tie(hra, hrb, iwg)
    qwg, kwg, vwg, mwg, *vectors = finish(ha, hra, hb, hrb)
    qb, vb, mb, fg, fb, ib, ob, sg, sb = vectors
    return (
        layer_out, input_grad, qwg, kwg, vwg, qb, vb, mwg, mb, fg, fb, iwg, ib, owg, ob, sg, sb,
    )


def solution(mesh):
    col, row, rep = P(None, "tensor"), P("tensor", None), P()
    vec, tok = P("tensor"), P("dp", None)
    return jax.shard_map(
        partial(local, mesh.shape["dp"]),
        mesh=mesh,
        in_specs=(tok, col, col, col, vec, vec, row, rep, rep, rep, col, vec, row, rep, rep, rep, tok, tok),
        out_specs=(tok, tok, col, col, col, vec, vec, row, rep, rep, rep, col, vec, row, rep, rep, rep),
        check_vma=False,
    )
```

time: 507 us -> 437 us (0.86)
  waiting for transfers between devices: 114 us -> 89 us
  other arithmetic: 42.4 us -> 19.9 us
  local copies, waits for them, and re-layouts: 37.4 us -> 16.3 us
    ppermute x42 -> x43, waiting for transfers between devices: 106 us -> 84.6 us  [swap(): return lax.ppermute(x, 'dp', [(i, i ^ mask) for i in range(n_dp)])]
    pallas_call x1 -> x5, Pallas kernels: 25.7 us -> 44 us  [the longest x1 26.3 us: ff_bwd_own(): pl.pallas_call(partial(ff_bwd_own_kernel, len(after)), grid=(n // MAXLEN,...]
    dynamic_slice x11 -> x8, local copies, waits for them, and re-layouts: 14.2 us -> 0.44 us  [away(): lax.dynamic_slice_in_dim(x, jnp.where(bit_of(mask), 0, rows), rows, 0)]
    pallas_call x4, Pallas kernels: 54.9 us -> 42.2 us  [attn_fwd(): pl.pallas_call(partial(attn_fwd_kernel, start, len(extra)), grid=(count,)...]
    select_n x22 -> x18, other arithmetic: 20.3 us -> 10.8 us  [in_order(): jnp.where(bit_of(mask), jnp.concatenate([other, mine]), jnp.concatenate([...]
    pallas_call x4 -> x6, Pallas kernels: 88.2 us -> 82.9 us  [attn_bwd(): pl.pallas_call(partial(attn_bwd_kernel, own, start, len(after)), grid=(co...]
    unnamed x93 -> x96, local copies, waits for them, and re-layouts: 13.1 us -> 11.8 us
    ppermute x42 -> x43, starting transfers between devices: 33.5 us -> 33.2 us  [swap(): return lax.ppermute(x, 'dp', [(i, i ^ mask) for i in range(n_dp)])]
  transfers between devices with their start and end apart: 46 -> 46, of which waited for: 15 -> 23; matrix products, arithmetic and copies ran while one was open for 9% -> 3% of each run, Pallas kernels for 40% -> 45%
where the time goes in v3:
time: 437 us; the launch traced here: 431 us
  Pallas kernels  265 us (61%)
  waiting for transfers between devices  89 us (20%)
  starting transfers between devices  39.2 us (9%)
  other arithmetic  19.9 us (5%)
  local copies, waits for them, and re-layouts  16.3 us (4%)
    ppermute x43, waiting for transfers between devices, swap(): return lax.ppermute(x, 'dp', [(i, i ^ mask) for i in range(n_dp)])  84.6 us
    pallas_call x6, Pallas kernels, attn_bwd(): pl.pallas_call(partial(attn_bwd_kernel, own, start, len(after)), grid=(co...  82.9 us
    pallas_call x1, Pallas kernels, ff_fwd(): pl.pallas_call(ff_fwd_kernel, grid=(n // MAXLEN,), in_specs=[SMEM, rows_s...  58.7 us
    pallas_call x4, Pallas kernels, attn_fwd(): pl.pallas_call(partial(attn_fwd_kernel, start, len(extra)), grid=(count,)...  42.2 us
    ppermute x43, starting transfers between devices, swap(): return lax.ppermute(x, 'dp', [(i, i ^ mask) for i in range(n_dp)])  33.2 us
    pallas_call x1, Pallas kernels, ff_bwd_own(): pl.pallas_call(partial(ff_bwd_own_kernel, len(after)), grid=(n // MAXLEN,...  26.3 us
    pallas_call x1, Pallas kernels, ff_bwd_peer(): pl.pallas_call(partial(ff_bwd_peer_kernel, len(after)), grid=(n // MAXLEN...  25 us
    pallas_call x3, Pallas kernels, assemble(): pl.pallas_call(partial(assemble_kernel, square), out_shape=[jax.ShapeDtyp...  11.8 us
  transfers between devices with their start and end apart: 46, of which 23 were waited for; matrix products, arithmetic and copies ran while one was open for 3% of the time, Pallas kernels for 45%

profile of v3, /device:TPU:0, one launch (start us, length us, event | category | flops | bytes accessed | tf_op | source)
XLA Modules:
  0.0 430.8 jit_solution(8474100635121067145)
XLA Ops:
  6.2 10.2 %attn_fwd.4 = (bf16[2048,384]{1,0:T(8,128)(2,1)}, bf16[2048,384]{1,0:T(8,128)(2,1)}, bf16[2048,384]{1,0:T(8,128)(2,1)}, bf16[2048,384]{1,0:T(8,128)(2,1)}, f32[32,512]{1,0:T(8,128)}) custom-call(s32[4,4]{1,0:T(4,128)} %len_ref.21, bf16[2048,768]{1,0:T(8,128)(2,1)} %rest_0_.3, bf16[768,384]{1,0:T(8,128)(2,1)} %wq_ref.7, bf16[768,384]{1,0:T(8,128)(2,1)} %wk_ref.7, ...), custom_call_target="tpu_custom_call" | custom-call | flops 14000000000 | bytes 1000000 | tf_op jit(solution)/shard_map/attn_fwd/pallas_call | solution.py:125
  25.7 10.7 %attn_fwd.5 = (bf16[2048,384]{1,0:T(8,128)(2,1)}, bf16[2048,384]{1,0:T(8,128)(2,1)}, bf16[2048,384]{1,0:T(8,128)(2,1)}, bf16[2048,384]{1,0:T(8,128)(2,1)}, f32[32,512]{1,0:T(8,128)}) custom-call(s32[4,4]{1,0:T(4,128)} %len_ref.21, bf16[2048,768]{1,0:T(8,128)(2,1)} %rest_0_.3, ...), custom_call_target="tpu_custom_call", output_to_operand_aliasing={{0}: (6, {}), {1}: (7, {}), {2}: (8, {}), {3}: (9, {}), {4}... | custom-call | flops 14000000000 | bytes 1000000 | tf_op jit(solution)/shard_map/attn_fwd/pallas_call | solution.py:125
  40.2 11.5 %collective-permute-done.5 = f32[96,1536]{1,0:T(8,128)S(1)} collective-permute-done((f32[96,1536]{1,0:T(8,128)S(1)}, f32[96,1536]{1,0:T(8,128)S(1)}, u32[]{:S(2)}, u32[]{:S(2)}) %collective-permute-start.5) | collective-permute-done | bytes 589856 | tf_op jit(solution)/shard_map/ppermute | solution.py:486
  56.5 5.3 %collective-permute-done.6 = f32[48,1536]{1,0:T(8,128)S(1)} collective-permute-done((f32[48,1536]{1,0:T(8,128)S(1)}, f32[48,1536]{1,0:T(8,128)S(1)}, u32[]{:S(2)}, u32[]{:S(2)}) %collective-permute-start.6) | collective-permute-done | bytes 294944 | tf_op jit(solution)/shard_map/ppermute | solution.py:486
  71.4 10.5 %attn_fwd.6 = (bf16[2048,384]{1,0:T(8,128)(2,1)}, bf16[2048,384]{1,0:T(8,128)(2,1)}, bf16[2048,384]{1,0:T(8,128)(2,1)}, bf16[2048,384]{1,0:T(8,128)(2,1)}, f32[32,512]{1,0:T(8,128)}) custom-call(s32[4,4]{1,0:T(4,128)} %len_ref.21, bf16[2048,768]{1,0:T(8,128)(2,1)} %rest_0_.3, bf16[768,384]{1,0:T(8,128)(2,1)} %get-tuple-element.166.wq_ref, ...), custom_call_target="tpu_custom_call" | custom-call | flops 14000000000 | bytes 1000000 | tf_op jit(solution)/shard_map/attn_fwd/pallas_call | solution.py:125
  87.1 10.8 %attn_fwd.7 = (bf16[2048,384]{1,0:T(8,128)(2,1)}, bf16[2048,384]{1,0:T(8,128)(2,1)}, bf16[2048,384]{1,0:T(8,128)(2,1)}, bf16[2048,384]{1,0:T(8,128)(2,1)}, f32[32,512]{1,0:T(8,128)}) custom-call(s32[4,4]{1,0:T(4,128)} %len_ref.21, bf16[2048,768]{1,0:T(8,128)(2,1)} %rest_0_.3, ...), custom_call_target="tpu_custom_call", output_to_operand_aliasing={{0}: (6, {}), {1}: (7, {}), {2}: (8, {}), {3}: (9, {}), {4}... | custom-call | flops 14000000000 | bytes 1000000 | tf_op jit(solution)/shard_map/attn_fwd/pallas_call | solution.py:125
  112.7 58.7 %ff_fwd.1 = (bf16[2048,768]{1,0:T(8,128)(2,1)}, f32[2048,768]{1,0:T(8,128)}, bf16[2048,768]{1,0:T(8,128)(2,1)}, f32[2048,768]{1,0:T(8,128)}, bf16[2048,768]{1,0:...) custom-call(s32[4,4]{1,0:T(4,128)} %len_ref.21, ...), custom_call_target="tpu_custom_call" | custom-call | flops 57999998976 | bytes 1000000 | tf_op jit(solution)/shard_map/ff_fwd/pallas_call | solution.py:232
  171.5 4.6 %collective-permute-done.19 = f32[768,768]{1,0:T(8,128)S(1)} collective-permute-done((f32[768,768]{1,0:T(8,128)}, f32[768,768]{1,0:T(8,128)S(1)}, u32[]{:S(2)}, u32[]{:S(2)}) %collective-permute-start.19) | collective-permute-done | bytes 2359328 | tf_op jit(solution)/shard_map/ppermute | solution.py:486
  181.5 26.3 %ff_bwd_own.1 = (f32[2048,768]{1,0:T(8,128)}, f32[384,1536]{1,0:T(8,128)}, f32[384,1536]{1,0:T(8,128)}, f32[1,1536]{1,0:T(1,128)}) custom-call(bf16[2048,768]{1,0:T(8,128)(2,1)} %get-tuple-element.188.lo_ref, bf16[2048,768]{1,0:T(8,128)(2,1)} %get-tuple-element.189.low_ref, f32[2048,1536]{1,0:T(8,128)} %get-tuple-element.190.gp_ref, ...), custom_call_target="tpu_custom_call" | custom-call | flops 25999998976 | bytes 1000000 | tf_op jit(solution)/shard_map/ff_bwd_own/pallas_call | solution.py:288
  216.6 25.0 %ff_bwd_peer.1 = (f32[2048,768]{1,0:T(8,128)}, bf16[2048,768]{1,0:T(8,128)(2,1)}, f32[384,768]{1,0:T(8,128)}, f32[8,768]{1,0:T(8,128)}) custom-call(bf16[2048,768]{1,0:T(8,128)(2,1)} %get-tuple-element.188.lo_ref, f32[2048,768]{1,0:T(8,128)} %get-tuple-element.198.gs_ref, f32[2048,768]{1,0:T(8,128)} %get-tuple-element.199.x_ref, ...), custom_call_target="tpu_custom_call" | custom-call | flops 24999999488 | bytes 1000000 | tf_op jit(solution)/shard_map/ff_bwd_peer/pallas_call | solution.py:339
  247.5 22.3 %attn_bwd_own.2 = (f32[2048,768]{1,0:T(8,128)}, f32[416,1536]{1,0:T(8,128)}, f32[416,1536]{1,0:T(8,128)}) custom-call(s32[4,4]{1,0:T(4,128)} %len_ref.21, bf16[2048,768]{1,0:T(8,128)(2,1)} %get-tuple-element.203.lm_ref, bf16[384,768]{1,0:T(8,128)(2,1)} %wm_ref.3, bf16[2048,384]{1,0:T(8,128)(2,1)} %get-tuple-element.204.q_ref, ...), custom_call_target="tpu_custom_call" | custom-call | flops 24000000000 | bytes 1000000 | tf_op jit(solution)/shard_map/attn_bwd_own/pallas_call | solution.py:459
  277.9 22.4 %attn_bwd_own.3 = (f32[2048,768]{1,0:T(8,128)}, f32[416,1536]{1,0:T(8,128)}, f32[416,1536]{1,0:T(8,128)}) custom-call(s32[4,4]{1,0:T(4,128)} %len_ref.21, bf16[2048,768]{1,0:T(8,128)(2,1)} %get-tuple-element.203.lm_ref, bf16[384,768]{1,0:T(8,128)(2,1)} %wm_ref.3, bf16[2048,384]{1,0:T(8,128)(2,1)} %get-tuple-element.204.q_ref, ...), custom_call_target="tpu_custom_call", output_to_operand_aliasing={{0}: (13, {})} | custom-call | flops 24000000000 | bytes 1000000 | tf_op jit(solution)/shard_map/attn_bwd_own/pallas_call | solution.py:459
  304.5 10.6 %attn_bwd_peer.4.rest_2_ = bf16[2048,768]{1,0:T(8,128)(2,1)} custom-call(s32[4,4]{1,0:T(4,128)} %len_ref.21, bf16[2048,768]{1,0:T(8,128)(2,1)} %get-tuple-element.203.lm_ref, bf16[384,768]{1,0:T(8,128)(2,1)} %get-tuple-element.180.wmp_ref.wm_ref, bf16[2048,384]{1,0:T(8,128)(2,1)} %get-tuple-element.226.q_ref, bf16[2048,384]{1,0:T(8,128)(2,1)} %get-tuple-element.227.k_ref, ...), custom_call_target="tpu_custom_call" | custom-call | flops 40000000000 | bytes 1000000 | tf_op jit(solution)/shard_map/attn_bwd_peer/pallas_call | solution.py:459
  319.6 8.5 %attn_bwd_peer.5.rest_2_ = bf16[2048,768]{1,0:T(8,128)(2,1)} custom-call(s32[4,4]{1,0:T(4,128)} %len_ref.21, bf16[2048,768]{1,0:T(8,128)(2,1)} %get-tuple-element.203.lm_ref, bf16[384,768]{1,0:T(8,128)(2,1)} %get-tuple-element.180.wmp_ref.wm_ref, bf16[2048,384]{1,0:T(8,128)(2,1)} %get-tuple-element.226.q_ref, ...), custom_call_target="tpu_custom_call", output_to_operand_aliasing={{}: (12, {})} | custom-call | flops 40000000000 | bytes 1000000 | tf_op jit(solution)/shard_map/attn_bwd_peer/pallas_call | solution.py:459
  328.1 6.2 %collective-permute-done.30 = f32[208,768]{1,0:T(8,128)S(1)} collective-permute-done((f32[208,768]{1,0:T(8,128)S(1)}, f32[208,768]{1,0:T(8,128)S(1)}, u32[]{:S(2)}, u32[]{:S(2)}) %collective-permute-start.30) | collective-permute-done | bytes 639008 | tf_op jit(solution)/shard_map/ppermute | solution.py:486
  337.9 8.6 %attn_bwd_peer.6.rest_2_ = bf16[2048,768]{1,0:T(8,128)(2,1)} custom-call(s32[4,4]{1,0:T(4,128)} %len_ref.21, bf16[2048,768]{1,0:T(8,128)(2,1)} %get-tuple-element.203.lm_ref, bf16[384,768]{1,0:T(8,128)(2,1)} %get-tuple-element.180.wmp_ref.wm_ref, bf16[2048,384]{1,0:T(8,128)(2,1)} %get-tuple-element.226.q_ref, ...), custom_call_target="tpu_custom_call", output_to_operand_aliasing={{}: (12, {})} | custom-call | flops 40000000000 | bytes 1000000 | tf_op jit(solution)/shard_map/attn_bwd_peer/pallas_call | solution.py:459
  346.9 6.1 %collective-permute-done.31 = f32[104,768]{1,0:T(8,128)S(1)} collective-permute-done((f32[104,768]{1,0:T(8,128)S(1)}, f32[104,768]{1,0:T(8,128)S(1)}, u32[]{:S(2)}, u32[]{:S(2)}) %collective-permute-start.31) | collective-permute-done | bytes 319520 | tf_op jit(solution)/shard_map/ppermute | solution.py:486
  354.6 10.5 %attn_bwd_peer.7 = bf16[2048,768]{1,0:T(8,128)(2,1)} custom-call(s32[4,4]{1,0:T(4,128)} %len_ref.21, bf16[2048,768]{1,0:T(8,128)(2,1)} %get-tuple-element.203.lm_ref, bf16[384,768]{1,0:T(8,128)(2,1)} %get-tuple-element.180.wmp_ref.wm_ref, bf16[2048,384]{1,0:T(8,128)(2,1)} %get-tuple-element.226.q_ref, ...), custom_call_target="tpu_custom_call", output_to_operand_aliasing={{}: (12, {})} | custom-call | flops 40000000000 | bytes 1000000 | tf_op jit(solution)/shard_map/attn_bwd_peer/pallas_call | solution.py:459
  365.1 18.5 %collective-permute-done.34 = f32[208,768]{1,0:T(8,128)S(1)} collective-permute-done((f32[208,768]{1,0:T(8,128)S(1)}, f32[208,768]{1,0:T(8,128)S(1)}, u32[]{:S(2)}, u32[]{:S(2)}) %collective-permute-start.34) | collective-permute-done | bytes 639008 | tf_op jit(solution)/shard_map/ppermute | solution.py:486
  384.5 8.8 %collective-permute-done.35 = f32[104,768]{1,0:T(8,128)S(1)} collective-permute-done((f32[104,768]{1,0:T(8,128)S(1)}, f32[104,768]{1,0:T(8,128)S(1)}, u32[]{:S(2)}, u32[]{:S(2)}) %collective-permute-start.35) | collective-permute-done | bytes 319520 | tf_op jit(solution)/shard_map/ppermute | solution.py:486
  399.6 4.9 %join.2 = f32[1536,768]{1,0:T(8,128)} custom-call(f32[768,768]{1,0:T(8,128)} %copy-done.3, f32[768,768]{1,0:T(8,128)} %collective-permute-done.42.other_ref), custom_call_target="tpu_custom_call" | custom-call | flops 100000000 | bytes 1000000 | tf_op jit(solution)/shard_map/join/pallas_call | solution.py:515
  404.5 8.7 %collective-permute-done.41 = f32[208,768]{1,0:T(8,128)S(1)} collective-permute-done((f32[208,768]{1,0:T(8,128)S(1)}, f32[208,768]{1,0:T(8,128)S(1)}, u32[]{:S(2)}, u32[]{:S(2)}) %collective-permute-start.41) | collective-permute-done | bytes 639008 | tf_op jit(solution)/shard_map/ppermute | solution.py:486
  418.1 5.3 %join.3 = f32[768,1536]{1,0:T(8,128)} custom-call(f32[384,1536]{1,0:T(8,128)} %copy-done.2, f32[384,1536]{1,0:T(8,128)} %copy-done.20), custom_call_target="tpu_custom_call" | custom-call | flops 100000000 | bytes 1000000 | tf_op jit(solution)/shard_map/join/pallas_call | solution.py:515
  425.6 4.9 %finish.1 = (f32[768,384]{1,0:T(8,128)}, f32[768,384]{1,0:T(8,128)}, f32[768,384]{1,0:T(8,128)}, f32[384,768]{1,0:T(8,128)}, f32[384]{0:T(512)}, /*index=5*/f32[...) custom-call(f32[416,768]{1,0:T(8,128)} %copy-done.5, ...), custom_call_target="tpu_custom_call" | custom-call | flops 100000000 | bytes 1000000 | tf_op jit(solution)/shard_map/finish/pallas_call | solution.py:604
  (236 shorter events, 109.0 us)
Async XLA Ops:
  3.2 17.6 %collective-permute-start = (f32[104,1536]{1,0:T(8,128)}, f32[104,1536]{1,0:T(8,128)S(1)}, u32[]{:S(2)}, u32[]{:S(2)}) collective-permute-start(f32[104,1536]{1,0:T(8,128)} %get-tuple-element.146), channel_id=1, source_target_pairs={{0,1},{1,0},{2,3},{3,2},{4,5},{5,4},{6,7},{7,6},{8,9},{9,8},{10,11... | collective-permute-start | bytes 1916936 | tf_op jit(solution)/shard_map/ppermute | solution.py:675
  20.9 15.6 %collective-permute-start.1 = (f32[48,1536]{1,0:T(8,128)S(1)}, f32[48,1536]{1,0:T(8,128)S(1)}, u32[]{:S(2)}, u32[]{:S(2)}) collective-permute-start(f32[48,1536]{1,0:T(8,128)S(1)} %get-tuple-element.288.rest_5_), channel_id=1, source_target_pairs={{0,4},{2,6},{4,0},{6,2},{8,12},{10,14},{12,8},{14,10},{16,20},{18,... | collective-permute-start | bytes 884744 | tf_op jit(solution)/shard_map/ppermute | solution.py:486
  55.0 27.8 %collective-permute-start.10 = (f32[384,768]{1,0:T(8,128)S(1)}, f32[384,768]{1,0:T(8,128)S(1)}, u32[]{:S(2)}, u32[]{:S(2)}) collective-permute-start(f32[384,768]{1,0:T(8,128)S(1)} %maximum_convert_fusion), channel_id=1, source_target_pairs={{0,1},{1,0},{2,3},{3,2},{4,5},{5,4},{6,7},{7,6},{8,9},{9,8},{10,11... | collective-permute-start | bytes 3538952 | tf_op jit(solution)/shard_map/ppermute | solution.py:687
  63.9 17.9 %collective-permute-start.9 = (f32[96,1536]{1,0:T(8,128)}, f32[96,1536]{1,0:T(8,128)S(1)}, u32[]{:S(2)}, u32[]{:S(2)}) collective-permute-start(f32[96,1536]{1,0:T(8,128)} %maximum_select_fusion.17.rest_1_), channel_id=1, source_target_pairs={{0,4},{2,6},{4,0},{6,2},{8,12},{10,14},{12,8},{14,10},{16,20},{18,... | collective-permute-start | bytes 1769480 | tf_op jit(solution)/shard_map/ppermute | solution.py:486
  64.5 17.3 %collective-permute-start.8 = (f32[96,1536]{1,0:T(8,128)S(1)}, f32[96,1536]{1,0:T(8,128)S(1)}, u32[]{:S(2)}, u32[]{:S(2)}) collective-permute-start(f32[96,1536]{1,0:T(8,128)S(1)} %maximum_select_fusion.16.rest_0_), channel_id=1, source_target_pairs={{0,8},{2,10},{4,12},{6,14},{8,0},{10,2},{12,4},{14,6},{16,24},{18,... | collective-permute-start | bytes 1769480 | tf_op jit(solution)/shard_map/ppermute | solution.py:486
  86.6 15.0 %collective-permute-start.15 = (f32[192,1536]{1,0:T(8,128)S(1)}, f32[192,1536]{1,0:T(8,128)S(1)}, u32[]{:S(2)}, u32[]{:S(2)}) collective-permute-start(f32[192,1536]{1,0:T(8,128)S(1)} %maximum_select_fusion.6.rest_5_.a_ref), channel_id=1, source_target_pairs={{0,2},{2,0},{4,6},{6,4},{8,10},{10,8},{12,14},{14,12},{16,18},{18,... | collective-permute-start | bytes 3538952 | tf_op jit(solution)/shard_map/ppermute | solution.py:486
  180.3 28.1 %collective-permute-start.20 = (f32[384,768]{1,0:T(8,128)S(1)}, f32[384,768]{1,0:T(8,128)S(1)}, u32[]{:S(2)}, u32[]{:S(2)}) collective-permute-start(f32[384,768]{1,0:T(8,128)S(1)} %constant_dynamic-slice_fusion.7.rest_0_), channel_id=1, source_target_pairs={{0,4},{2,6},{4,0},{6,2},{8,12},{10,14},{12,8},{14,10},{16,20},{18,... | collective-permute-start | bytes 3538952 | tf_op jit(solution)/shard_map/ppermute | solution.py:486
  208.6 33.0 %collective-permute-start.21 = (f32[192,768]{1,0:T(8,128)S(1)}, f32[192,768]{1,0:T(8,128)S(1)}, u32[]{:S(2)}, u32[]{:S(2)}) collective-permute-start(f32[192,768]{1,0:T(8,128)S(1)} %constant_dynamic-slice_fusion.6.rest_0_), channel_id=1, source_target_pairs={{0,8},{2,10},{4,12},{6,14},{8,0},{10,2},{12,4},{14,6},{16,24},{18,... | collective-permute-start | bytes 1769480 | tf_op jit(solution)/shard_map/ppermute | solution.py:486
  215.4 28.1 %collective-permute-start.23 = (f32[192,1536]{1,0:T(8,128)S(1)}, f32[192,1536]{1,0:T(8,128)S(1)}, u32[]{:S(2)}, u32[]{:S(2)}) collective-permute-start(f32[192,1536]{1,0:T(8,128)S(1)} %constant_dynamic-slice_fusion.5.rest_1_), channel_id=1, source_target_pairs={{0,4},{2,6},{4,0},{6,2},{8,12},{10,14},{12,8},{14,10},{16,20},{18,... | collective-permute-start | bytes 3538952 | tf_op jit(solution)/shard_map/ppermute | solution.py:486
  243.7 29.1 %collective-permute-start.25 = (f32[96,1536]{1,0:T(8,128)S(1)}, f32[96,1536]{1,0:T(8,128)S(1)}, u32[]{:S(2)}, u32[]{:S(2)}) collective-permute-start(f32[96,1536]{1,0:T(8,128)S(1)} %constant_dynamic-slice_fusion.4.rest_6_), channel_id=1, source_target_pairs={{0,8},{2,10},{4,12},{6,14},{8,0},{10,2},{12,4},{14,6},{16,24},{18,... | collective-permute-start | bytes 1769480 | tf_op jit(solution)/shard_map/ppermute | solution.py:486
  244.9 27.9 %collective-permute-start.24 = (f32[192,768]{1,0:T(8,128)S(1)}, f32[192,768]{1,0:T(8,128)S(1)}, u32[]{:S(2)}, u32[]{:S(2)}) collective-permute-start(f32[192,768]{1,0:T(8,128)S(1)} %dynamic-slice_add_fusion.5.rest_5_), channel_id=1, source_target_pairs={{0,16},{2,18},{4,20},{6,22},{8,24},{10,26},{12,28},{14,30},{16,0},... | collective-permute-start | bytes 1769480 | tf_op jit(solution)/shard_map/ppermute | solution.py:486
  273.9 26.5 %collective-permute-start.28 = (f32[192,768]{1,0:T(8,128)S(1)}, f32[192,768]{1,0:T(8,128)S(1)}, u32[]{:S(2)}, u32[]{:S(2)}) collective-permute-start(f32[192,768]{1,0:T(8,128)S(1)} %add.110.rest_4_), channel_id=1, source_target_pairs={{0,8},{2,10},{4,12},{6,14},{8,0},{10,2},{12,4},{14,6},{16,24},{18,... | collective-permute-start | bytes 1769480 | tf_op jit(solution)/shard_map/ppermute | solution.py:486
  275.2 40.0 %collective-permute-start.27 = (f32[96,1536]{1,0:T(8,128)}, f32[96,1536]{1,0:T(8,128)S(1)}, u32[]{:S(2)}, u32[]{:S(2)}) collective-permute-start(f32[96,1536]{1,0:T(8,128)} %dynamic-slice_add_fusion.4.rest_5_), channel_id=1, source_target_pairs={{0,16},{2,18},{4,20},{6,22},{8,24},{10,26},{12,28},{14,30},{16,0},... | collective-permute-start | bytes 1769480 | tf_op jit(solution)/shard_map/ppermute | solution.py:486
  302.9 81.7 %collective-permute-start.38 = (f32[192,768]{1,0:T(8,128)}, f32[192,768]{1,0:T(8,128)}, u32[]{:S(2)}, u32[]{:S(2)}) collective-permute-start(f32[192,768]{1,0:T(8,128)} %get-tuple-element.281), channel_id=1, source_target_pairs={{0,4},{2,6},{4,0},{6,2},{8,12},{10,14},{12,8},{14,10},{16,20},{18,... | collective-permute-start | bytes 1769480 | tf_op jit(solution)/shard_map/ppermute | solution.py:486
  317.0 17.3 %collective-permute-start.30 = (f32[208,768]{1,0:T(8,128)S(1)}, f32[208,768]{1,0:T(8,128)S(1)}, u32[]{:S(2)}, u32[]{:S(2)}) collective-permute-start(f32[208,768]{1,0:T(8,128)S(1)} %constant_dynamic-slice_fusion.2.rest_4_), channel_id=1, source_target_pairs={{0,8},{2,10},{4,12},{6,14},{8,0},{10,2},{12,4},{14,6},{16,24},{18,... | collective-permute-start | bytes 1916936 | tf_op jit(solution)/shard_map/ppermute | solution.py:486
  317.2 17.1 %collective-permute-start.29 = (f32[208,768]{1,0:T(8,128)S(1)}, f32[208,768]{1,0:T(8,128)S(1)}, u32[]{:S(2)}, u32[]{:S(2)}) collective-permute-start(f32[208,768]{1,0:T(8,128)S(1)} %constant_dynamic-slice_fusion.3.rest_3_), channel_id=1, source_target_pairs={{0,4},{2,6},{4,0},{6,2},{8,12},{10,14},{12,8},{14,10},{16,20},{18,... | collective-permute-start | bytes 1916936 | tf_op jit(solution)/shard_map/ppermute | solution.py:486
  317.6 29.3 %collective-permute-start.33 = (f32[96,1536]{1,0:T(8,128)S(1)}, f32[96,1536]{1,0:T(8,128)S(1)}, u32[]{:S(2)}, u32[]{:S(2)}) collective-permute-start(f32[96,1536]{1,0:T(8,128)S(1)} %add.112.rest_5_), channel_id=1, source_target_pairs={{0,8},{2,10},{4,12},{6,14},{8,0},{10,2},{12,4},{14,6},{16,24},{18,... | collective-permute-start | bytes 1769480 | tf_op jit(solution)/shard_map/ppermute | solution.py:486
  335.1 17.9 %collective-permute-start.31 = (f32[104,768]{1,0:T(8,128)S(1)}, f32[104,768]{1,0:T(8,128)S(1)}, u32[]{:S(2)}, u32[]{:S(2)}) collective-permute-start(f32[104,768]{1,0:T(8,128)S(1)} %constant_dynamic-slice_fusion.1.rest_3_), channel_id=1, source_target_pairs={{0,8},{2,10},{4,12},{6,14},{8,0},{10,2},{12,4},{14,6},{16,24},{18,... | collective-permute-start | bytes 958472 | tf_op jit(solution)/shard_map/ppermute | solution.py:486
  336.3 48.2 %collective-permute-start.39 = (f32[192,768]{1,0:T(8,128)S(1)}, f32[192,768]{1,0:T(8,128)S(1)}, u32[]{:S(2)}, u32[]{:S(2)}) collective-permute-start(f32[192,768]{1,0:T(8,128)S(1)} %get-tuple-element.243.rest_5_), channel_id=1, source_target_pairs={{0,4},{2,6},{4,0},{6,2},{8,12},{10,14},{12,8},{14,10},{16,20},{18,... | collective-permute-start | bytes 1769480 | tf_op jit(solution)/shard_map/ppermute | solution.py:486
  353.3 30.3 %collective-permute-start.34 = (f32[208,768]{1,0:T(8,128)S(1)}, f32[208,768]{1,0:T(8,128)S(1)}, u32[]{:S(2)}, u32[]{:S(2)}) collective-permute-start(f32[208,768]{1,0:T(8,128)S(1)} %pad_maximum_fusion.rest_3_), channel_id=1, source_target_pairs={{0,16},{2,18},{4,20},{6,22},{8,24},{10,26},{12,28},{14,30},{16,0},... | collective-permute-start | bytes 1916936 | tf_op jit(solution)/shard_map/ppermute | solution.py:486
  354.2 39.2 %collective-permute-start.37 = (f32[192,1536]{1,0:T(8,128)S(1)}, f32[192,1536]{1,0:T(8,128)S(1)}, u32[]{:S(2)}, u32[]{:S(2)}) collective-permute-start(f32[192,1536]{1,0:T(8,128)S(1)} %maximum_select_fusion.11.rest_4_), channel_id=1, source_target_pairs={{0,4},{2,6},{4,0},{6,2},{8,12},{10,14},{12,8},{14,10},{16,20},{18,... | collective-permute-start | bytes 3538952 | tf_op jit(solution)/shard_map/ppermute | solution.py:486
  396.3 18.4 %collective-permute-start.43 = (f32[384,1536]{1,0:T(8,128)S(1)}, f32[384,1536]{1,0:T(8,128)S(1)}, u32[]{:S(2)}, u32[]{:S(2)}) collective-permute-start(f32[384,1536]{1,0:T(8,128)S(1)} %maximum_select_fusion.1.mine_ref), channel_id=1, source_target_pairs={{0,2},{2,0},{4,6},{6,4},{8,10},{10,8},{12,14},{14,12},{16,18},{18,... | collective-permute-start | bytes 7077896 | tf_op jit(solution)/shard_map/ppermute | solution.py:486
  396.4 16.9 %collective-permute-start.41 = (f32[208,768]{1,0:T(8,128)S(1)}, f32[208,768]{1,0:T(8,128)S(1)}, u32[]{:S(2)}, u32[]{:S(2)}) collective-permute-start(f32[208,768]{1,0:T(8,128)S(1)} %maximum_select_fusion.13), channel_id=1, source_target_pairs={{0,8},{2,10},{4,12},{6,14},{8,0},{10,2},{12,4},{14,6},{16,24},{18,... | collective-permute-start | bytes 1916936 | tf_op jit(solution)/shard_map/ppermute | solution.py:486
  398.1 16.6 %collective-permute-start.40 = (f32[208,768]{1,0:T(8,128)S(1)}, f32[208,768]{1,0:T(8,128)S(1)}, u32[]{:S(2)}, u32[]{:S(2)}) collective-permute-start(f32[208,768]{1,0:T(8,128)S(1)} %maximum_select_fusion.12), channel_id=1, source_target_pairs={{0,4},{2,6},{4,0},{6,2},{8,12},{10,14},{12,8},{14,10},{16,20},{18,... | collective-permute-start | bytes 1916936 | tf_op jit(solution)/shard_map/ppermute | solution.py:486
  (70 other events, 453.6 us)

commit v4 on v3

--- a/solution.py
+++ b/solution.py
@@ -18,7 +18,6 @@
 BWD_GROUP = (2, 6, 6)
 BF = jnp.bfloat16
 F32 = jnp.float32
-VMEM_LIMIT = 56 * 1024 * 1024
 PAD = 32
 V_QV, V_MB, V_FG, V_FB, V_IB, V_OB, V_SG, V_SB = (0, 0), (0, 1), (1, 0), (1, 1), 2, (3, 0), (3, 1), (4, 0)
 
@@ -50,8 +49,8 @@
     return lax.broadcasted_iota(jnp.int32, (rows, 2 * HD), 1) < HD
 
 
-def params(**kw):
-    return pltpu.CompilerParams(vmem_limit_bytes=VMEM_LIMIT, **kw)
+def params(mib):
+    return pltpu.CompilerParams(vmem_limit_bytes=mib * 1024 * 1024)
 
 
 def full(shape):
@@ -115,7 +114,7 @@
                 l_ref[:, rows] = logs.T[:8]
 
 
-def attn_fwd(lengths, hidden, wq, wk, wv, vec, start, count, prior=None, after=()):
+def attn_fwd(lengths, hidden, wq, wk, wv, vec, start, count, prior=None, after=(), peer=False):
     n, d = hidden.shape
     half = wq.shape[1]
     blocks = n // MAXLEN
@@ -132,7 +131,7 @@
         out_specs=[rows_spec(half, start)] * 4 + [pl.BlockSpec((8, MAXLEN), lambda b: (b + start, 0))],
         out_shape=[wide] * 4 + [jax.ShapeDtypeStruct((8 * blocks, MAXLEN), F32)],
         input_output_aliases={6 + i: i for i in range(len(prior))},
-        compiler_params=params(),
+        compiler_params=params(20 if peer else 60),
         cost_estimate=cost(7 * count),
         name="attn_fwd",
     )(lengths, hidden, wq, wk, wv, vec, *extra)
@@ -253,7 +252,7 @@
             jax.ShapeDtypeStruct((8, d), F32),
         ],
         scratch_shapes=[pltpu.VMEM((MAXLEN, ff), BF), pltpu.VMEM((MAXLEN, d), F32), pltpu.VMEM((MAXLEN, d), F32)],
-        compiler_params=params(),
+        compiler_params=params(46),
         cost_estimate=cost(58),
         name="ff_fwd",
     )(lengths, hidden, co, cp, cot, wmo, wmp, wio, wip, woo, wop, vec, pvec)
@@ -297,7 +296,7 @@
             jax.ShapeDtypeStruct((1, ff), F32),
         ],
         scratch_shapes=[pltpu.VMEM((MAXLEN, ff), BF)],
-        compiler_params=params(),
+        compiler_params=params(30),
         cost_estimate=cost(26),
         name="ff_bwd_own",
     )(lo, low, gp, wi, wo, *after)
@@ -351,7 +350,7 @@
             jax.ShapeDtypeStruct((8, d), F32),
         ],
         scratch_shapes=[pltpu.VMEM((MAXLEN, d), F32)],
-        compiler_params=params(),
+        compiler_params=params(30),
         cost_estimate=cost(25),
         name="ff_bwd_peer",
     )(lo, gs, x, gp, opart, co, wi, wo, vec, *after)
@@ -468,7 +467,7 @@
         out_shape=out_shape,
         input_output_aliases={} if prior is None else {10 + len(extra): 0},
         scratch_shapes=[pltpu.VMEM((MAXLEN, half), BF)] * 4 + ([] if own else [pltpu.VMEM((MAXLEN, d), F32)]),
-        compiler_params=params(),
+        compiler_params=params(26 if own else 60),
         cost_estimate=cost(12 * count if own else 40),
         name="attn_bwd_own" if own else "attn_bwd_peer",
     )(lengths, lm, wm, q, k, v, logs, wq, wk, wv, *extra, *after)
@@ -515,7 +514,7 @@
     return pl.pallas_call(
         join_kernel,
         out_shape=jax.ShapeDtypeStruct((2 * mine.shape[0], mine.shape[1]), mine.dtype),
-        compiler_params=params(),
+        compiler_params=params(20),
         cost_estimate=cost(0.1),
         name="join",
     )(mine, other)
@@ -571,7 +570,7 @@
     return pl.pallas_call(
         prepare_kernel,
         out_shape=[jax.ShapeDtypeStruct((8, 2 * d), F32), jax.ShapeDtypeStruct((d // 8 + 8, 2 * d), F32)],
-        compiler_params=params(),
+        compiler_params=params(60),
         cost_estimate=cost(2),
         name="prepare",
     )(*weights, *vectors)
@@ -606,7 +605,7 @@
         out_shape=[jax.ShapeDtypeStruct((d, half), F32)] * 3
         + [jax.ShapeDtypeStruct((half, d), F32)]
         + [jax.ShapeDtypeStruct((size,), F32) for size in (half, half, d, d, d, 2 * d, d, d, d)],
-        compiler_params=params(),
+        compiler_params=params(20),
         cost_estimate=cost(0.1),
         name="finish",
     )(a, ra, b, rb)
@@ -640,7 +639,7 @@
     return pl.pallas_call(
         partial(assemble_kernel, square),
         out_shape=[jax.ShapeDtypeStruct(shape, BF) for shape in shapes],
-        compiler_params=params(),
+        compiler_params=params(16),
         cost_estimate=cost(4),
         name="assemble",
     )(a, ra, b, rb)
@@ -693,13 +692,13 @@
     ia, ib = in_order(NEAR, ia, ira), in_order(FAR, ib, irb)
     ira, irb = swap(ia, FAR, n_dp), swap(ib, NEAR, n_dp)
     wqp, wkp, wvp, wmp = assemble(True, ha, hra, hb, hrb)
-    peer = list(attn_fwd(lengths, hidden_in, wqp, wkp, wvp, pvec, 0, 2, None, (ia, ib)))
+    peer = list(attn_fwd(lengths, hidden_in, wqp, wkp, wvp, pvec, 0, 2, None, (ia, ib), True))
     ira, irb, o0, peer[0] = tie(ira, irb, o0, peer[0])
     ia, ib = in_order(FAR, ia, ira), in_order(NEAR, ib, irb)
     ira, irb = swap(ia, CORE, n_dp), swap(ib, CORE, n_dp)
     oa, ob = o0[:eighth], o0[eighth:]
     ora, orb = swap(oa, NEAR, n_dp), swap(ob, FAR, n_dp)
-    qp, kp, vp, cp, lgp = attn_fwd(lengths, hidden_in, wqp, wkp, wvp, pvec, 2, 2, peer, (ia, ib, oa, ob))
+    qp, kp, vp, cp, lgp = attn_fwd(lengths, hidden_in, wqp, wkp, wvp, pvec, 2, 2, peer, (ia, ib, oa, ob), True)
     ora, orb, cp = tie(ora, orb, cp)
     oa, ob = in_order(NEAR, oa, ora), in_order(FAR, ob, orb)
     ora, orb = swap(oa, CORE, n_dp), swap(ob, CORE, n_dp)

time: 437 us -> 416 us (0.952)
  Pallas kernels: 265 us -> 223 us
  waiting for transfers between devices: 89 us -> 100 us
  local copies, waits for them, and re-layouts: 16.3 us -> 22.6 us
    pallas_call x3, Pallas kernels: 11.8 us -> 0.73 us  [assemble(): pl.pallas_call(partial(assemble_kernel, square), out_shape=[jax.ShapeDtyp...]
    ppermute x43, waiting for transfers between devices: 84.6 us -> 93.1 us  [swap(): return lax.ppermute(x, 'dp', [(i, i ^ mask) for i in range(n_dp)])]
    pallas_call x6, Pallas kernels: 82.9 us -> 74.6 us  [attn_bwd(): pl.pallas_call(partial(attn_bwd_kernel, own, start, len(after)), grid=(co...]
    unnamed x96 -> x102, local copies, waits for them, and re-layouts: 11.8 us -> 18.5 us
    pallas_call x2, Pallas kernels: 10.2 us -> 5.01 us  [join(): pl.pallas_call(join_kernel, out_shape=jax.ShapeDtypeStruct((2 * mine.shap...]
    pallas_call x1, Pallas kernels: 25 us -> 20.2 us  [ff_bwd_peer(): pl.pallas_call(partial(ff_bwd_peer_kernel, len(after)), grid=(n // MAXLEN...]
  transfers between devices with their start and end apart: 46 -> 46, of which waited for: 23 -> 27; matrix products, arithmetic and copies ran while one was open for 3% -> 5% of each run, Pallas kernels for 45% -> 39%
where the time goes in v4:
time: 416 us; the launch traced here: 410 us
  Pallas kernels  223 us (54%)
  waiting for transfers between devices  100 us (24%)
  starting transfers between devices  40.8 us (10%)
  local copies, waits for them, and re-layouts  22.6 us (5%)
  other arithmetic  20.7 us (5%)
    ppermute x43, waiting for transfers between devices, swap(): return lax.ppermute(x, 'dp', [(i, i ^ mask) for i in range(n_dp)])  93.1 us
    pallas_call x6, Pallas kernels, attn_bwd(): pl.pallas_call(partial(attn_bwd_kernel, own, start, len(after)), grid=(co...  74.6 us
    pallas_call x1, Pallas kernels, ff_fwd(): pl.pallas_call(ff_fwd_kernel, grid=(n // MAXLEN,), in_specs=[SMEM, rows_s...  57.3 us
    pallas_call x4, Pallas kernels, attn_fwd(): pl.pallas_call(partial(attn_fwd_kernel, start, len(extra)), grid=(count,)...  37.8 us
    ppermute x43, starting transfers between devices, swap(): return lax.ppermute(x, 'dp', [(i, i ^ mask) for i in range(n_dp)])  34.8 us
    pallas_call x1, Pallas kernels, ff_bwd_own(): pl.pallas_call(partial(ff_bwd_own_kernel, len(after)), grid=(n // MAXLEN,...  22.7 us
    pallas_call x1, Pallas kernels, ff_bwd_peer(): pl.pallas_call(partial(ff_bwd_peer_kernel, len(after)), grid=(n // MAXLEN...  20.2 us
    unnamed x102, local copies, waits for them, and re-layouts  18.5 us
  transfers between devices with their start and end apart: 46, of which 27 were waited for; matrix products, arithmetic and copies ran while one was open for 5% of the time, Pallas kernels for 39%

profile of v4, /device:TPU:0, one launch (start us, length us, event | category | flops | bytes accessed | tf_op | source)
XLA Modules:
  0.0 409.7 jit_solution(18388301439743977822)
XLA Ops:
  6.2 10.2 %attn_fwd.4 = (bf16[2048,384]{1,0:T(8,128)(2,1)}, bf16[2048,384]{1,0:T(8,128)(2,1)}, bf16[2048,384]{1,0:T(8,128)(2,1)}, bf16[2048,384]{1,0:T(8,128)(2,1)}, f32[32,512]{1,0:T(8,128)}) custom-call(s32[4,4]{1,0:T(4,128)} %len_ref.21, bf16[2048,768]{1,0:T(8,128)(2,1)} %rest_0_.3, bf16[768,384]{1,0:T(8,128)(2,1)} %wq_ref.7, bf16[768,384]{1,0:T(8,128)(2,1)} %wk_ref.7, ...), custom_call_target="tpu_custom_call" | custom-call | flops 14000000000 | bytes 1000000 | tf_op jit(solution)/shard_map/attn_fwd/pallas_call | solution.py:124
  25.7 10.7 %attn_fwd.5 = (bf16[2048,384]{1,0:T(8,128)(2,1)}, bf16[2048,384]{1,0:T(8,128)(2,1)}, bf16[2048,384]{1,0:T(8,128)(2,1)}, bf16[2048,384]{1,0:T(8,128)(2,1)}, f32[32,512]{1,0:T(8,128)}) custom-call(s32[4,4]{1,0:T(4,128)} %len_ref.21, bf16[2048,768]{1,0:T(8,128)(2,1)} %rest_0_.3, ...), custom_call_target="tpu_custom_call", output_to_operand_aliasing={{0}: (6, {}), {1}: (7, {}), {2}: (8, {}), {3}: (9, {}), {4}... | custom-call | flops 14000000000 | bytes 1000000 | tf_op jit(solution)/shard_map/attn_fwd/pallas_call | solution.py:124
  40.5 11.5 %collective-permute-done.5 = f32[96,1536]{1,0:T(8,128)S(1)} collective-permute-done((f32[96,1536]{1,0:T(8,128)S(1)}, f32[96,1536]{1,0:T(8,128)S(1)}, u32[]{:S(2)}, u32[]{:S(2)}) %collective-permute-start.5) | collective-permute-done | bytes 589856 | tf_op jit(solution)/shard_map/ppermute | solution.py:485
  56.1 5.9 %collective-permute-done.6 = f32[48,1536]{1,0:T(8,128)S(1)} collective-permute-done((f32[48,1536]{1,0:T(8,128)S(1)}, f32[48,1536]{1,0:T(8,128)S(1)}, u32[]{:S(2)}, u32[]{:S(2)}) %collective-permute-start.6) | collective-permute-done | bytes 294944 | tf_op jit(solution)/shard_map/ppermute | solution.py:485
  65.9 8.3 %attn_fwd.6 = (bf16[2048,384]{1,0:T(8,128)(2,1)S(1)}, bf16[2048,384]{1,0:T(8,128)(2,1)S(1)}, bf16[2048,384]{1,0:T(8,128)(2,1)S(1)}, bf16[2048,384]{1,0:T(8,128)(2,1)S(1)}, f32[32,512]{1,0:T(8,128)S(1)}) custom-call(s32[4,4]{1,0:T(4,128)S(1)} %copy-done.8, bf16[2048,768]{1,0:T(8,128)(2,1)S(1)} %copy-done.2, bf16[768,384]{1,0:T(8,128)(2,1)S(1)} %get-tuple-element.166.wq_ref, ...), custom_call_target="tpu_custom_call" | custom-call | flops 14000000000 | bytes 1000000 | tf_op jit(solution)/shard_map/attn_fwd/pallas_call | solution.py:124
  74.1 3.9 collective-permute-done.9
  78.5 3.9 collective-permute-done.10
  85.4 8.6 %attn_fwd.7 = (bf16[2048,384]{1,0:T(8,128)(2,1)S(1)}, bf16[2048,384]{1,0:T(8,128)(2,1)S(1)}, bf16[2048,384]{1,0:T(8,128)(2,1)S(1)}, bf16[2048,384]{1,0:T(8,128)(2,1)S(1)}, f32[32,512]{1,0:T(8,128)S(1)}) custom-call(s32[4,4]{1,0:T(4,128)S(1)} %copy-done.8, ...), custom_call_target="tpu_custom_call", output_to_operand_aliasing={{0}: (6, {}), {1}: (7, {}), {2}: (8, {}), {3}: (9, {}), {4}... | custom-call | flops 14000000000 | bytes 1000000 | tf_op jit(solution)/shard_map/attn_fwd/pallas_call | solution.py:124
  104.1 57.3 %ff_fwd.1 = (bf16[2048,768]{1,0:T(8,128)(2,1)}, f32[2048,768]{1,0:T(8,128)}, bf16[2048,768]{1,0:T(8,128)(2,1)}, f32[2048,768]{1,0:T(8,128)}, bf16[2048,768]{1,0:...) custom-call(s32[4,4]{1,0:T(4,128)S(1)} %copy-done.8, ...), custom_call_target="tpu_custom_call" | custom-call | flops 57999998976 | bytes 1000000 | tf_op jit(solution)/shard_map/ff_fwd/pallas_call | solution.py:231
  161.6 4.8 %collective-permute-done.19 = f32[768,768]{1,0:T(8,128)} collective-permute-done((f32[768,768]{1,0:T(8,128)}, f32[768,768]{1,0:T(8,128)}, u32[]{:S(2)}, u32[]{:S(2)}) %collective-permute-start.19) | collective-permute-done | bytes 2359328 | tf_op jit(solution)/shard_map/ppermute | solution.py:485
  173.2 22.7 %ff_bwd_own.1 = (f32[2048,768]{1,0:T(8,128)S(1)}, f32[384,1536]{1,0:T(8,128)S(1)}, f32[384,1536]{1,0:T(8,128)}, f32[1,1536]{1,0:T(1,128)S(1)}) custom-call(bf16[2048,768]{1,0:T(8,128)(2,1)S(1)} %copy-done.22, bf16[2048,768]{1,0:T(8,128)(2,1)S(1)} %copy-done.33, f32[2048,1536]{1,0:T(8,128)} %get-tuple-element.190.gp_ref, bf16[768,1536]{1,0:T(8,128)(2,1)S(1)} %copy-done.1, ...), custom_call_target="tpu_custom_call" | custom-call | flops 25999998976 | bytes 1000000 | tf_op jit(solution)/shard_map/ff_bwd_own/pallas_call | solution.py:287
  208.1 20.2 %ff_bwd_peer.1 = (f32[2048,768]{1,0:T(8,128)S(1)}, bf16[2048,768]{1,0:T(8,128)(2,1)S(1)}, f32[384,768]{1,0:T(8,128)S(1)}, f32[8,768]{1,0:T(8,128)S(1)}) custom-call(bf16[2048,768]{1,0:T(8,128)(2,1)S(1)} %copy-done.23, f32[2048,768]{1,0:T(8,128)} %get-tuple-element.198.gs_ref, f32[2048,768]{1,0:T(8,128)} %get-tuple-element.199.x_ref, ...), custom_call_target="tpu_custom_call" | custom-call | flops 24999999488 | bytes 1000000 | tf_op jit(solution)/shard_map/ff_bwd_peer/pallas_call | solution.py:338
  237.9 17.8 %attn_bwd_own.2 = (f32[2048,768]{1,0:T(8,128)S(1)}, f32[416,1536]{1,0:T(8,128)S(1)}, f32[416,1536]{1,0:T(8,128)S(1)}) custom-call(s32[4,4]{1,0:T(4,128)S(1)} %copy-done.8, bf16[2048,768]{1,0:T(8,128)(2,1)S(1)} %get-tuple-element.203.lm_ref, bf16[384,768]{1,0:T(8,128)(2,1)S(1)} %copy-done.7, bf16[2048,384]{1,0:T(8,128)(2,1)S(1)} %copy-done.27, ...), custom_call_target="tpu_custom_call" | custom-call | flops 24000000000 | bytes 1000000 | tf_op jit(solution)/shard_map/attn_bwd_own/pallas_call | solution.py:458
  258.4 4.8 %collective-permute-done.24 = f32[192,768]{1,0:T(8,128)S(1)} collective-permute-done((f32[192,768]{1,0:T(8,128)S(1)}, f32[192,768]{1,0:T(8,128)S(1)}, u32[]{:S(2)}, u32[]{:S(2)}) %collective-permute-start.24) | collective-permute-done | bytes 589856 | tf_op jit(solution)/shard_map/ppermute | solution.py:485
  266.5 18.7 %attn_bwd_own.3 = (f32[2048,768]{1,0:T(8,128)}, f32[416,1536]{1,0:T(8,128)S(1)}, f32[416,1536]{1,0:T(8,128)}) custom-call(s32[4,4]{1,0:T(4,128)S(1)} %copy-done.8, bf16[2048,768]{1,0:T(8,128)(2,1)S(1)} %get-tuple-element.203.lm_ref, bf16[384,768]{1,0:T(8,128)(2,1)S(1)} %copy-done.7, ...), custom_call_target="tpu_custom_call", output_to_operand_aliasing={{0}: (13, {})} | custom-call | flops 24000000000 | bytes 1000000 | tf_op jit(solution)/shard_map/attn_bwd_own/pallas_call | solution.py:458
  290.8 10.5 %attn_bwd_peer.4.rest_2_ = bf16[2048,768]{1,0:T(8,128)(2,1)} custom-call(s32[4,4]{1,0:T(4,128)} %len_ref.21, bf16[2048,768]{1,0:T(8,128)(2,1)} %copy-done.21, bf16[384,768]{1,0:T(8,128)(2,1)} %copy-done.16, bf16[2048,384]{1,0:T(8,128)(2,1)} %copy-done.24, bf16[2048,384]{1,0:T(8,128)(2,1)} %copy-done.25, bf16[2048,384]{1,0:T(8,128)(2,1)} %copy-done.26, ...), custom_call_target="tpu_custom_call" | custom-call | flops 40000000000 | bytes 1000000 | tf_op jit(solution)/shard_map/attn_bwd_peer/pallas_call | solution.py:458
  308.2 8.5 %attn_bwd_peer.5.rest_2_ = bf16[2048,768]{1,0:T(8,128)(2,1)} custom-call(s32[4,4]{1,0:T(4,128)} %len_ref.21, bf16[2048,768]{1,0:T(8,128)(2,1)} %copy-done.21, bf16[384,768]{1,0:T(8,128)(2,1)} %copy-done.16, bf16[2048,384]{1,0:T(8,128)(2,1)} %copy-done.24, bf16[2048,384]{1,0:T(8,128)(2,1)} %copy-done.25, ...), custom_call_target="tpu_custom_call", output_to_operand_aliasing={{}: (12, {})} | custom-call | flops 40000000000 | bytes 1000000 | tf_op jit(solution)/shard_map/attn_bwd_peer/pallas_call | solution.py:458
  316.7 6.4 %collective-permute-done.30 = f32[208,768]{1,0:T(8,128)} collective-permute-done((f32[208,768]{1,0:T(8,128)S(1)}, f32[208,768]{1,0:T(8,128)}, u32[]{:S(2)}, u32[]{:S(2)}) %collective-permute-start.30) | collective-permute-done | bytes 639008 | tf_op jit(solution)/shard_map/ppermute | solution.py:485
  327.8 8.6 %attn_bwd_peer.6.rest_2_ = bf16[2048,768]{1,0:T(8,128)(2,1)} custom-call(s32[4,4]{1,0:T(4,128)} %len_ref.21, bf16[2048,768]{1,0:T(8,128)(2,1)} %copy-done.21, bf16[384,768]{1,0:T(8,128)(2,1)} %copy-done.16, bf16[2048,384]{1,0:T(8,128)(2,1)} %copy-done.24, bf16[2048,384]{1,0:T(8,128)(2,1)} %copy-done.25, ...), custom_call_target="tpu_custom_call", output_to_operand_aliasing={{}: (12, {})} | custom-call | flops 40000000000 | bytes 1000000 | tf_op jit(solution)/shard_map/attn_bwd_peer/pallas_call | solution.py:458
  337.1 3.0 collective-permute-done.31
  345.2 10.5 %attn_bwd_peer.7 = bf16[2048,768]{1,0:T(8,128)(2,1)} custom-call(s32[4,4]{1,0:T(4,128)} %len_ref.21, bf16[2048,768]{1,0:T(8,128)(2,1)} %copy-done.21, bf16[384,768]{1,0:T(8,128)(2,1)} %copy-done.16, bf16[2048,384]{1,0:T(8,128)(2,1)} %copy-done.24, bf16[2048,384]{1,0:T(8,128)(2,1)} %copy-done.25, ...), custom_call_target="tpu_custom_call", output_to_operand_aliasing={{}: (12, {})} | custom-call | flops 40000000000 | bytes 1000000 | tf_op jit(solution)/shard_map/attn_bwd_peer/pallas_call | solution.py:458
  355.7 15.7 %collective-permute-done.34 = f32[208,768]{1,0:T(8,128)} collective-permute-done((f32[208,768]{1,0:T(8,128)S(1)}, f32[208,768]{1,0:T(8,128)}, u32[]{:S(2)}, u32[]{:S(2)}) %collective-permute-start.34) | collective-permute-done | bytes 639008 | tf_op jit(solution)/shard_map/ppermute | solution.py:485
  373.7 7.5 %collective-permute-done.35 = f32[104,768]{1,0:T(8,128)S(1)} collective-permute-done((f32[104,768]{1,0:T(8,128)S(1)}, f32[104,768]{1,0:T(8,128)S(1)}, u32[]{:S(2)}, u32[]{:S(2)}) %collective-permute-start.35) | collective-permute-done | bytes 319520 | tf_op jit(solution)/shard_map/ppermute | solution.py:485
  391.5 10.2 %collective-permute-done.41 = f32[208,768]{1,0:T(8,128)S(1)} collective-permute-done((f32[208,768]{1,0:T(8,128)S(1)}, f32[208,768]{1,0:T(8,128)S(1)}, u32[]{:S(2)}, u32[]{:S(2)}) %collective-permute-start.41) | collective-permute-done | bytes 639008 | tf_op jit(solution)/shard_map/ppermute | solution.py:485
  (242 shorter events, 117.8 us)
Async XLA Ops:
  3.2 17.6 %collective-permute-start = (f32[104,1536]{1,0:T(8,128)}, f32[104,1536]{1,0:T(8,128)S(1)}, u32[]{:S(2)}, u32[]{:S(2)}) collective-permute-start(f32[104,1536]{1,0:T(8,128)} %get-tuple-element.146), channel_id=1, source_target_pairs={{0,1},{1,0},{2,3},{3,2},{4,5},{5,4},{6,7},{7,6},{8,9},{9,8},{10,11... | collective-permute-start | bytes 1916936 | tf_op jit(solution)/shard_map/ppermute | solution.py:674
  20.9 15.6 %collective-permute-start.1 = (f32[48,1536]{1,0:T(8,128)S(1)}, f32[48,1536]{1,0:T(8,128)S(1)}, u32[]{:S(2)}, u32[]{:S(2)}) collective-permute-start(f32[48,1536]{1,0:T(8,128)S(1)} %get-tuple-element.288.rest_5_), channel_id=1, source_target_pairs={{0,4},{2,6},{4,0},{6,2},{8,12},{10,14},{12,8},{14,10},{16,20},{18,... | collective-permute-start | bytes 884744 | tf_op jit(solution)/shard_map/ppermute | solution.py:485
  54.6 27.8 %collective-permute-start.10 = (f32[384,768]{1,0:T(8,128)S(1)}, f32[384,768]{1,0:T(8,128)S(1)}, u32[]{:S(2)}, u32[]{:S(2)}) collective-permute-start(f32[384,768]{1,0:T(8,128)S(1)} %maximum_convert_fusion), channel_id=1, source_target_pairs={{0,1},{1,0},{2,3},{3,2},{4,5},{5,4},{6,7},{7,6},{8,9},{9,8},{10,11... | collective-permute-start | bytes 3538952 | tf_op jit(solution)/shard_map/ppermute | solution.py:686
  63.3 14.7 %collective-permute-start.9 = (f32[96,1536]{1,0:T(8,128)S(1)}, f32[96,1536]{1,0:T(8,128)S(1)}, u32[]{:S(2)}, u32[]{:S(2)}) collective-permute-start(f32[96,1536]{1,0:T(8,128)S(1)} %maximum_select_fusion.17.rest_1_), channel_id=1, source_target_pairs={{0,4},{2,6},{4,0},{6,2},{8,12},{10,14},{12,8},{14,10},{16,20},{18,... | collective-permute-start | bytes 1769480 | tf_op jit(solution)/shard_map/ppermute | solution.py:485
  64.0 14.5 %collective-permute-start.8 = (f32[96,1536]{1,0:T(8,128)S(1)}, f32[96,1536]{1,0:T(8,128)S(1)}, u32[]{:S(2)}, u32[]{:S(2)}) collective-permute-start(f32[96,1536]{1,0:T(8,128)S(1)} %maximum_select_fusion.16.rest_0_), channel_id=1, source_target_pairs={{0,8},{2,10},{4,12},{6,14},{8,0},{10,2},{12,4},{14,6},{16,24},{18,... | collective-permute-start | bytes 1769480 | tf_op jit(solution)/shard_map/ppermute | solution.py:485
  82.7 14.4 %collective-permute-start.13 = (f32[192,768]{1,0:T(8,128)S(1)}, f32[192,768]{1,0:T(8,128)S(1)}, u32[]{:S(2)}, u32[]{:S(2)}) collective-permute-start(f32[192,768]{1,0:T(8,128)S(1)} %get-tuple-element.284.rest_7_), channel_id=1, source_target_pairs={{0,4},{2,6},{4,0},{6,2},{8,12},{10,14},{12,8},{14,10},{16,20},{18,... | collective-permute-start | bytes 1769480 | tf_op jit(solution)/shard_map/ppermute | solution.py:485
  168.6 29.9 %collective-permute-start.20 = (f32[384,768]{1,0:T(8,128)S(1)}, f32[384,768]{1,0:T(8,128)}, u32[]{:S(2)}, u32[]{:S(2)}) collective-permute-start(f32[384,768]{1,0:T(8,128)S(1)} %constant_dynamic-slice_fusion.7.rest_0_), channel_id=1, source_target_pairs={{0,4},{2,6},{4,0},{6,2},{8,12},{10,14},{12,8},{14,10},{16,20},{18,... | collective-permute-start | bytes 3538952 | tf_op jit(solution)/shard_map/ppermute | solution.py:485
  200.4 30.4 %collective-permute-start.21 = (f32[192,768]{1,0:T(8,128)S(1)}, f32[192,768]{1,0:T(8,128)S(1)}, u32[]{:S(2)}, u32[]{:S(2)}) collective-permute-start(f32[192,768]{1,0:T(8,128)S(1)} %constant_dynamic-slice_fusion.6.rest_0_), channel_id=1, source_target_pairs={{0,8},{2,10},{4,12},{6,14},{8,0},{10,2},{12,4},{14,6},{16,24},{18,... | collective-permute-start | bytes 1769480 | tf_op jit(solution)/shard_map/ppermute | solution.py:485
  205.7 28.1 %collective-permute-start.23 = (f32[192,1536]{1,0:T(8,128)S(1)}, f32[192,1536]{1,0:T(8,128)S(1)}, u32[]{:S(2)}, u32[]{:S(2)}) collective-permute-start(f32[192,1536]{1,0:T(8,128)S(1)} %constant_dynamic-slice_fusion.5.rest_1_), channel_id=1, source_target_pairs={{0,4},{2,6},{4,0},{6,2},{8,12},{10,14},{12,8},{14,10},{16,20},{18,... | collective-permute-start | bytes 3538952 | tf_op jit(solution)/shard_map/ppermute | solution.py:485
  234.0 29.1 %collective-permute-start.25 = (f32[96,1536]{1,0:T(8,128)S(1)}, f32[96,1536]{1,0:T(8,128)S(1)}, u32[]{:S(2)}, u32[]{:S(2)}) collective-permute-start(f32[96,1536]{1,0:T(8,128)S(1)} %constant_dynamic-slice_fusion.4.rest_6_), channel_id=1, source_target_pairs={{0,8},{2,10},{4,12},{6,14},{8,0},{10,2},{12,4},{14,6},{16,24},{18,... | collective-permute-start | bytes 1769480 | tf_op jit(solution)/shard_map/ppermute | solution.py:485
  235.2 28.0 %collective-permute-start.24 = (f32[192,768]{1,0:T(8,128)S(1)}, f32[192,768]{1,0:T(8,128)S(1)}, u32[]{:S(2)}, u32[]{:S(2)}) collective-permute-start(f32[192,768]{1,0:T(8,128)S(1)} %dynamic-slice_add_fusion.5.rest_5_), channel_id=1, source_target_pairs={{0,16},{2,18},{4,20},{6,22},{8,24},{10,26},{12,28},{14,30},{16,0},... | collective-permute-start | bytes 1769480 | tf_op jit(solution)/shard_map/ppermute | solution.py:485
  263.3 23.6 %collective-permute-start.28 = (f32[192,768]{1,0:T(8,128)S(1)}, f32[192,768]{1,0:T(8,128)S(1)}, u32[]{:S(2)}, u32[]{:S(2)}) collective-permute-start(f32[192,768]{1,0:T(8,128)S(1)} %add.110.rest_4_), channel_id=1, source_target_pairs={{0,8},{2,10},{4,12},{6,14},{8,0},{10,2},{12,4},{14,6},{16,24},{18,... | collective-permute-start | bytes 1769480 | tf_op jit(solution)/shard_map/ppermute | solution.py:485
  263.6 37.6 %collective-permute-start.27 = (f32[96,1536]{1,0:T(8,128)S(1)}, f32[96,1536]{1,0:T(8,128)}, u32[]{:S(2)}, u32[]{:S(2)}) collective-permute-start(f32[96,1536]{1,0:T(8,128)S(1)} %dynamic-slice_add_fusion.4.rest_5_), channel_id=1, source_target_pairs={{0,16},{2,18},{4,20},{6,22},{8,24},{10,26},{12,28},{14,30},{16,0},... | collective-permute-start | bytes 1769480 | tf_op jit(solution)/shard_map/ppermute | solution.py:485
  285.2 16.1 %collective-permute-start.26 = (f32[416,1536]{1,0:T(8,128)}, f32[416,1536]{1,0:T(8,128)}, u32[]{:S(2)}, u32[]{:S(2)}) collective-permute-start(f32[416,1536]{1,0:T(8,128)} %get-tuple-element.225), channel_id=1, source_target_pairs={{0,2},{2,0},{4,6},{6,4},{8,10},{10,8},{12,14},{14,12},{16,18},{18,... | collective-permute-start | bytes 7667720 | tf_op jit(solution)/shard_map/ppermute | solution.py:485
  289.1 84.6 %collective-permute-start.38 = (f32[192,768]{1,0:T(8,128)}, f32[192,768]{1,0:T(8,128)}, u32[]{:S(2)}, u32[]{:S(2)}) collective-permute-start(f32[192,768]{1,0:T(8,128)} %get-tuple-element.281), channel_id=1, source_target_pairs={{0,4},{2,6},{4,0},{6,2},{8,12},{10,14},{12,8},{14,10},{16,20},{18,... | collective-permute-start | bytes 1769480 | tf_op jit(solution)/shard_map/ppermute | solution.py:485
  305.6 17.5 %collective-permute-start.30 = (f32[208,768]{1,0:T(8,128)S(1)}, f32[208,768]{1,0:T(8,128)}, u32[]{:S(2)}, u32[]{:S(2)}) collective-permute-start(f32[208,768]{1,0:T(8,128)S(1)} %constant_dynamic-slice_fusion.2.rest_4_), channel_id=1, source_target_pairs={{0,8},{2,10},{4,12},{6,14},{8,0},{10,2},{12,4},{14,6},{16,24},{18,... | collective-permute-start | bytes 1916936 | tf_op jit(solution)/shard_map/ppermute | solution.py:485
  305.8 17.3 %collective-permute-start.29 = (f32[208,768]{1,0:T(8,128)S(1)}, f32[208,768]{1,0:T(8,128)}, u32[]{:S(2)}, u32[]{:S(2)}) collective-permute-start(f32[208,768]{1,0:T(8,128)S(1)} %constant_dynamic-slice_fusion.3.rest_3_), channel_id=1, source_target_pairs={{0,4},{2,6},{4,0},{6,2},{8,12},{10,14},{12,8},{14,10},{16,20},{18,... | collective-permute-start | bytes 1916936 | tf_op jit(solution)/shard_map/ppermute | solution.py:485
  306.2 30.2 %collective-permute-start.33 = (f32[96,1536]{1,0:T(8,128)}, f32[96,1536]{1,0:T(8,128)}, u32[]{:S(2)}, u32[]{:S(2)}) collective-permute-start(f32[96,1536]{1,0:T(8,128)} %add.112.rest_5_), channel_id=1, source_target_pairs={{0,8},{2,10},{4,12},{6,14},{8,0},{10,2},{12,4},{14,6},{16,24},{18,... | collective-permute-start | bytes 1769480 | tf_op jit(solution)/shard_map/ppermute | solution.py:485
  326.0 47.6 %collective-permute-start.39 = (f32[192,768]{1,0:T(8,128)}, f32[192,768]{1,0:T(8,128)}, u32[]{:S(2)}, u32[]{:S(2)}) collective-permute-start(f32[192,768]{1,0:T(8,128)} %get-tuple-element.243.rest_5_), channel_id=1, source_target_pairs={{0,4},{2,6},{4,0},{6,2},{8,12},{10,14},{12,8},{14,10},{16,20},{18,... | collective-permute-start | bytes 1769480 | tf_op jit(solution)/shard_map/ppermute | solution.py:485
  342.2 29.2 %collective-permute-start.34 = (f32[208,768]{1,0:T(8,128)S(1)}, f32[208,768]{1,0:T(8,128)}, u32[]{:S(2)}, u32[]{:S(2)}) collective-permute-start(f32[208,768]{1,0:T(8,128)S(1)} %pad_maximum_fusion.rest_3_), channel_id=1, source_target_pairs={{0,16},{2,18},{4,20},{6,22},{8,24},{10,26},{12,28},{14,30},{16,0},... | collective-permute-start | bytes 1916936 | tf_op jit(solution)/shard_map/ppermute | solution.py:485
  344.9 37.6 %collective-permute-start.37 = (f32[192,1536]{1,0:T(8,128)S(1)}, f32[192,1536]{1,0:T(8,128)S(1)}, u32[]{:S(2)}, u32[]{:S(2)}) collective-permute-start(f32[192,1536]{1,0:T(8,128)S(1)} %maximum_select_fusion.11.rest_4_), channel_id=1, source_target_pairs={{0,4},{2,6},{4,0},{6,2},{8,12},{10,14},{12,8},{14,10},{16,20},{18,... | collective-permute-start | bytes 3538952 | tf_op jit(solution)/shard_map/ppermute | solution.py:485
  384.7 17.3 %collective-permute-start.43 = (f32[384,1536]{1,0:T(8,128)S(1)}, f32[384,1536]{1,0:T(8,128)S(1)}, u32[]{:S(2)}, u32[]{:S(2)}) collective-permute-start(f32[384,1536]{1,0:T(8,128)S(1)} %maximum_select_fusion.1.mine_ref), channel_id=1, source_target_pairs={{0,2},{2,0},{4,6},{6,4},{8,10},{10,8},{12,14},{14,12},{16,18},{18,... | collective-permute-start | bytes 7077896 | tf_op jit(solution)/shard_map/ppermute | solution.py:485
  385.3 16.4 %collective-permute-start.41 = (f32[208,768]{1,0:T(8,128)S(1)}, f32[208,768]{1,0:T(8,128)S(1)}, u32[]{:S(2)}, u32[]{:S(2)}) collective-permute-start(f32[208,768]{1,0:T(8,128)S(1)} %maximum_select_fusion.13), channel_id=1, source_target_pairs={{0,8},{2,10},{4,12},{6,14},{8,0},{10,2},{12,4},{14,6},{16,24},{18,... | collective-permute-start | bytes 1916936 | tf_op jit(solution)/shard_map/ppermute | solution.py:485
  385.9 16.1 %collective-permute-start.40 = (f32[208,768]{1,0:T(8,128)S(1)}, f32[208,768]{1,0:T(8,128)S(1)}, u32[]{:S(2)}, u32[]{:S(2)}) collective-permute-start(f32[208,768]{1,0:T(8,128)S(1)} %maximum_select_fusion.12), channel_id=1, source_target_pairs={{0,4},{2,6},{4,0},{6,2},{8,12},{10,14},{12,8},{14,10},{16,20},{18,... | collective-permute-start | bytes 1916936 | tf_op jit(solution)/shard_map/ppermute | solution.py:485
  (73 other events, 591.3 us)

commit v5 on v4

--- a/solution.py
+++ b/solution.py
@@ -172,7 +172,7 @@
     b = pl.program_id(0)
     d = h_ref.shape[1]
     ff = wio_ref.shape[1]
-    width = 512
+    width = 1536
     pa_ref[...] = dot(co_ref[...], wmo_ref[...])
     pb_ref[...] = dot(cp_ref[...], wmp_ref[...])
     mixed = (pa_ref[...] + pb_ref[...]) + vector(vec_ref, V_MB)
@@ -724,10 +724,10 @@
     o, i, lm = tie(o, i, lm)
     i2 = kept(i1, NEAR) + i
     i_out = away(i2, FAR)
+    o3 = kept(o2, FAR) + o
+    o = exchange(o3, 2 * FAR, n_dp)
+    i_out, o3 = tie(i_out, o3)
     i = swap(i_out, FAR, n_dp)
-    o3 = kept(o2, FAR) + o
-    o3, i_out = tie(o3, i_out)
-    o = exchange(o3, 2 * FAR, n_dp)
     own = (lengths, lm, mixer_weight, qo, ko, vo, lgo, query_weight, key_weight, value_weight)
     part, hk, ha = attn_bwd(True, 0, 2, *own, (hidden_in, mwg, isums, ibg, osums), None, (o3, i_out))
     o, i, part = tie(o, i, part)
@@ -743,7 +743,7 @@
     cut = o.shape[0] // 2
     oa_, ob = swap(o[:cut], NEAR, n_dp), o[cut:]
     peer = (lengths, lm, wmp, qp, kp, vp, lgp, wqp, wkp, wvp)
-    (ig,) = attn_bwd(False, 0, 1, *peer, (gm, part), None, (o,))
+    (ig,) = attn_bwd(False, 1, 1, *peer, (gm, part), None, (o,))
     h, i, ig = tie(h, i, ig)
     h1 = hk + h
     ha, hb = h1[:, :d], h1[:, d:]
@@ -752,7 +752,7 @@
     i = beyond(i3 + i, n_dp)
     i, hb_out = tie(i, hb_out)
     i_ = swap(i, FAR, n_dp)
-    (ig,) = attn_bwd(False, 1, 1, *peer, (gm, part), ig, (ha_out, hb_out, i))
+    (ig,) = attn_bwd(False, 0, 1, *peer, (gm, part), ig, (ha_out, hb_out, i))
     hra, hrb, ob, ig = tie(hra, hrb, ob, ig)
     ha, hb = kept(ha, NEAR) + hra, kept(hb, FAR) + hrb
     ha_out, hb_out = away(ha, FAR), away(hb, NEAR)

time: 416 us -> 412 us (level)
  transfers between devices with their start and end apart: 46 -> 46, of which waited for: 27 -> 27; matrix products, arithmetic and copies ran while one was open for 5% -> 5% of each run, Pallas kernels for 39% -> 40%
where the time goes in v5:
time: 412 us; the launch traced here: 405 us
  Pallas kernels  220 us (53%)
  waiting for transfers between devices  99.1 us (24%)
  starting transfers between devices  41 us (10%)
  local copies, waits for them, and re-layouts  22.6 us (5%)
  other arithmetic  20.7 us (5%)
    ppermute x43, waiting for transfers between devices, swap(): return lax.ppermute(x, 'dp', [(i, i ^ mask) for i in range(n_dp)])  91.8 us
    pallas_call x6, Pallas kernels, attn_bwd(): pl.pallas_call(partial(attn_bwd_kernel, own, start, len(after)), grid=(co...  74.6 us
    pallas_call x1, Pallas kernels, ff_fwd(): pl.pallas_call(ff_fwd_kernel, grid=(n // MAXLEN,), in_specs=[SMEM, rows_s...  54 us
    pallas_call x4, Pallas kernels, attn_fwd(): pl.pallas_call(partial(attn_fwd_kernel, start, len(extra)), grid=(count,)...  37.8 us
    ppermute x43, starting transfers between devices, swap(): return lax.ppermute(x, 'dp', [(i, i ^ mask) for i in range(n_dp)])  35 us
    pallas_call x1, Pallas kernels, ff_bwd_own(): pl.pallas_call(partial(ff_bwd_own_kernel, len(after)), grid=(n // MAXLEN,...  22.7 us
    pallas_call x1, Pallas kernels, ff_bwd_peer(): pl.pallas_call(partial(ff_bwd_peer_kernel, len(after)), grid=(n // MAXLEN...  20.2 us
    unnamed x102, local copies, waits for them, and re-layouts  18.6 us
  transfers between devices with their start and end apart: 46, of which 27 were waited for; matrix products, arithmetic and copies ran while one was open for 5% of the time, Pallas kernels for 40%

profile of v5, /device:TPU:0, one launch (start us, length us, event | category | flops | bytes accessed | tf_op | source)
XLA Modules:
  0.0 405.3 jit_solution(5551115276199037663)
XLA Ops:
  6.2 10.2 %attn_fwd.4 = (bf16[2048,384]{1,0:T(8,128)(2,1)}, bf16[2048,384]{1,0:T(8,128)(2,1)}, bf16[2048,384]{1,0:T(8,128)(2,1)}, bf16[2048,384]{1,0:T(8,128)(2,1)}, f32[32,512]{1,0:T(8,128)}) custom-call(s32[4,4]{1,0:T(4,128)} %len_ref.21, bf16[2048,768]{1,0:T(8,128)(2,1)} %rest_0_.3, bf16[768,384]{1,0:T(8,128)(2,1)} %wq_ref.7, bf16[768,384]{1,0:T(8,128)(2,1)} %wk_ref.7, ...), custom_call_target="tpu_custom_call" | custom-call | flops 14000000000 | bytes 1000000 | tf_op jit(solution)/shard_map/attn_fwd/pallas_call | solution.py:124
  25.7 10.7 %attn_fwd.5 = (bf16[2048,384]{1,0:T(8,128)(2,1)}, bf16[2048,384]{1,0:T(8,128)(2,1)}, bf16[2048,384]{1,0:T(8,128)(2,1)}, bf16[2048,384]{1,0:T(8,128)(2,1)}, f32[32,512]{1,0:T(8,128)}) custom-call(s32[4,4]{1,0:T(4,128)} %len_ref.21, bf16[2048,768]{1,0:T(8,128)(2,1)} %rest_0_.3, ...), custom_call_target="tpu_custom_call", output_to_operand_aliasing={{0}: (6, {}), {1}: (7, {}), {2}: (8, {}), {3}: (9, {}), {4}... | custom-call | flops 14000000000 | bytes 1000000 | tf_op jit(solution)/shard_map/attn_fwd/pallas_call | solution.py:124
  40.5 11.5 %collective-permute-done.5 = f32[96,1536]{1,0:T(8,128)S(1)} collective-permute-done((f32[96,1536]{1,0:T(8,128)S(1)}, f32[96,1536]{1,0:T(8,128)S(1)}, u32[]{:S(2)}, u32[]{:S(2)}) %collective-permute-start.5) | collective-permute-done | bytes 589856 | tf_op jit(solution)/shard_map/ppermute | solution.py:485
  56.1 5.9 %collective-permute-done.6 = f32[48,1536]{1,0:T(8,128)S(1)} collective-permute-done((f32[48,1536]{1,0:T(8,128)S(1)}, f32[48,1536]{1,0:T(8,128)S(1)}, u32[]{:S(2)}, u32[]{:S(2)}) %collective-permute-start.6) | collective-permute-done | bytes 294944 | tf_op jit(solution)/shard_map/ppermute | solution.py:485
  65.9 8.3 %attn_fwd.6 = (bf16[2048,384]{1,0:T(8,128)(2,1)S(1)}, bf16[2048,384]{1,0:T(8,128)(2,1)S(1)}, bf16[2048,384]{1,0:T(8,128)(2,1)S(1)}, bf16[2048,384]{1,0:T(8,128)(2,1)S(1)}, f32[32,512]{1,0:T(8,128)S(1)}) custom-call(s32[4,4]{1,0:T(4,128)S(1)} %copy-done.8, bf16[2048,768]{1,0:T(8,128)(2,1)S(1)} %copy-done.2, bf16[768,384]{1,0:T(8,128)(2,1)S(1)} %get-tuple-element.166.wq_ref, ...), custom_call_target="tpu_custom_call" | custom-call | flops 14000000000 | bytes 1000000 | tf_op jit(solution)/shard_map/attn_fwd/pallas_call | solution.py:124
  74.1 3.9 collective-permute-done.9
  78.5 3.9 collective-permute-done.10
  85.4 8.6 %attn_fwd.7 = (bf16[2048,384]{1,0:T(8,128)(2,1)S(1)}, bf16[2048,384]{1,0:T(8,128)(2,1)S(1)}, bf16[2048,384]{1,0:T(8,128)(2,1)S(1)}, bf16[2048,384]{1,0:T(8,128)(2,1)S(1)}, f32[32,512]{1,0:T(8,128)S(1)}) custom-call(s32[4,4]{1,0:T(4,128)S(1)} %copy-done.8, ...), custom_call_target="tpu_custom_call", output_to_operand_aliasing={{0}: (6, {}), {1}: (7, {}), {2}: (8, {}), {3}: (9, {}), {4}... | custom-call | flops 14000000000 | bytes 1000000 | tf_op jit(solution)/shard_map/attn_fwd/pallas_call | solution.py:124
  104.1 54.0 %ff_fwd.1 = (bf16[2048,768]{1,0:T(8,128)(2,1)}, f32[2048,768]{1,0:T(8,128)}, bf16[2048,768]{1,0:T(8,128)(2,1)}, f32[2048,768]{1,0:T(8,128)}, bf16[2048,768]{1,0:...) custom-call(s32[4,4]{1,0:T(4,128)S(1)} %copy-done.8, ...), custom_call_target="tpu_custom_call" | custom-call | flops 57999998976 | bytes 1000000 | tf_op jit(solution)/shard_map/ff_fwd/pallas_call | solution.py:231
  158.2 4.8 %collective-permute-done.19 = f32[768,768]{1,0:T(8,128)} collective-permute-done((f32[768,768]{1,0:T(8,128)}, f32[768,768]{1,0:T(8,128)}, u32[]{:S(2)}, u32[]{:S(2)}) %collective-permute-start.19) | collective-permute-done | bytes 2359328 | tf_op jit(solution)/shard_map/ppermute | solution.py:485
  169.9 22.7 %ff_bwd_own.1 = (f32[2048,768]{1,0:T(8,128)S(1)}, f32[384,1536]{1,0:T(8,128)S(1)}, f32[384,1536]{1,0:T(8,128)}, f32[1,1536]{1,0:T(1,128)S(1)}) custom-call(bf16[2048,768]{1,0:T(8,128)(2,1)S(1)} %copy-done.22, bf16[2048,768]{1,0:T(8,128)(2,1)S(1)} %copy-done.33, f32[2048,1536]{1,0:T(8,128)} %get-tuple-element.190.gp_ref, bf16[768,1536]{1,0:T(8,128)(2,1)S(1)} %copy-done.1, ...), custom_call_target="tpu_custom_call" | custom-call | flops 25999998976 | bytes 1000000 | tf_op jit(solution)/shard_map/ff_bwd_own/pallas_call | solution.py:287
  204.8 20.2 %ff_bwd_peer.1 = (f32[2048,768]{1,0:T(8,128)S(1)}, bf16[2048,768]{1,0:T(8,128)(2,1)S(1)}, f32[384,768]{1,0:T(8,128)S(1)}, f32[8,768]{1,0:T(8,128)S(1)}) custom-call(bf16[2048,768]{1,0:T(8,128)(2,1)S(1)} %copy-done.23, f32[2048,768]{1,0:T(8,128)} %get-tuple-element.198.gs_ref, f32[2048,768]{1,0:T(8,128)} %get-tuple-element.199.x_ref, ...), custom_call_target="tpu_custom_call" | custom-call | flops 24999999488 | bytes 1000000 | tf_op jit(solution)/shard_map/ff_bwd_peer/pallas_call | solution.py:338
  234.6 17.8 %attn_bwd_own.2 = (f32[2048,768]{1,0:T(8,128)S(1)}, f32[416,1536]{1,0:T(8,128)S(1)}, f32[416,1536]{1,0:T(8,128)S(1)}) custom-call(s32[4,4]{1,0:T(4,128)S(1)} %copy-done.8, bf16[2048,768]{1,0:T(8,128)(2,1)S(1)} %get-tuple-element.203.lm_ref, bf16[384,768]{1,0:T(8,128)(2,1)S(1)} %copy-done.7, bf16[2048,384]{1,0:T(8,128)(2,1)S(1)} %copy-done.27, ...), custom_call_target="tpu_custom_call" | custom-call | flops 24000000000 | bytes 1000000 | tf_op jit(solution)/shard_map/attn_bwd_own/pallas_call | solution.py:458
  255.1 4.2 %collective-permute-done.25 = f32[96,1536]{1,0:T(8,128)S(1)} collective-permute-done((f32[96,1536]{1,0:T(8,128)S(1)}, f32[96,1536]{1,0:T(8,128)S(1)}, u32[]{:S(2)}, u32[]{:S(2)}) %collective-permute-start.25) | collective-permute-done | bytes 589856 | tf_op jit(solution)/shard_map/ppermute | solution.py:485
  262.5 18.7 %attn_bwd_own.3 = (f32[2048,768]{1,0:T(8,128)}, f32[416,1536]{1,0:T(8,128)S(1)}, f32[416,1536]{1,0:T(8,128)}) custom-call(s32[4,4]{1,0:T(4,128)S(1)} %copy-done.8, bf16[2048,768]{1,0:T(8,128)(2,1)S(1)} %get-tuple-element.203.lm_ref, bf16[384,768]{1,0:T(8,128)(2,1)S(1)} %copy-done.7, ...), custom_call_target="tpu_custom_call", output_to_operand_aliasing={{0}: (13, {})} | custom-call | flops 24000000000 | bytes 1000000 | tf_op jit(solution)/shard_map/attn_bwd_own/pallas_call | solution.py:458
  281.2 4.7 %collective-permute-done.28 = f32[192,768]{1,0:T(8,128)S(1)} collective-permute-done((f32[192,768]{1,0:T(8,128)S(1)}, f32[192,768]{1,0:T(8,128)S(1)}, u32[]{:S(2)}, u32[]{:S(2)}) %collective-permute-start.28) | collective-permute-done | bytes 589856 | tf_op jit(solution)/shard_map/ppermute | solution.py:485
  288.7 8.5 %attn_bwd_peer.4.rest_2_ = bf16[2048,768]{1,0:T(8,128)(2,1)} custom-call(s32[4,4]{1,0:T(4,128)} %len_ref.21, bf16[2048,768]{1,0:T(8,128)(2,1)} %copy-done.21, bf16[384,768]{1,0:T(8,128)(2,1)} %copy-done.16, bf16[2048,384]{1,0:T(8,128)(2,1)} %copy-done.24, bf16[2048,384]{1,0:T(8,128)(2,1)} %copy-done.25, bf16[2048,384]{1,0:T(8,128)(2,1)} %copy-done.26, ...), custom_call_target="tpu_custom_call" | custom-call | flops 40000000000 | bytes 1000000 | tf_op jit(solution)/shard_map/attn_bwd_peer/pallas_call | solution.py:458
  305.3 10.5 %attn_bwd_peer.5.rest_2_ = bf16[2048,768]{1,0:T(8,128)(2,1)} custom-call(s32[4,4]{1,0:T(4,128)} %len_ref.21, bf16[2048,768]{1,0:T(8,128)(2,1)} %copy-done.21, bf16[384,768]{1,0:T(8,128)(2,1)} %copy-done.16, bf16[2048,384]{1,0:T(8,128)(2,1)} %copy-done.24, bf16[2048,384]{1,0:T(8,128)(2,1)} %copy-done.25, ...), custom_call_target="tpu_custom_call", output_to_operand_aliasing={{}: (12, {})} | custom-call | flops 40000000000 | bytes 1000000 | tf_op jit(solution)/shard_map/attn_bwd_peer/pallas_call | solution.py:458
  315.8 3.3 collective-permute-done.30
  323.8 8.6 %attn_bwd_peer.6.rest_2_ = bf16[2048,768]{1,0:T(8,128)(2,1)} custom-call(s32[4,4]{1,0:T(4,128)} %len_ref.21, bf16[2048,768]{1,0:T(8,128)(2,1)} %copy-done.21, bf16[384,768]{1,0:T(8,128)(2,1)} %copy-done.16, bf16[2048,384]{1,0:T(8,128)(2,1)} %copy-done.24, bf16[2048,384]{1,0:T(8,128)(2,1)} %copy-done.25, ...), custom_call_target="tpu_custom_call", output_to_operand_aliasing={{}: (12, {})} | custom-call | flops 40000000000 | bytes 1000000 | tf_op jit(solution)/shard_map/attn_bwd_peer/pallas_call | solution.py:458
  340.6 10.5 %attn_bwd_peer.7 = bf16[2048,768]{1,0:T(8,128)(2,1)} custom-call(s32[4,4]{1,0:T(4,128)} %len_ref.21, bf16[2048,768]{1,0:T(8,128)(2,1)} %copy-done.21, bf16[384,768]{1,0:T(8,128)(2,1)} %copy-done.16, bf16[2048,384]{1,0:T(8,128)(2,1)} %copy-done.24, bf16[2048,384]{1,0:T(8,128)(2,1)} %copy-done.25, ...), custom_call_target="tpu_custom_call", output_to_operand_aliasing={{}: (12, {})} | custom-call | flops 40000000000 | bytes 1000000 | tf_op jit(solution)/shard_map/attn_bwd_peer/pallas_call | solution.py:458
  351.1 16.0 %collective-permute-done.34 = f32[208,768]{1,0:T(8,128)} collective-permute-done((f32[208,768]{1,0:T(8,128)S(1)}, f32[208,768]{1,0:T(8,128)}, u32[]{:S(2)}, u32[]{:S(2)}) %collective-permute-start.34) | collective-permute-done | bytes 639008 | tf_op jit(solution)/shard_map/ppermute | solution.py:485
  369.3 7.5 %collective-permute-done.35 = f32[104,768]{1,0:T(8,128)S(1)} collective-permute-done((f32[104,768]{1,0:T(8,128)S(1)}, f32[104,768]{1,0:T(8,128)S(1)}, u32[]{:S(2)}, u32[]{:S(2)}) %collective-permute-start.35) | collective-permute-done | bytes 319520 | tf_op jit(solution)/shard_map/ppermute | solution.py:485
  387.1 10.2 %collective-permute-done.41 = f32[208,768]{1,0:T(8,128)S(1)} collective-permute-done((f32[208,768]{1,0:T(8,128)S(1)}, f32[208,768]{1,0:T(8,128)S(1)}, u32[]{:S(2)}, u32[]{:S(2)}) %collective-permute-start.41) | collective-permute-done | bytes 639008 | tf_op jit(solution)/shard_map/ppermute | solution.py:485
  (242 shorter events, 118.4 us)
Async XLA Ops:
  3.2 17.6 %collective-permute-start = (f32[104,1536]{1,0:T(8,128)}, f32[104,1536]{1,0:T(8,128)S(1)}, u32[]{:S(2)}, u32[]{:S(2)}) collective-permute-start(f32[104,1536]{1,0:T(8,128)} %get-tuple-element.146), channel_id=1, source_target_pairs={{0,1},{1,0},{2,3},{3,2},{4,5},{5,4},{6,7},{7,6},{8,9},{9,8},{10,11... | collective-permute-start | bytes 1916936 | tf_op jit(solution)/shard_map/ppermute | solution.py:674
  20.9 15.6 %collective-permute-start.1 = (f32[48,1536]{1,0:T(8,128)S(1)}, f32[48,1536]{1,0:T(8,128)S(1)}, u32[]{:S(2)}, u32[]{:S(2)}) collective-permute-start(f32[48,1536]{1,0:T(8,128)S(1)} %get-tuple-element.288.rest_5_), channel_id=1, source_target_pairs={{0,4},{2,6},{4,0},{6,2},{8,12},{10,14},{12,8},{14,10},{16,20},{18,... | collective-permute-start | bytes 884744 | tf_op jit(solution)/shard_map/ppermute | solution.py:485
  54.6 27.8 %collective-permute-start.10 = (f32[384,768]{1,0:T(8,128)S(1)}, f32[384,768]{1,0:T(8,128)S(1)}, u32[]{:S(2)}, u32[]{:S(2)}) collective-permute-start(f32[384,768]{1,0:T(8,128)S(1)} %maximum_convert_fusion), channel_id=1, source_target_pairs={{0,1},{1,0},{2,3},{3,2},{4,5},{5,4},{6,7},{7,6},{8,9},{9,8},{10,11... | collective-permute-start | bytes 3538952 | tf_op jit(solution)/shard_map/ppermute | solution.py:686
  63.3 14.7 %collective-permute-start.9 = (f32[96,1536]{1,0:T(8,128)S(1)}, f32[96,1536]{1,0:T(8,128)S(1)}, u32[]{:S(2)}, u32[]{:S(2)}) collective-permute-start(f32[96,1536]{1,0:T(8,128)S(1)} %maximum_select_fusion.17.rest_1_), channel_id=1, source_target_pairs={{0,4},{2,6},{4,0},{6,2},{8,12},{10,14},{12,8},{14,10},{16,20},{18,... | collective-permute-start | bytes 1769480 | tf_op jit(solution)/shard_map/ppermute | solution.py:485
  64.0 14.5 %collective-permute-start.8 = (f32[96,1536]{1,0:T(8,128)S(1)}, f32[96,1536]{1,0:T(8,128)S(1)}, u32[]{:S(2)}, u32[]{:S(2)}) collective-permute-start(f32[96,1536]{1,0:T(8,128)S(1)} %maximum_select_fusion.16.rest_0_), channel_id=1, source_target_pairs={{0,8},{2,10},{4,12},{6,14},{8,0},{10,2},{12,4},{14,6},{16,24},{18,... | collective-permute-start | bytes 1769480 | tf_op jit(solution)/shard_map/ppermute | solution.py:485
  82.7 14.4 %collective-permute-start.13 = (f32[192,768]{1,0:T(8,128)S(1)}, f32[192,768]{1,0:T(8,128)S(1)}, u32[]{:S(2)}, u32[]{:S(2)}) collective-permute-start(f32[192,768]{1,0:T(8,128)S(1)} %get-tuple-element.284.rest_7_), channel_id=1, source_target_pairs={{0,4},{2,6},{4,0},{6,2},{8,12},{10,14},{12,8},{14,10},{16,20},{18,... | collective-permute-start | bytes 1769480 | tf_op jit(solution)/shard_map/ppermute | solution.py:485
  165.3 29.9 %collective-permute-start.20 = (f32[384,768]{1,0:T(8,128)S(1)}, f32[384,768]{1,0:T(8,128)}, u32[]{:S(2)}, u32[]{:S(2)}) collective-permute-start(f32[384,768]{1,0:T(8,128)S(1)} %constant_dynamic-slice_fusion.7.rest_0_), channel_id=1, source_target_pairs={{0,4},{2,6},{4,0},{6,2},{8,12},{10,14},{12,8},{14,10},{16,20},{18,... | collective-permute-start | bytes 3538952 | tf_op jit(solution)/shard_map/ppermute | solution.py:485
  197.1 30.4 %collective-permute-start.21 = (f32[192,768]{1,0:T(8,128)S(1)}, f32[192,768]{1,0:T(8,128)S(1)}, u32[]{:S(2)}, u32[]{:S(2)}) collective-permute-start(f32[192,768]{1,0:T(8,128)S(1)} %constant_dynamic-slice_fusion.6.rest_0_), channel_id=1, source_target_pairs={{0,8},{2,10},{4,12},{6,14},{8,0},{10,2},{12,4},{14,6},{16,24},{18,... | collective-permute-start | bytes 1769480 | tf_op jit(solution)/shard_map/ppermute | solution.py:485
  202.4 28.1 %collective-permute-start.23 = (f32[192,1536]{1,0:T(8,128)S(1)}, f32[192,1536]{1,0:T(8,128)S(1)}, u32[]{:S(2)}, u32[]{:S(2)}) collective-permute-start(f32[192,1536]{1,0:T(8,128)S(1)} %constant_dynamic-slice_fusion.5.rest_1_), channel_id=1, source_target_pairs={{0,4},{2,6},{4,0},{6,2},{8,12},{10,14},{12,8},{14,10},{16,20},{18,... | collective-permute-start | bytes 3538952 | tf_op jit(solution)/shard_map/ppermute | solution.py:485
  230.6 28.7 %collective-permute-start.24 = (f32[192,768]{1,0:T(8,128)S(1)}, f32[192,768]{1,0:T(8,128)S(1)}, u32[]{:S(2)}, u32[]{:S(2)}) collective-permute-start(f32[192,768]{1,0:T(8,128)S(1)} %dynamic-slice_add_fusion.5.rest_5_), channel_id=1, source_target_pairs={{0,16},{2,18},{4,20},{6,22},{8,24},{10,26},{12,28},{14,30},{16,0},... | collective-permute-start | bytes 1769480 | tf_op jit(solution)/shard_map/ppermute | solution.py:485
  232.9 26.4 %collective-permute-start.25 = (f32[96,1536]{1,0:T(8,128)S(1)}, f32[96,1536]{1,0:T(8,128)S(1)}, u32[]{:S(2)}, u32[]{:S(2)}) collective-permute-start(f32[96,1536]{1,0:T(8,128)S(1)} %constant_dynamic-slice_fusion.4.rest_6_), channel_id=1, source_target_pairs={{0,8},{2,10},{4,12},{6,14},{8,0},{10,2},{12,4},{14,6},{16,24},{18,... | collective-permute-start | bytes 1769480 | tf_op jit(solution)/shard_map/ppermute | solution.py:485
  259.4 26.6 %collective-permute-start.28 = (f32[192,768]{1,0:T(8,128)S(1)}, f32[192,768]{1,0:T(8,128)S(1)}, u32[]{:S(2)}, u32[]{:S(2)}) collective-permute-start(f32[192,768]{1,0:T(8,128)S(1)} %add.110.rest_4_), channel_id=1, source_target_pairs={{0,8},{2,10},{4,12},{6,14},{8,0},{10,2},{12,4},{14,6},{16,24},{18,... | collective-permute-start | bytes 1769480 | tf_op jit(solution)/shard_map/ppermute | solution.py:485
  260.1 37.2 %collective-permute-start.27 = (f32[96,1536]{1,0:T(8,128)S(1)}, f32[96,1536]{1,0:T(8,128)}, u32[]{:S(2)}, u32[]{:S(2)}) collective-permute-start(f32[96,1536]{1,0:T(8,128)S(1)} %dynamic-slice_add_fusion.4.rest_5_), channel_id=1, source_target_pairs={{0,16},{2,18},{4,20},{6,22},{8,24},{10,26},{12,28},{14,30},{16,0},... | collective-permute-start | bytes 1769480 | tf_op jit(solution)/shard_map/ppermute | solution.py:485
  281.1 16.1 %collective-permute-start.26 = (f32[416,1536]{1,0:T(8,128)}, f32[416,1536]{1,0:T(8,128)}, u32[]{:S(2)}, u32[]{:S(2)}) collective-permute-start(f32[416,1536]{1,0:T(8,128)} %get-tuple-element.225), channel_id=1, source_target_pairs={{0,2},{2,0},{4,6},{6,4},{8,10},{10,8},{12,14},{14,12},{16,18},{18,... | collective-permute-start | bytes 7667720 | tf_op jit(solution)/shard_map/ppermute | solution.py:485
  288.2 81.1 %collective-permute-start.38 = (f32[192,768]{1,0:T(8,128)}, f32[192,768]{1,0:T(8,128)}, u32[]{:S(2)}, u32[]{:S(2)}) collective-permute-start(f32[192,768]{1,0:T(8,128)} %get-tuple-element.281), channel_id=1, source_target_pairs={{0,4},{2,6},{4,0},{6,2},{8,12},{10,14},{12,8},{14,10},{16,20},{18,... | collective-permute-start | bytes 1769480 | tf_op jit(solution)/shard_map/ppermute | solution.py:485
  301.6 17.5 %collective-permute-start.30 = (f32[208,768]{1,0:T(8,128)S(1)}, f32[208,768]{1,0:T(8,128)}, u32[]{:S(2)}, u32[]{:S(2)}) collective-permute-start(f32[208,768]{1,0:T(8,128)S(1)} %constant_dynamic-slice_fusion.2.rest_4_), channel_id=1, source_target_pairs={{0,8},{2,10},{4,12},{6,14},{8,0},{10,2},{12,4},{14,6},{16,24},{18,... | collective-permute-start | bytes 1916936 | tf_op jit(solution)/shard_map/ppermute | solution.py:485
  301.7 17.3 %collective-permute-start.29 = (f32[208,768]{1,0:T(8,128)S(1)}, f32[208,768]{1,0:T(8,128)}, u32[]{:S(2)}, u32[]{:S(2)}) collective-permute-start(f32[208,768]{1,0:T(8,128)S(1)} %constant_dynamic-slice_fusion.3.rest_3_), channel_id=1, source_target_pairs={{0,4},{2,6},{4,0},{6,2},{8,12},{10,14},{12,8},{14,10},{16,20},{18,... | collective-permute-start | bytes 1916936 | tf_op jit(solution)/shard_map/ppermute | solution.py:485
  303.3 29.1 %collective-permute-start.33 = (f32[96,1536]{1,0:T(8,128)}, f32[96,1536]{1,0:T(8,128)}, u32[]{:S(2)}, u32[]{:S(2)}) collective-permute-start(f32[96,1536]{1,0:T(8,128)} %add.112.rest_5_), channel_id=1, source_target_pairs={{0,8},{2,10},{4,12},{6,14},{8,0},{10,2},{12,4},{14,6},{16,24},{18,... | collective-permute-start | bytes 1769480 | tf_op jit(solution)/shard_map/ppermute | solution.py:485
  323.2 46.1 %collective-permute-start.39 = (f32[192,768]{1,0:T(8,128)}, f32[192,768]{1,0:T(8,128)}, u32[]{:S(2)}, u32[]{:S(2)}) collective-permute-start(f32[192,768]{1,0:T(8,128)} %get-tuple-element.243.rest_5_), channel_id=1, source_target_pairs={{0,4},{2,6},{4,0},{6,2},{8,12},{10,14},{12,8},{14,10},{16,20},{18,... | collective-permute-start | bytes 1769480 | tf_op jit(solution)/shard_map/ppermute | solution.py:485
  337.2 29.8 %collective-permute-start.34 = (f32[208,768]{1,0:T(8,128)S(1)}, f32[208,768]{1,0:T(8,128)}, u32[]{:S(2)}, u32[]{:S(2)}) collective-permute-start(f32[208,768]{1,0:T(8,128)S(1)} %pad_maximum_fusion.rest_3_), channel_id=1, source_target_pairs={{0,16},{2,18},{4,20},{6,22},{8,24},{10,26},{12,28},{14,30},{16,0},... | collective-permute-start | bytes 1916936 | tf_op jit(solution)/shard_map/ppermute | solution.py:485
  340.2 37.9 %collective-permute-start.37 = (f32[192,1536]{1,0:T(8,128)S(1)}, f32[192,1536]{1,0:T(8,128)S(1)}, u32[]{:S(2)}, u32[]{:S(2)}) collective-permute-start(f32[192,1536]{1,0:T(8,128)S(1)} %maximum_select_fusion.11.rest_4_), channel_id=1, source_target_pairs={{0,4},{2,6},{4,0},{6,2},{8,12},{10,14},{12,8},{14,10},{16,20},{18,... | collective-permute-start | bytes 3538952 | tf_op jit(solution)/shard_map/ppermute | solution.py:485
  380.3 17.3 %collective-permute-start.43 = (f32[384,1536]{1,0:T(8,128)S(1)}, f32[384,1536]{1,0:T(8,128)S(1)}, u32[]{:S(2)}, u32[]{:S(2)}) collective-permute-start(f32[384,1536]{1,0:T(8,128)S(1)} %maximum_select_fusion.1.mine_ref), channel_id=1, source_target_pairs={{0,2},{2,0},{4,6},{6,4},{8,10},{10,8},{12,14},{14,12},{16,18},{18,... | collective-permute-start | bytes 7077896 | tf_op jit(solution)/shard_map/ppermute | solution.py:485
  380.9 16.4 %collective-permute-start.41 = (f32[208,768]{1,0:T(8,128)S(1)}, f32[208,768]{1,0:T(8,128)S(1)}, u32[]{:S(2)}, u32[]{:S(2)}) collective-permute-start(f32[208,768]{1,0:T(8,128)S(1)} %maximum_select_fusion.13), channel_id=1, source_target_pairs={{0,8},{2,10},{4,12},{6,14},{8,0},{10,2},{12,4},{14,6},{16,24},{18,... | collective-permute-start | bytes 1916936 | tf_op jit(solution)/shard_map/ppermute | solution.py:485
  381.5 16.1 %collective-permute-start.40 = (f32[208,768]{1,0:T(8,128)S(1)}, f32[208,768]{1,0:T(8,128)S(1)}, u32[]{:S(2)}, u32[]{:S(2)}) collective-permute-start(f32[208,768]{1,0:T(8,128)S(1)} %maximum_select_fusion.12), channel_id=1, source_target_pairs={{0,4},{2,6},{4,0},{6,2},{8,12},{10,14},{12,8},{14,10},{16,20},{18,... | collective-permute-start | bytes 1916936 | tf_op jit(solution)/shard_map/ppermute | solution.py:485
  (73 other events, 591.9 us)
